TPU v7x, 256 devices: a whole 4x4x8 slice. The times are simulated.
256 devices in a mesh: blk: 32 (over y_hi, z, core), phase: 8 (over y_lo, x).
Axes of the slice: x: 4, y: 4 (y_hi: 2, y_lo: 2; y = y_hi * 2 + y_lo), z: 8, core: 2. Of those that a mesh axis runs over, the one named last changes fastest.
Arguments:
- acts: bfloat16 [8, 4096, 2048], P('phase', 'blk'), may hold values from -6 to 6
- order: int32 [4096], replicated, may hold values from 0 to 4095, each once
- doc_ids: int32 [4096], replicated, may hold values from 0 to 7, never falling along the last dimension, each value on 1 to 1024 neighbouring positions
- gain: float32 [8, 2048], P('phase'), may hold values from 0.1 to 1.9
- w_query: bfloat16 [8, 2048, 1024], P('phase'), may hold values from -0.125 to 0.125
- w_keyval: bfloat16 [8, 2048, 2048], P('phase', 'blk'), may hold values from -0.125 to 0.125
- w_out: bfloat16 [8, 1024, 2048], P('phase'), may hold values from -0.5 to 0.5
- head_temp: float32 [8, 8], P('phase'), may hold values from 1 to 400
Outputs:
- layer_out: bfloat16 [8, 4096, 2048], P('phase', 'blk')
- next_input: bfloat16 [8, 4096, 2048], P('phase', 'blk')
Inputs may be any that keep to these rules, and one draw needn't show every extreme that they name: order holds every position of the sequence once. doc_ids never falls along positions; each document covers 1 to 1024 positions and one covers exactly 1024.
All inputs are finite; a program needn't handle non-finite values.
Results may differ from a plain program's by a relative error of at most 0.006.
The roundings to bfloat16 on the way count: a program that leaves them out, or rounds other values in their place, can miss the bound.
Values may be sent and summed in bfloat16 or wider, within the bound.
No kernel may reach another device: no remote copies, remote signals or barrier semaphores. Data moves between devices by JAX's collectives and lax.ppermute only.
A program may use at most 128 MiB of HBM per device.

v0:
```python
import jax
import jax.numpy as jnp
from jax import lax
from jax.sharding import PartitionSpec as P

mask_floor = -1e30


def passed_along(block, axis, distance):
    devices = range(lax.axis_size(axis))
    route = [(i - distance, i) for i in devices if i - distance in devices]
    return lax.ppermute(block, axis, route)


def per_device(acts, order, doc_ids, gain, w_query, w_keyval, w_out, head_temp):
    inputs = acts[0]
    tok_rows = inputs.shape[0]
    attn_width = w_query.shape[2]
    head_count = head_temp.shape[1]
    head_dim = attn_width // head_count
    block_index = lax.axis_index("blk")
    own_positions = lax.dynamic_slice_in_dim(order, block_index * tok_rows, tok_rows)
    own_docs = jnp.take(doc_ids, own_positions)
    upcast = inputs.astype(jnp.float32)
    normed = (
        upcast
        * lax.rsqrt(jnp.mean(upcast * upcast, axis=-1, keepdims=True) + 1e-05)
        * gain[0][None, :]
    ).astype(jnp.bfloat16)
    queries = jnp.dot(normed, w_query[0], preferred_element_type=jnp.float32)
    keyval = jnp.dot(
        normed,
        lax.all_gather(w_keyval[0], "blk", axis=0, tiled=True),
        preferred_element_type=jnp.float32,
    )
    query_heads = queries.reshape(tok_rows, head_count, head_dim)
    q_norm = (
        query_heads
        * lax.rsqrt(jnp.mean(query_heads * query_heads, axis=-1, keepdims=True) + 1e-06)
        * head_temp[0][None, :, None]
        / head_dim
    ).astype(jnp.bfloat16)
    key_heads = keyval[:, :attn_width].reshape(tok_rows, head_count, head_dim)
    k_norm = (
        (key_heads * lax.rsqrt(jnp.mean(key_heads * key_heads, axis=-1, keepdims=True) + 1e-06))
        .astype(jnp.bfloat16)
        .reshape(tok_rows, attn_width)
    )
    packed = jnp.concatenate([k_norm, keyval[:, attn_width:].astype(jnp.bfloat16)], axis=1)
    piece = lax.all_gather(packed, "blk", axis=0, tiled=True)
    peak = jnp.full((head_count, tok_rows), mask_floor, jnp.float32)
    count = piece.shape[0]
    key_doc = jnp.take(doc_ids, order)
    visible = (order[None, :] <= own_positions[:, None]) & (key_doc[None, :] == own_docs[:, None])
    remote_keys = piece[:, :attn_width].reshape(count, head_count, head_dim)
    remote_values = piece[:, attn_width:].reshape(count, head_count, head_dim).astype(jnp.float32)
    scores = jnp.einsum("qhd,khd->hqk", q_norm, remote_keys, preferred_element_type=jnp.float32)
    scores = jnp.where(visible[None], scores, mask_floor)
    new_peak = jnp.maximum(peak, jnp.max(scores, axis=-1))
    weights = jnp.where(visible[None], jnp.exp(scores - new_peak[..., None]), 0.0)
    total = jnp.sum(weights, axis=-1)
    accum = jnp.einsum(
        "hqk,khd->hqd",
        weights,
        remote_values,
        precision=lax.Precision.HIGHEST,
        preferred_element_type=jnp.float32,
    )
    peak, total, accum = (new_peak, total, accum)
    mixed = (
        (accum / total[..., None])
        .transpose(1, 0, 2)
        .reshape(tok_rows, attn_width)
        .astype(jnp.bfloat16)
    )
    produced = (upcast + jnp.dot(mixed, w_out[0], preferred_element_type=jnp.float32)).astype(
        jnp.bfloat16
    )
    handed = passed_along(produced, "phase", 1)
    return (produced[None], handed[None])


def solution(mesh):
    return jax.shard_map(
        per_device,
        mesh=mesh,
        in_specs=(
            P("phase", "blk", None),
            P(),
            P(),
            P("phase", None),
            P("phase", None, None),
            P("phase", "blk", None),
            P("phase", None, None),
            P("phase", None),
        ),
        out_specs=(P("phase", "blk", None), P("phase", "blk", None)),
        check_vma=False,
    )
```

profile of v0, /device:TPU:8, one launch (start us, length us, event | category | flops | bytes accessed | tf_op | source)
XLA Modules:
  0.0 339.7 jit_solution(15806795730808162947)
XLA Ops:
  7.2 0.0 copy-start
  7.2 0.0 all-gather.6.cloned.1.call-start
  7.2 0.7 all-gather.6.cloned.1.call-update
  7.9 0.0 all-gather.4.cloned.1.call-start
  8.0 1.2 fusion.22
  9.2 105.0 %all-gather.6.cloned.1.call-done = bf16[1,2048,2048]{2,1,0:T(8,128)(2,1)} async-done(((bf16[1,64,2048]{2,1,0:T(8,128)(2,1)}), bf16[1,2048,2048]{2,1,0:T(8,128)(2,1)}) %all-gather.6.cloned.1.call-update) | async-done | bytes 8388624 | tf_op jit(solution)/shard_map/all_gather | solution.py:33
  114.2 0.0 copy-start.5
  114.2 4.9 %fusion.5 = f32[128,2048]{1,0:T(8,128)S(1)} fusion(bf16[1,2048,2048]{2,1,0:T(8,128)(2,1)} %all-gather.6.cloned.1.call-done, bf16[1,128,2048]{2,1,0:T(8,128)(2,1)} %param.8, f32[2048]{0:T(1024)} %bitcast.74, f32[128]{0:T(128)S(1)} %add_rsqrt_fusion.2), kind=kOutput, calls=%fused_computation.10 | convolution fusion | flops 1074790400 | bytes 9970176 | tf_op jit(solution)/shard_map/dot_general | solution.py:31
  119.2 0.1 copy.35
  119.3 0.2 reduce_sum.38
  119.6 0.1 copy.27
  119.7 0.2 mul.91
  119.9 0.1 fusion.33
  120.1 0.8 pad_maximum_fusion
  120.9 0.0 all-gather.4.cloned.1.call-update
  120.9 0.0 copy-done.5
  120.9 0.1 compare_select_fusion.1
  121.0 0.0 copy-done
  121.0 1.1 gather_fusion.1
  122.2 23.0 %gather_fusion = s32[4096]{0:T(1024)S(1)} fusion(s32[4096]{0:T(1024)S(1)} %copy-done, s32[4096]{0:T(1024)S(1)} %fusion.41), kind=kCustom, calls=%fused_computation | custom fusion | bytes 49152 | tf_op jit(solution)/shard_map/jit(_take)/gather | solution.py:53
  145.2 0.0 copy-start.3
  145.3 0.0 copy-start.6
  145.3 6.6 %copy.32 = bf16[1024,2048]{1,0:T(8,128)(2,1)} copy(bf16[1024,2048]{0,1:T(8,128)(2,1)} %bitcast.68) | data formatting | bytes 8388608 | tf_op jit(solution)/shard_map/dot_general | solution.py:30
  151.9 0.0 copy-done.3
  151.9 0.0 copy-done.6
  151.9 4.4 %multiply_reduce_fusion = (f32[128,8]{0,1:T(8,128)S(1)}, f32[128,8,128]{0,2,1:T(8,128)}) fusion(bf16[8,128,2048]{2,1,0:T(8,128)(2,1)} %bitcast.66, bf16[1,128,2048]{2,1,0:T(8,128)(2,1)S(1)} %copy-done.3, f32[2048]{0:T(1024)S(1)} %bitcast.75, f32[128]{0:T(128)S(1)} %add_rsqrt_fusion.2), kind=kOutput, calls=%fused_computation.43 | convolution fusion | flops 538180608 | bytes 5255680 | tf_op jit(solution)/shard_map/dot_general | solution.py:30
  156.3 1.3 compare_and_fusion
  157.6 0.0 copy-start.7
  157.6 97.7 %all-gather.4.cloned.1.call-done = bf16[4096,2048]{1,0:T(8,128)(2,1)} async-done(((bf16[128,2048]{1,0:T(8,128)(2,1)}), bf16[4096,2048]{1,0:T(8,128)(2,1)}) %all-gather.4.cloned.1.call-update) | async-done | bytes 16777232 | tf_op jit(solution)/shard_map/all_gather | solution.py:50
  255.3 10.1 %slice_bitcast_fusion = (bf16[512,8,8,128]{3,2,1,0:T(8,128)(2,1)S(1)}, bf16[4096,1024]{1,0:T(8,128)(2,1)}) fusion(bf16[4096,2048]{1,0:T(8,128)(2,1)} %all-gather.4.cloned.1.call-done), kind=kLoop, calls=%fused_computation.9 | loop fusion | bytes 33554432
  265.5 0.0 copy-done.7
  265.5 8.9 %select_reduce_fusion = (f32[8,128]{1,0:T(8,128)S(1)}, f32[8,128,4096]{2,1,0:T(8,128)}) fusion(pred[128,4096]{1,0:T(8,128)(4,1)} %compare_and_fusion, bf16[512,8,8,128]{3,2,1,0:T(8,128)(2,1)S(1)} %get-tuple-element.4, f32[128,8,128]{0,2,1:T(8,128)} %get-tuple-element.7, f32[8]{0:T(128)S(1)} %bitcast.77, f32[128,8]{0,1:T(8,128)S(1)} %add_rsqrt_fusion.1), kind=kOutput, calls=%fused_computation.3 | convolution fusion | flops 1082653696 | bytes 26222624 | tf_op jit(solution)/shard_map/qhd,khd->hqk/dot_general | solution.py:57
  274.4 11.2 %copy.33 = bf16[4096,1024]{0,1:T(8,128)(2,1)} copy(bf16[4096,1024]{1,0:T(8,128)(2,1)} %get-tuple-element.5) | data formatting | bytes 16777216 | tf_op jit(solution)/shard_map/reshape | solution.py:56
  285.6 0.0 copy-start.2
  285.6 8.7 %fusion = f32[8,128]{1,0:T(8,128)S(1)} fusion(f32[8,128,4096]{2,1,0:T(8,128)} %get-tuple-element.9, f32[8,128]{1,0:T(8,128)S(1)} %broadcast_maximum_fusion, pred[128,4096]{1,0:T(8,128)(4,1)} %compare_and_fusion), kind=kLoop, calls=%fused_computation.4 | loop fusion | flops 16776192 | bytes 17309696 | tf_op jit(solution)/shard_map/reduce_sum | solution.py:61
  294.3 2.2 copy-done.2
  296.5 0.0 copy-start.1
  296.5 14.5 %fusion.28 = bf16[128,8,128]{0,2,1:T(8,128)(2,1)S(1)} fusion(bf16[4096,8,128]{0,2,1:T(8,128)(2,1)} %bitcast.67, f32[8,128,4096]{2,1,0:T(8,128)S(1)} %copy-done.2, f32[8,128]{1,0:T(8,128)S(1)} %broadcast_maximum_fusion, pred[128,4096]{1,0:T(8,128)(4,1)} %compare_and_fusion, f32[128,8]{0,1:T(8,128)S(1)} %bitcast.76), kind=kOutput, calls=%fused_computation.32 | convolution fusion | flops 6455296000 | bytes 25960448 | tf_op jit(solution)/shard_map/hqk,khd->hqd/dot_general | solution.py:62
  311.0 2.9 fusion.16
  313.9 0.0 copy-start.4
  314.0 3.4 collective-permute-start
  317.3 14.7 %collective-permute-done = bf16[128,2048]{1,0:T(8,128)(2,1)S(1)} collective-permute-done((bf16[128,2048]{1,0:T(8,128)(2,1)S(1)}, bf16[128,2048]{1,0:T(8,128)(2,1)S(1)}, u32[]{:S(2)}, u32[]{:S(2)}) %collective-permute-start) | collective-permute-done | bytes 524320 | tf_op jit(solution)/shard_map/ppermute | solution.py:12
  332.0 0.8 copy.45
  332.8 0.0 copy-done.4
  332.8 0.0 copy-done.1
  (11 shorter events, 0.2 us)
Async XLA Ops:
  7.2 113.9 %copy-start = (s32[4096]{0:T(1024)S(1)}, s32[4096]{0:T(1024)}, u32[]{:S(2)}) copy-start(s32[4096]{0:T(1024)} %param.10) | copy-start | bytes 49156
  7.2 107.1 %all-gather.6.cloned.1.call-start = ((), (), s32[]{:S(2)}) async-start(), calls=%async_computation.1 | async-start | bytes 8650752 | tf_op jit(solution)/shard_map/all_gather | solution.py:33
  7.9 247.4 %all-gather.4.cloned.1.call-start = ((), (), s32[]{:S(2)}) async-start(), calls=%async_computation | async-start | bytes 17301504 | tf_op jit(solution)/shard_map/all_gather | solution.py:50
  114.2 6.7 %copy-start.5 = (s32[4096]{0:T(1024)S(1)}, s32[4096]{0:T(1024)}, u32[]{:S(2)}) copy-start(s32[4096]{0:T(1024)} %param.9) | copy-start | bytes 49156
  145.2 6.7 %copy-start.3 = (bf16[1,128,2048]{2,1,0:T(8,128)(2,1)S(1)}, bf16[1,128,2048]{2,1,0:T(8,128)(2,1)}, u32[]{:S(2)}) copy-start(bf16[1,128,2048]{2,1,0:T(8,128)(2,1)} %param.8) | copy-start | bytes 1572868
  145.3 6.7 %copy-start.6 = (f32[1,2048]{1,0:T(1,128)S(1)}, f32[1,2048]{1,0:T(1,128)}, u32[]{:S(2)}) copy-start(f32[1,2048]{1,0:T(1,128)} %param.11) | copy-start | bytes 24580
  157.6 107.9 %copy-start.7 = (f32[1,8]{1,0:T(1,128)S(1)}, f32[1,8]{1,0:T(1,128)}, u32[]{:S(2)}) copy-start(f32[1,8]{1,0:T(1,128)} %param.15) | copy-start | bytes 100
  285.6 10.9 %copy-start.2 = (f32[8,128,4096]{2,1,0:T(8,128)S(1)}, f32[8,128,4096]{2,1,0:T(8,128)}, u32[]{:S(2)}) copy-start(f32[8,128,4096]{2,1,0:T(8,128)} %get-tuple-element.9) | copy-start | bytes 50331652
  296.5 36.3 %copy-start.1 = (s32[4096]{0:T(1024)S(1)}, s32[4096]{0:T(1024)}, u32[]{:S(2)}) copy-start(s32[4096]{0:T(1024)} %param.10) | copy-start | bytes 49156
  313.9 18.9 %copy-start.4 = (bf16[128,2048]{1,0:T(8,128)(2,1)}, bf16[128,2048]{1,0:T(8,128)(2,1)S(1)}, u32[]{:S(2)}) copy-start(bf16[128,2048]{1,0:T(8,128)(2,1)S(1)} %fusion.16) | copy-start | bytes 1572868
  314.0 18.1 %collective-permute-start = (bf16[128,2048]{1,0:T(8,128)(2,1)S(1)}, bf16[128,2048]{1,0:T(8,128)(2,1)S(1)}, u32[]{:S(2)}, u32[]{:S(2)}) collective-permute-start(bf16[128,2048]{1,0:T(8,128)(2,1)S(1)} %fusion.16), channel_id=1, source_target_pairs={{0,1},{1,2},{2,3},{3,4},{4,5},{5,6},{6,7},{8,9},{9,10},{10,11},{11... | collective-permute-start | bytes 1572872 | tf_op jit(solution)/shard_map/ppermute | solution.py:12
Sparse Core Ops, SparseCore 0:
  10.8 103.4 all-gather.5
  121.0 134.2 all-gather.3
where the time goes:
time: 340 us
  waiting for transfers between devices  218 us (64%)
  local copies, waits for them, and re-layouts  55.7 us (16%)
  matrix products  35.6 us (10%)
  between operations  14.2 us (4%)
  other arithmetic  12.5 us (4%)
  starting transfers between devices  3.45 us (1%)
    all_gather x1, waiting for transfers between devices, per_device(): lax.all_gather(w_keyval[0], 'blk', axis=0, tiled=True)  105 us
    all_gather x1, waiting for transfers between devices, per_device(): piece = lax.all_gather(packed, 'blk', axis=0, tiled=True)  97.7 us
    gather x1, local copies, waits for them, and re-layouts, per_device(): key_doc = jnp.take(doc_ids, order)  23 us
    ppermute x1, waiting for transfers between devices, passed_along(): return lax.ppermute(block, axis, route)  14.7 us
    dot_general x1, matrix products, per_device(): jnp.einsum('hqk,khd->hqd', weights, remote_values, precision=lax.Precisio...  14.5 us
    unnamed x19, local copies, waits for them, and re-layouts  13.3 us
    reshape x1, local copies, waits for them, and re-layouts, per_device(): piece[:, attn_width:].reshape(count, head_count, head_dim)  11.2 us
    dot_general x1, matrix products, per_device(): jnp.einsum('qhd,khd->hqk', q_norm, remote_keys, preferred_element_type=jn...  8.92 us
  transfers between devices with their start and end apart: 3, of which 3 were waited for; matrix products, arithmetic and copies ran while one was open for 11% of the time, Pallas kernels for 0%

commit v1 on v0

v1 whole, which is shorter than its diff:
```python
import functools

import jax
import jax.numpy as jnp
import numpy as np
from jax import lax
from jax.experimental import pallas as pl
from jax.experimental.pallas import tpu as pltpu
from jax.sharding import Mesh
from jax.sharding import PartitionSpec as P

ZS = 8
MIB = 1024 * 1024


def shifted(block, axis, distance):
    count = lax.axis_size(axis)
    return lax.ppermute(block, axis, [(i, (i + distance) % count) for i in range(count)])


def passed_along(block, axis, distance):
    devices = range(lax.axis_size(axis))
    route = [(i - distance, i) for i in devices if i - distance in devices]
    return lax.ppermute(block, axis, route)


def params(mib):
    return pltpu.CompilerParams(vmem_limit_bytes=mib * MIB)


def norm_kernel(x_ref, g_ref, o_ref):
    x = x_ref[...].astype(jnp.float32)
    o_ref[...] = (
        x * lax.rsqrt(jnp.mean(x * x, axis=-1, keepdims=True) + 1e-05) * g_ref[...]
    ).astype(jnp.bfloat16)


def normalized(x, gain):
    return pl.pallas_call(
        norm_kernel,
        out_shape=jax.ShapeDtypeStruct(x.shape, jnp.bfloat16),
        compiler_params=params(16),
        cost_estimate=pl.CostEstimate(flops=0, bytes_accessed=2 * x.size * 2, transcendentals=0),
    )(x, gain)


def project_kernel(count, temp_ref, *refs):
    blocks, (wq_ref, wkv_ref, q_ref, kv_ref) = refs[:count], refs[count:]
    head_dim = wq_ref.shape[1]
    start = 0
    for block in blocks:
        rows = pl.ds(start, block.shape[0])
        start += block.shape[0]
        x = block[...]
        q = jnp.dot(x, wq_ref[...], preferred_element_type=jnp.float32)
        kv = jnp.dot(x, wkv_ref[...], preferred_element_type=jnp.float32)
        k = kv[:, :head_dim]
        q_scale = lax.rsqrt(jnp.mean(q * q, axis=-1, keepdims=True) + 1e-06)
        q_ref[rows, :] = (q * q_scale * temp_ref[0, 0] / head_dim).astype(jnp.bfloat16)
        k_scale = lax.rsqrt(jnp.mean(k * k, axis=-1, keepdims=True) + 1e-06)
        kv_ref[rows, :head_dim] = (k * k_scale).astype(jnp.bfloat16)
        kv_ref[rows, head_dim:] = kv[:, head_dim:].astype(jnp.bfloat16)


def projected(blocks, wq, wkv, temp):
    rows = sum(b.shape[0] for b in blocks)
    vmem = pl.BlockSpec(memory_space=pltpu.VMEM)
    return pl.pallas_call(
        functools.partial(project_kernel, len(blocks)),
        in_specs=[pl.BlockSpec(memory_space=pltpu.SMEM)] + [vmem] * (len(blocks) + 2),
        out_specs=[vmem, vmem],
        out_shape=[
            jax.ShapeDtypeStruct((rows, wq.shape[1]), jnp.bfloat16),
            jax.ShapeDtypeStruct((rows, wkv.shape[1]), jnp.bfloat16),
        ],
        compiler_params=params(32),
        cost_estimate=pl.CostEstimate(
            flops=2 * rows * 2048 * 384, bytes_accessed=rows * 5632 + 1572864, transcendentals=0
        ),
    )(temp, *blocks, wq, wkv)


def attend_kernel(sizes, at_ref, *refs):
    steps = len(sizes)
    q_refs, kv_refs = refs[:steps], refs[steps : 4 * steps]
    qpos_ref, qspan_ref, kpos_ref, o_ref, q_all, k_all, v_all, s_all = refs[4 * steps :]
    head_dim = q_all.shape[1]
    own_rows, keys = q_all.shape[0], k_all.shape[0]
    start = 0
    for step, size in enumerate(sizes):
        q_all[pl.ds(start, size), :] = q_refs[step][...]
        own, other, pair = kv_refs[3 * step : 3 * step + 3]
        for place, part in enumerate((own[...], other[...], pair[0], pair[1])):
            rows = pl.ds(place * own_rows + start, size)
            k_all[rows, :] = part[:, :head_dim]
            v_all[rows, :] = part[:, head_dim:]
        start += size
    tile, wide = 128, 512
    first_z = at_ref[0, 0]

    def one_block(b, _):
        rows = pl.ds(pl.multiple_of(b * tile, tile), tile)
        q = q_all[rows, :]
        qpos = jnp.broadcast_to(qpos_ref[rows, :], (tile, 128))
        qspan = jnp.broadcast_to(qspan_ref[rows, :], (tile, 128))
        peak = jnp.full((tile, 128), -1e30, jnp.float32)
        for t in range(keys // wide):
            s = lax.dot_general(
                q,
                k_all[t * wide : (t + 1) * wide, :],
                (((1,), (1,)), ((), ())),
                preferred_element_type=jnp.float32,
            )
            for u in range(wide // 128):
                lanes = slice(t * wide + u * 128, t * wide + (u + 1) * 128)
                back = qpos - kpos_ref[0:1, lanes]
                seen = (back >= 0) & (back <= qspan)
                part = jnp.where(seen, s[:, u * 128 : (u + 1) * 128], -1e30)
                s_all[:, lanes] = part
                peak = jnp.maximum(peak, part)
        top = jnp.max(peak, axis=-1, keepdims=True)
        total = jnp.zeros((tile, 128), jnp.float32)
        mixed = jnp.zeros((tile, head_dim), jnp.float32)
        for t in range(keys // wide):
            lanes = slice(t * wide, (t + 1) * wide)
            w = jnp.exp(s_all[:, lanes] - top)
            for u in range(wide // 128):
                total = total + w[:, u * 128 : (u + 1) * 128]
            mixed = mixed + jnp.dot(
                w.astype(jnp.bfloat16), v_all[lanes, :], preferred_element_type=jnp.float32
            )
        offset = lax.select(b == 0, 0, b)
        place = lax.rem(first_z + offset, ZS)
        o_ref[pl.ds(pl.multiple_of(place * tile, tile), tile), :] = (
            mixed / jnp.sum(total, axis=-1, keepdims=True)
        ).astype(jnp.bfloat16)
        return 0

    lax.fori_loop(0, own_rows // tile, one_block, 0)


def attended(at, queries, keyvals, qpos, qspan, kpos):
    sizes = tuple(q.shape[0] for q in queries)
    rows, keys, head_dim = sum(sizes), 4 * sum(sizes), queries[0].shape[1]
    vmem = pl.BlockSpec(memory_space=pltpu.VMEM)
    operands = [*queries, *[a for three in keyvals for a in three], qpos, qspan, kpos]
    return pl.pallas_call(
        functools.partial(attend_kernel, sizes),
        in_specs=[pl.BlockSpec(memory_space=pltpu.SMEM)] + [vmem] * len(operands),
        out_specs=vmem,
        out_shape=jax.ShapeDtypeStruct((rows, head_dim), jnp.bfloat16),
        scratch_shapes=[
            pltpu.VMEM((rows, head_dim), jnp.bfloat16),
            pltpu.VMEM((keys, head_dim), jnp.bfloat16),
            pltpu.VMEM((keys, head_dim), jnp.bfloat16),
            pltpu.VMEM((128, keys), jnp.float32),
        ],
        compiler_params=params(40),
        cost_estimate=pl.CostEstimate(
            flops=4 * rows * keys * head_dim, bytes_accessed=8 * keys * head_dim, transcendentals=rows * keys
        ),
    )(at, *operands)


def output_kernel(m_ref, w_ref, x_ref, o_ref):
    mixed = jnp.concatenate([m_ref[h] for h in range(m_ref.shape[0])], axis=1)
    wide = 512
    for t in range(w_ref.shape[1] // wide):
        lanes = slice(t * wide, (t + 1) * wide)
        added = jnp.dot(mixed, w_ref[:, lanes], preferred_element_type=jnp.float32)
        o_ref[:, lanes] = (x_ref[:, lanes].astype(jnp.float32) + added).astype(jnp.bfloat16)


def outputs(mixed, w_out, x):
    return pl.pallas_call(
        output_kernel,
        out_shape=jax.ShapeDtypeStruct(x.shape, jnp.bfloat16),
        compiler_params=params(24),
        cost_estimate=pl.CostEstimate(
            flops=2 * 128 * 1024 * 2048, bytes_accessed=6 * MIB, transcendentals=0
        ),
    )(mixed, w_out, x)


def per_device(acts, order, doc_ids, gain, w_query, w_keyval, w_out, head_temp):
    inputs = acts[0]
    width = w_query.shape[2]
    heads = head_temp.shape[1]
    head_dim = width // heads
    yh, z, c = (lax.axis_index(a) for a in ("yh", "z", "c"))

    normed = normalized(inputs, gain)

    slab = w_keyval[0]
    rows = slab.shape[0]
    by_head = jnp.concatenate(
        [slab[:, :width].reshape(rows, heads, head_dim), slab[:, width:].reshape(rows, heads, head_dim)], axis=2
    ).transpose(1, 0, 2)
    own_w = lax.all_to_all(by_head, "z", 0, 0, tiled=True)
    other_w = shifted(own_w, "yh", 1)
    both = jnp.stack([jnp.where(yh == 0, own_w, other_w), jnp.where(yh == 0, other_w, own_w)])
    across = shifted(both, "c", 1)
    wkv = jnp.stack(
        [jnp.where(c == 0, both, across), jnp.where(c == 0, across, both)], axis=2
    ).reshape(-1, 2 * head_dim)
    wq = lax.dynamic_slice_in_dim(w_query[0], z * head_dim, head_dim, axis=1)
    temp = lax.dynamic_slice_in_dim(head_temp, z, 1, axis=1)

    grid = order.reshape(2, ZS, 2, -1)
    grid = lax.dynamic_slice_in_dim(jnp.concatenate([grid, grid], axis=1), z, ZS, axis=1)
    grid = jnp.where(yh == 0, grid, grid[::-1])
    grid = jnp.where(c == 0, grid, grid[:, :, ::-1])
    qpos = grid[0, :, 0].reshape(-1, 1)
    begins = jnp.sum(
        (doc_ids[None, :] < jnp.arange(1, 8, dtype=jnp.int32)[:, None]).astype(jnp.int32), axis=1
    )
    began = jnp.max(jnp.where(begins[None, :] <= qpos, begins[None, :], 0), axis=1, keepdims=True)
    qspan = qpos - began
    kpos = grid.transpose(2, 0, 1, 3).reshape(1, -1)

    half = inputs.shape[0] // 2
    right, left = [normed], [normed]
    for _ in range(3):
        right.append(shifted(right[-1], "z", 1))
        left.append(shifted(left[-1], "z", -1))
    far_top = shifted(right[-1][:half], "z", 1)
    far_bottom = shifted(left[-1][half:], "z", -1)
    groups = [[normed, left[1]], [left[2], left[3]], [far_top, far_bottom], [right[3], right[2]], [right[1]]]
    groups = [[normed], [left[1]], [left[2]], [left[3]], [far_top, far_bottom], [right[3]], [right[2]], [right[1]]]
    queries, keyvals = [None] * 8, [None] * 8
    for g in (0, 1, 7, 2, 6, 3, 5, 4):
        q, kv = projected(groups[g], wq, wkv, temp)
        other = shifted(kv, "yh", 1)
        pair = shifted(jnp.stack([kv, other]), "c", 1)
        queries[g], keyvals[g] = q, (kv, other, pair)

    at = z.astype(jnp.int32).reshape(1, 1)
    mixed = attended(at, queries, keyvals, qpos, qspan, kpos)
    mixed = lax.all_to_all(mixed.reshape(ZS, -1, head_dim), "z", 0, 0, tiled=True)
    produced = outputs(mixed, w_out[0], inputs)
    handed = passed_along(produced, ("yl", "x"), 1)
    return (produced[None], handed[None])


def solution(mesh):
    devices = np.asarray(mesh.devices).reshape(2, ZS, 2, 2, 4)
    fine = Mesh(devices, ("yh", "z", "c", "yl", "x"))
    phase, blk = ("yl", "x"), ("yh", "z", "c")
    return jax.shard_map(
        per_device,
        mesh=fine,
        in_specs=(
            P(phase, blk, None),
            P(),
            P(),
            P(phase, None),
            P(phase, None, None),
            P(phase, blk, None),
            P(phase, None, None),
            P(phase, None),
        ),
        out_specs=(P(phase, blk, None), P(phase, blk, None)),
        check_vma=False,
    )
```

time: 340 us -> 139 us (0.41)
  waiting for transfers between devices: 218 us -> 44.2 us
  local copies, waits for them, and re-layouts: 55.7 us -> 6.53 us
  starting transfers between devices: 3.45 us -> 41.7 us
  matrix products: 35.6 us -> 0 us
  Pallas kernels: 0 us -> 21.5 us
  blocking collectives: 0 us -> 19 us
  between operations: 14.2 us -> 0.98 us
  other arithmetic: 12.5 us -> 4.79 us
    all_gather x2 -> x0, waiting for transfers between devices: 203 us -> none  [the longest x1 105 us: per_device(): lax.all_gather(w_keyval[0], 'blk', axis=0, tiled=True)]
    dot_general x5 -> x0, matrix products: 35.6 us -> none  [the longest x1 14.5 us: per_device(): jnp.einsum('hqk,khd->hqd', weights, remote_values, precision=lax.Precisio...]
    ppermute x0 -> x26, starting transfers between devices: none -> 29.8 us  [shifted(): lax.ppermute(block, axis, [(i, (i + distance) % count) for i in range(cou...]
    gather x2 -> x0, local copies, waits for them, and re-layouts: 24.2 us -> none  [the longest x1 23 us: per_device(): key_doc = jnp.take(doc_ids, order)]
    ppermute x0 -> x26, waiting for transfers between devices: none -> 23.1 us  [shifted(): lax.ppermute(block, axis, [(i, (i + distance) % count) for i in range(cou...]
    pallas_call x0 -> x11, Pallas kernels: none -> 21.5 us  [the longest x1 10.3 us: attended(): pl.pallas_call(functools.partial(attend_kernel, sizes), in_specs=[pl.Bloc...]
    all_to_all x0 -> x1, blocking collectives: none -> 19 us  [per_device(): lax.all_to_all(mixed.reshape(ZS, -1, head_dim), 'z', 0, 0, tiled=True)]
    reshape x1, local copies, waits for them, and re-layouts: 11.2 us -> 0.06 us  [per_device(): slab[:, width:].reshape(rows, heads, head_dim)]
  transfers between devices with their start and end apart: 3 -> 28, of which waited for: 3 -> 10; matrix products, arithmetic and copies ran while one was open for 11% -> 5% of each run, Pallas kernels for 0% -> 7%
where the time goes in v1:
time: 139 us
  waiting for transfers between devices  44.2 us (32%)
  starting transfers between devices  41.7 us (30%)
  Pallas kernels  21.5 us (15%)
  blocking collectives  19 us (14%)
  local copies, waits for them, and re-layouts  6.53 us (5%)
  other arithmetic  4.79 us (3%)
    ppermute x26, starting transfers between devices, shifted(): lax.ppermute(block, axis, [(i, (i + distance) % count) for i in range(cou...  29.8 us
    ppermute x26, waiting for transfers between devices, shifted(): lax.ppermute(block, axis, [(i, (i + distance) % count) for i in range(cou...  23.1 us
    all_to_all x1, blocking collectives, per_device(): lax.all_to_all(mixed.reshape(ZS, -1, head_dim), 'z', 0, 0, tiled=True)  19 us
    ppermute x1, waiting for transfers between devices, passed_along(): return lax.ppermute(block, axis, route)  14.6 us
    pallas_call x1, Pallas kernels, attended(): pl.pallas_call(functools.partial(attend_kernel, sizes), in_specs=[pl.Bloc...  10.3 us
    pallas_call x8, Pallas kernels, projected(): pl.pallas_call(functools.partial(project_kernel, len(blocks)), in_specs=[...  9.49 us
    all_to_all x1, starting transfers between devices, per_device(): own_w = lax.all_to_all(by_head, 'z', 0, 0, tiled=True)  8.47 us
    all_to_all x1, waiting for transfers between devices, per_device(): own_w = lax.all_to_all(by_head, 'z', 0, 0, tiled=True)  6.56 us
  transfers between devices with their start and end apart: 28, of which 10 were waited for; matrix products, arithmetic and copies ran while one was open for 5% of the time, Pallas kernels for 7%

profile of v1, /device:TPU:8, one launch (start us, length us, event | category | flops | bytes accessed | tf_op | source)
XLA Modules:
  0.0 138.7 jit_solution(13998627671185595692)
XLA Ops:
  0.7 1.0 slice_bitcast_fusion.1
  1.7 0.7 maximum_bitcast_fusion
  2.5 8.5 %all-to-all-start = ((bf16[8,64,256]{2,1,0:T(8,128)(2,1)}), bf16[8,64,256]{2,1,0:T(8,128)(2,1)S(1)}, u32[]{:S(2)}, u32[]{:S(2)}) async-start(bf16[8,64,256]{2,1,0:T(8,128)(2,1)} %maximum_bitcast_fusion), calls=%async_computation | async-start | bytes 524288 | tf_op jit(solution)/shard_map/all_to_all | solution.py:199
  10.9 1.0 copy-done.2
  12.0 0.7 copy-done.4
  12.9 3.3 %collective-permute-start.2 = (bf16[128,2048]{1,0:T(8,128)(2,1)S(1)}, bf16[128,2048]{1,0:T(8,128)(2,1)S(1)}, u32[]{:S(2)}, u32[]{:S(2)}) collective-permute-start(bf16[128,2048]{1,0:T(8,128)(2,1)S(1)} %shard_map.95.refs_0_), channel_id=1, source_target_pairs={{0,112},{16,0},{32,16},{48,32},{64,48},{80,64},{96,80},{112,96},{1... | collective-permute-start | bytes 1572872 | tf_op jit(solution)/shard_map/ppermute | solution.py:18
  16.2 0.7 fusion
  17.0 6.6 %all-to-all-done = bf16[8,64,256]{2,1,0:T(8,128)(2,1)S(1)} async-done(((bf16[8,64,256]{2,1,0:T(8,128)(2,1)}), bf16[8,64,256]{2,1,0:T(8,128)(2,1)S(1)}, u32[]{:S(2)}, u32[]{:S(2)}) %all-to-all-start) | async-done | bytes 262176 | tf_op jit(solution)/shard_map/all_to_all | solution.py:199
  23.6 2.3 %collective-permute-start = (bf16[8,64,256]{2,1,0:T(8,128)(2,1)S(1)}, bf16[8,64,256]{2,1,0:T(8,128)(2,1)S(1)}, u32[]{:S(2)}, u32[]{:S(2)}) collective-permute-start(bf16[8,64,256]{2,1,0:T(8,128)(2,1)S(1)} %all-to-all-done), channel_id=1, source_target_pairs={{0,128},{128,0},{1,129},{129,1},{2,130},{130,2},{3,131},{131,3},{4... | collective-permute-start | bytes 786440 | tf_op jit(solution)/shard_map/ppermute | solution.py:18
  26.2 0.6 constant_dynamic-slice_fusion.temp_ref
  26.7 3.4 %collective-permute-done.2.refs_0_ = bf16[128,2048]{1,0:T(8,128)(2,1)S(1)} collective-permute-done((bf16[128,2048]{1,0:T(8,128)(2,1)S(1)}, bf16[128,2048]{1,0:T(8,128)(2,1)S(1)}, u32[]{:S(2)}, u32[]{:S(2)}) %collective-permute-start.2) | collective-permute-done | bytes 524320 | tf_op jit(solution)/shard_map/ppermute | solution.py:18
  30.1 2.2 %collective-permute-start.3 = (bf16[128,2048]{1,0:T(8,128)(2,1)S(1)}, bf16[128,2048]{1,0:T(8,128)(2,1)S(1)}, u32[]{:S(2)}, u32[]{:S(2)}) collective-permute-start(bf16[128,2048]{1,0:T(8,128)(2,1)S(1)} %collective-permute-done.2.refs_0_), channel_id=1, source_target_pairs={{0,112},{16,0},{32,16},{48,32},{64,48},{80,64},{96,80},{112,96},{1... | collective-permute-start | bytes 1572872 | tf_op jit(solution)/shard_map/ppermute | solution.py:18
  32.8 1.1 dynamic-slice_bitcast_fusion.refs_1_.refs_2_
  33.9 9.1 %collective-permute-done.3.refs_0_ = bf16[128,2048]{1,0:T(8,128)(2,1)S(1)} collective-permute-done((bf16[128,2048]{1,0:T(8,128)(2,1)S(1)}, bf16[128,2048]{1,0:T(8,128)(2,1)S(1)}, u32[]{:S(2)}, u32[]{:S(2)}) %collective-permute-start.3) | collective-permute-done | bytes 524320 | tf_op jit(solution)/shard_map/ppermute | solution.py:18
  43.0 3.2 %collective-permute-start.4 = (bf16[128,2048]{1,0:T(8,128)(2,1)S(1)}, bf16[128,2048]{1,0:T(8,128)(2,1)S(1)}, u32[]{:S(2)}, u32[]{:S(2)}) collective-permute-start(bf16[128,2048]{1,0:T(8,128)(2,1)S(1)} %collective-permute-done.3.refs_0_), channel_id=1, source_target_pairs={{0,112},{16,0},{32,16},{48,32},{64,48},{80,64},{96,80},{112,96},{1... | collective-permute-start | bytes 1572872 | tf_op jit(solution)/shard_map/ppermute | solution.py:18
  46.4 1.2 shard_map.96
  47.5 2.4 %collective-permute-start.10 = (bf16[128,256]{1,0:T(8,128)(2,1)S(1)}, bf16[128,256]{1,0:T(8,128)(2,1)S(1)}, u32[]{:S(2)}, u32[]{:S(2)}) collective-permute-start(bf16[128,256]{1,0:T(8,128)(2,1)S(1)} %get-tuple-element.26.refs_8_), channel_id=1, source_target_pairs={{0,128},{128,0},{1,129},{129,1},{2,130},{130,2},{3,131},{131,3},{4... | collective-permute-start | bytes 196616 | tf_op jit(solution)/shard_map/ppermute | solution.py:18
  49.9 1.2 shard_map.97
  51.1 1.3 collective-permute-start.12
  52.4 1.2 shard_map.98
  53.6 2.4 %collective-permute-start.14 = (bf16[128,256]{1,0:T(8,128)(2,1)S(1)}, bf16[128,256]{1,0:T(8,128)(2,1)S(1)}, u32[]{:S(2)}, u32[]{:S(2)}) collective-permute-start(bf16[128,256]{1,0:T(8,128)(2,1)S(1)} %get-tuple-element.28.refs_14_), channel_id=1, source_target_pairs={{0,128},{128,0},{1,129},{129,1},{2,130},{130,2},{3,131},{131,3},{4... | collective-permute-start | bytes 196616 | tf_op jit(solution)/shard_map/ppermute | solution.py:18
  55.9 1.2 shard_map.102
  57.1 1.2 shard_map.103
  58.3 1.3 collective-permute-start.22
  59.6 2.4 %collective-permute-start.24 = (bf16[128,256]{1,0:T(8,128)(2,1)S(1)}, bf16[128,256]{1,0:T(8,128)(2,1)S(1)}, u32[]{:S(2)}, u32[]{:S(2)}) collective-permute-start(bf16[128,256]{1,0:T(8,128)(2,1)S(1)} %get-tuple-element.33.refs_29_), channel_id=1, source_target_pairs={{0,128},{128,0},{1,129},{129,1},{2,130},{130,2},{3,131},{131,3},{4... | collective-permute-start | bytes 196616 | tf_op jit(solution)/shard_map/ppermute | solution.py:18
  62.3 1.8 %collective-permute-done.22.refs_27_ = bf16[128,256]{1,0:T(8,128)(2,1)S(1)} collective-permute-done((bf16[128,256]{1,0:T(8,128)(2,1)S(1)}, bf16[128,256]{1,0:T(8,128)(2,1)S(1)}, u32[]{:S(2)}, u32[]{:S(2)}) %collective-permute-start.22) | collective-permute-done | bytes 65568 | tf_op jit(solution)/shard_map/ppermute | solution.py:18
  64.2 1.1 collective-permute-start.8
  65.3 2.3 %collective-permute-start.9 = (bf16[64,2048]{1,0:T(8,128)(2,1)S(1)}, bf16[64,2048]{1,0:T(8,128)(2,1)S(1)}, u32[]{:S(2)}, u32[]{:S(2)}) collective-permute-start(bf16[64,2048]{1,0:T(8,128)(2,1)S(1)} %slice.23), channel_id=1, source_target_pairs={{0,112},{16,0},{32,16},{48,32},{64,48},{80,64},{96,80},{112,96},{1... | collective-permute-start | bytes 786440 | tf_op jit(solution)/shard_map/ppermute | solution.py:18
  67.6 1.2 shard_map.99
  68.8 1.3 collective-permute-start.16
  70.1 0.7 pad_maximum_fusion.9
  70.8 1.2 shard_map.101
  71.9 2.7 %collective-permute-done.16.refs_18_ = bf16[128,256]{1,0:T(8,128)(2,1)S(1)} collective-permute-done((bf16[128,256]{1,0:T(8,128)(2,1)S(1)}, bf16[128,256]{1,0:T(8,128)(2,1)S(1)}, u32[]{:S(2)}, u32[]{:S(2)}) %collective-permute-start.16) | collective-permute-done | bytes 65568 | tf_op jit(solution)/shard_map/ppermute | solution.py:18
  74.7 1.2 collective-permute-start.20
  75.9 0.7 pad_maximum_fusion.5
  77.1 1.4 %shard_map.100 = (bf16[128,128]{1,0:T(8,128)(2,1)S(1)}, bf16[128,256]{1,0:T(8,128)(2,1)S(1)}) custom-call(f32[1,1]{1,0:T(1,128)} %constant_dynamic-slice_fusion.temp_ref, bf16[64,2048]{1,0:T(8,128)(2,1)S(1)} %collective-permute-done.8.refs_0_, bf16[64,2048]{1,0:T(8,128)(2,1)S(1)} %collective-permute-done.9.refs_1_, ...), custom_call_target="tpu_custom_call" | custom-call | flops 201326592 | bytes 2293760 | tf_op jit(solution)/shard_map/pallas_call | solution.py:68
  78.5 1.9 %collective-permute-done.20.refs_24_ = bf16[128,256]{1,0:T(8,128)(2,1)S(1)} collective-permute-done((bf16[128,256]{1,0:T(8,128)(2,1)S(1)}, bf16[128,256]{1,0:T(8,128)(2,1)S(1)}, u32[]{:S(2)}, u32[]{:S(2)}) %collective-permute-start.20) | collective-permute-done | bytes 65568 | tf_op jit(solution)/shard_map/ppermute | solution.py:18
  80.4 1.2 collective-permute-start.18
  81.7 0.7 pad_maximum_fusion.7
  82.3 3.9 %collective-permute-done.18.refs_21_ = bf16[128,256]{1,0:T(8,128)(2,1)S(1)} collective-permute-done((bf16[128,256]{1,0:T(8,128)(2,1)S(1)}, bf16[128,256]{1,0:T(8,128)(2,1)S(1)}, u32[]{:S(2)}, u32[]{:S(2)}) %collective-permute-start.18) | collective-permute-done | bytes 65568 | tf_op jit(solution)/shard_map/ppermute | solution.py:18
  86.2 0.7 pad_maximum_fusion.6
  88.1 0.7 copy.30
  89.1 10.3 %shard_map.104 = bf16[1024,128]{1,0:T(8,128)(2,1)S(1)} custom-call(s32[1,1]{1,0:T(1,128)} %bitcast.at_ref, bf16[128,128]{1,0:T(8,128)(2,1)S(1)} %get-tuple-element.18.refs_0_, bf16[128,128]{1,0:T(8,128)(2,1)S(1)} %get-tuple-element.19.refs_1_, bf16[128,128]{1,0:T(8,128)(2,1)S(1)} %get-tuple-element.20.refs_2_, ...), custom_call_target="tpu_custom_call" | custom-call | flops 2147483648 | bytes 4194304 | tf_op jit(solution)/shard_map/pallas_call | solution.py:147
  99.4 19.0 %all_to_all.10.m_ref = bf16[8,128,128]{2,1,0:T(8,128)(2,1)S(1)} all-to-all(bf16[8,128,128]{2,1,0:T(8,128)(2,1)S(1)} %bitcast.65), channel_id=1, replica_groups=mesh['yh'=2,'z'=8,'c'=2,'yl'=2,'x'=4] {'z'}, dimensions={0} | all-to-all | bytes 524288 | tf_op jit(solution)/shard_map/all_to_all | solution.py:239
  118.4 1.5 %shard_map.105 = bf16[128,2048]{1,0:T(8,128)(2,1)} custom-call(bf16[8,128,128]{2,1,0:T(8,128)(2,1)S(1)} %all_to_all.10.m_ref, bf16[1024,2048]{1,0:T(8,128)(2,1)S(1)} %bitcast.62, bf16[128,2048]{1,0:T(8,128)(2,1)S(1)} %bitcast.64), custom_call_target="tpu_custom_call" | custom-call | flops 536870912 | bytes 6291456 | tf_op jit(solution)/shard_map/pallas_call | solution.py:175
  119.9 3.4 %collective-permute-start.26 = (bf16[128,2048]{1,0:T(8,128)(2,1)}, bf16[128,2048]{1,0:T(8,128)(2,1)S(1)}, u32[]{:S(2)}, u32[]{:S(2)}) collective-permute-start(bf16[128,2048]{1,0:T(8,128)(2,1)} %shard_map.105), channel_id=1, source_target_pairs={{0,1},{1,2},{2,3},{3,4},{4,5},{5,6},{6,7},{8,9},{9,10},{10,11},{11... | collective-permute-start | bytes 1572872 | tf_op jit(solution)/shard_map/ppermute | solution.py:24
  123.3 14.6 %collective-permute-done.26 = bf16[128,2048]{1,0:T(8,128)(2,1)S(1)} collective-permute-done((bf16[128,2048]{1,0:T(8,128)(2,1)}, bf16[128,2048]{1,0:T(8,128)(2,1)S(1)}, u32[]{:S(2)}, u32[]{:S(2)}) %collective-permute-start.26) | collective-permute-done | bytes 524320 | tf_op jit(solution)/shard_map/ppermute | solution.py:24
  137.9 0.8 copy.38
  (66 shorter events, 3.7 us)
Async XLA Ops:
  0.6 25.5 %copy-start = (f32[1,8]{1,0:T(1,128)S(1)}, f32[1,8]{1,0:T(1,128)}, u32[]{:S(2)}) copy-start(f32[1,8]{1,0:T(1,128)} %param.15) | copy-start | bytes 100
  0.6 31.9 %copy-start.6 = (s32[4096]{0:T(1024)S(1)}, s32[4096]{0:T(1024)}, u32[]{:S(2)}) copy-start(s32[4096]{0:T(1024)} %param.10) | copy-start | bytes 49156
  2.5 21.1 %all-to-all-start = ((bf16[8,64,256]{2,1,0:T(8,128)(2,1)}), bf16[8,64,256]{2,1,0:T(8,128)(2,1)S(1)}, u32[]{:S(2)}, u32[]{:S(2)}) async-start(bf16[8,64,256]{2,1,0:T(8,128)(2,1)} %maximum_bitcast_fusion), calls=%async_computation | async-start | bytes 524288 | tf_op jit(solution)/shard_map/all_to_all | solution.py:199
  10.9 1.0 copy-start.2
  12.0 0.7 copy-start.4
  12.9 17.2 %collective-permute-start.2 = (bf16[128,2048]{1,0:T(8,128)(2,1)S(1)}, bf16[128,2048]{1,0:T(8,128)(2,1)S(1)}, u32[]{:S(2)}, u32[]{:S(2)}) collective-permute-start(bf16[128,2048]{1,0:T(8,128)(2,1)S(1)} %shard_map.95.refs_0_), channel_id=1, source_target_pairs={{0,112},{16,0},{32,16},{48,32},{64,48},{80,64},{96,80},{112,96},{1... | collective-permute-start | bytes 1572872 | tf_op jit(solution)/shard_map/ppermute | solution.py:18
  16.2 16.1 %collective-permute-start.5 = (bf16[128,2048]{1,0:T(8,128)(2,1)S(1)}, bf16[128,2048]{1,0:T(8,128)(2,1)S(1)}, u32[]{:S(2)}, u32[]{:S(2)}) collective-permute-start(bf16[128,2048]{1,0:T(8,128)(2,1)S(1)} %shard_map.95.refs_0_), channel_id=1, source_target_pairs={{0,16},{16,32},{32,48},{48,64},{64,80},{80,96},{96,112},{112,0},{1... | collective-permute-start | bytes 1572872 | tf_op jit(solution)/shard_map/ppermute | solution.py:18
  23.6 8.7 %collective-permute-start = (bf16[8,64,256]{2,1,0:T(8,128)(2,1)S(1)}, bf16[8,64,256]{2,1,0:T(8,128)(2,1)S(1)}, u32[]{:S(2)}, u32[]{:S(2)}) collective-permute-start(bf16[8,64,256]{2,1,0:T(8,128)(2,1)S(1)} %all-to-all-done), channel_id=1, source_target_pairs={{0,128},{128,0},{1,129},{129,1},{2,130},{130,2},{3,131},{131,3},{4... | collective-permute-start | bytes 786440 | tf_op jit(solution)/shard_map/ppermute | solution.py:18
  25.9 62.0 %copy-start.5 = (s32[2,8,2,128]{3,2,1,0:T(2,128)}, s32[2,8,2,128]{3,2,1,0:T(2,128)S(1)}, u32[]{:S(2)}) copy-start(s32[2,8,2,128]{3,2,1,0:T(2,128)S(1)} %broadcast_select_fusion) | copy-start | bytes 49156
  30.1 12.9 %collective-permute-start.3 = (bf16[128,2048]{1,0:T(8,128)(2,1)S(1)}, bf16[128,2048]{1,0:T(8,128)(2,1)S(1)}, u32[]{:S(2)}, u32[]{:S(2)}) collective-permute-start(bf16[128,2048]{1,0:T(8,128)(2,1)S(1)} %collective-permute-done.2.refs_0_), channel_id=1, source_target_pairs={{0,112},{16,0},{32,16},{48,32},{64,48},{80,64},{96,80},{112,96},{1... | collective-permute-start | bytes 1572872 | tf_op jit(solution)/shard_map/ppermute | solution.py:18
  32.3 13.9 %collective-permute-start.6 = (bf16[128,2048]{1,0:T(8,128)(2,1)S(1)}, bf16[128,2048]{1,0:T(8,128)(2,1)S(1)}, u32[]{:S(2)}, u32[]{:S(2)}) collective-permute-start(bf16[128,2048]{1,0:T(8,128)(2,1)S(1)} %collective-permute-done.5.refs_0_), channel_id=1, source_target_pairs={{0,16},{16,32},{32,48},{48,64},{64,80},{80,96},{96,112},{112,0},{1... | collective-permute-start | bytes 1572872 | tf_op jit(solution)/shard_map/ppermute | solution.py:18
  32.4 13.8 %collective-permute-start.1 = (bf16[2,8,64,256]{3,2,1,0:T(8,128)(2,1)S(1)}, bf16[2,8,64,256]{3,2,1,0:T(8,128)(2,1)S(1)}, u32[]{:S(2)}, u32[]{:S(2)}) collective-permute-start(bf16[2,8,64,256]{3,2,1,0:T(8,128)(2,1)S(1)} %pad_maximum_fusion.1), channel_id=1, source_target_pairs={{0,8},{8,0},{1,9},{9,1},{2,10},{10,2},{3,11},{11,3},{4,12},{12,4},... | collective-permute-start | bytes 1572872 | tf_op jit(solution)/shard_map/ppermute | solution.py:18
  43.0 22.3 %collective-permute-start.4 = (bf16[128,2048]{1,0:T(8,128)(2,1)S(1)}, bf16[128,2048]{1,0:T(8,128)(2,1)S(1)}, u32[]{:S(2)}, u32[]{:S(2)}) collective-permute-start(bf16[128,2048]{1,0:T(8,128)(2,1)S(1)} %collective-permute-done.3.refs_0_), channel_id=1, source_target_pairs={{0,112},{16,0},{32,16},{48,32},{64,48},{80,64},{96,80},{112,96},{1... | collective-permute-start | bytes 1572872 | tf_op jit(solution)/shard_map/ppermute | solution.py:18
  46.2 18.0 %collective-permute-start.7 = (bf16[128,2048]{1,0:T(8,128)(2,1)S(1)}, bf16[128,2048]{1,0:T(8,128)(2,1)S(1)}, u32[]{:S(2)}, u32[]{:S(2)}) collective-permute-start(bf16[128,2048]{1,0:T(8,128)(2,1)S(1)} %collective-permute-done.6.refs_0_), channel_id=1, source_target_pairs={{0,16},{16,32},{32,48},{48,64},{64,80},{80,96},{96,112},{112,0},{1... | collective-permute-start | bytes 1572872 | tf_op jit(solution)/shard_map/ppermute | solution.py:18
  47.5 10.7 %collective-permute-start.10 = (bf16[128,256]{1,0:T(8,128)(2,1)S(1)}, bf16[128,256]{1,0:T(8,128)(2,1)S(1)}, u32[]{:S(2)}, u32[]{:S(2)}) collective-permute-start(bf16[128,256]{1,0:T(8,128)(2,1)S(1)} %get-tuple-element.26.refs_8_), channel_id=1, source_target_pairs={{0,128},{128,0},{1,129},{129,1},{2,130},{130,2},{3,131},{131,3},{4... | collective-permute-start | bytes 196616 | tf_op jit(solution)/shard_map/ppermute | solution.py:18
  51.1 8.5 %collective-permute-start.12 = (bf16[128,256]{1,0:T(8,128)(2,1)S(1)}, bf16[128,256]{1,0:T(8,128)(2,1)S(1)}, u32[]{:S(2)}, u32[]{:S(2)}) collective-permute-start(bf16[128,256]{1,0:T(8,128)(2,1)S(1)} %get-tuple-element.27.refs_11_), channel_id=1, source_target_pairs={{0,128},{128,0},{1,129},{129,1},{2,130},{130,2},{3,131},{131,3},{4... | collective-permute-start | bytes 196616 | tf_op jit(solution)/shard_map/ppermute | solution.py:18
  53.6 8.5 %collective-permute-start.14 = (bf16[128,256]{1,0:T(8,128)(2,1)S(1)}, bf16[128,256]{1,0:T(8,128)(2,1)S(1)}, u32[]{:S(2)}, u32[]{:S(2)}) collective-permute-start(bf16[128,256]{1,0:T(8,128)(2,1)S(1)} %get-tuple-element.28.refs_14_), channel_id=1, source_target_pairs={{0,128},{128,0},{1,129},{129,1},{2,130},{130,2},{3,131},{131,3},{4... | collective-permute-start | bytes 196616 | tf_op jit(solution)/shard_map/ppermute | solution.py:18
  58.3 5.9 %collective-permute-start.22 = (bf16[128,256]{1,0:T(8,128)(2,1)S(1)}, bf16[128,256]{1,0:T(8,128)(2,1)S(1)}, u32[]{:S(2)}, u32[]{:S(2)}) collective-permute-start(bf16[128,256]{1,0:T(8,128)(2,1)S(1)} %get-tuple-element.32.refs_26_), channel_id=1, source_target_pairs={{0,128},{128,0},{1,129},{129,1},{2,130},{130,2},{3,131},{131,3},{4... | collective-permute-start | bytes 196616 | tf_op jit(solution)/shard_map/ppermute | solution.py:18
  59.6 9.2 %collective-permute-start.24 = (bf16[128,256]{1,0:T(8,128)(2,1)S(1)}, bf16[128,256]{1,0:T(8,128)(2,1)S(1)}, u32[]{:S(2)}, u32[]{:S(2)}) collective-permute-start(bf16[128,256]{1,0:T(8,128)(2,1)S(1)} %get-tuple-element.33.refs_29_), channel_id=1, source_target_pairs={{0,128},{128,0},{1,129},{129,1},{2,130},{130,2},{3,131},{131,3},{4... | collective-permute-start | bytes 196616 | tf_op jit(solution)/shard_map/ppermute | solution.py:18
  62.0 24.8 %collective-permute-start.11 = (bf16[2,128,256]{2,1,0:T(8,128)(2,1)S(1)}, bf16[2,128,256]{2,1,0:T(8,128)(2,1)S(1)}, u32[]{:S(2)}, u32[]{:S(2)}) collective-permute-start(bf16[2,128,256]{2,1,0:T(8,128)(2,1)S(1)} %pad_maximum_fusion.2), channel_id=1, source_target_pairs={{0,8},{8,0},{1,9},{9,1},{2,10},{10,2},{3,11},{11,3},{4,12},{12,4},... | collective-permute-start | bytes 393224 | tf_op jit(solution)/shard_map/ppermute | solution.py:18
  64.1 23.2 %collective-permute-start.13 = (bf16[2,128,256]{2,1,0:T(8,128)(2,1)S(1)}, bf16[2,128,256]{2,1,0:T(8,128)(2,1)S(1)}, u32[]{:S(2)}, u32[]{:S(2)}) collective-permute-start(bf16[2,128,256]{2,1,0:T(8,128)(2,1)S(1)} %pad_maximum_fusion.3), channel_id=1, source_target_pairs={{0,8},{8,0},{1,9},{9,1},{2,10},{10,2},{3,11},{11,3},{4,12},{12,4},... | collective-permute-start | bytes 393224 | tf_op jit(solution)/shard_map/ppermute | solution.py:18
  64.2 12.4 %collective-permute-start.8 = (bf16[64,2048]{1,0:T(8,128)(2,1)S(1)}, bf16[64,2048]{1,0:T(8,128)(2,1)S(1)}, u32[]{:S(2)}, u32[]{:S(2)}) collective-permute-start(bf16[64,2048]{1,0:T(8,128)(2,1)S(1)} %slice.22), channel_id=1, source_target_pairs={{0,16},{16,32},{32,48},{48,64},{64,80},{80,96},{96,112},{112,0},{1... | collective-permute-start | bytes 786440 | tf_op jit(solution)/shard_map/ppermute | solution.py:18
  65.3 11.3 %collective-permute-start.9 = (bf16[64,2048]{1,0:T(8,128)(2,1)S(1)}, bf16[64,2048]{1,0:T(8,128)(2,1)S(1)}, u32[]{:S(2)}, u32[]{:S(2)}) collective-permute-start(bf16[64,2048]{1,0:T(8,128)(2,1)S(1)} %slice.23), channel_id=1, source_target_pairs={{0,112},{16,0},{32,16},{48,32},{64,48},{80,64},{96,80},{112,96},{1... | collective-permute-start | bytes 786440 | tf_op jit(solution)/shard_map/ppermute | solution.py:18
  68.8 5.9 %collective-permute-start.16 = (bf16[128,256]{1,0:T(8,128)(2,1)S(1)}, bf16[128,256]{1,0:T(8,128)(2,1)S(1)}, u32[]{:S(2)}, u32[]{:S(2)}) collective-permute-start(bf16[128,256]{1,0:T(8,128)(2,1)S(1)} %get-tuple-element.29.refs_17_), channel_id=1, source_target_pairs={{0,128},{128,0},{1,129},{129,1},{2,130},{130,2},{3,131},{131,3},{4... | collective-permute-start | bytes 196616 | tf_op jit(solution)/shard_map/ppermute | solution.py:18
  74.7 5.8 %collective-permute-start.20 = (bf16[128,256]{1,0:T(8,128)(2,1)S(1)}, bf16[128,256]{1,0:T(8,128)(2,1)S(1)}, u32[]{:S(2)}, u32[]{:S(2)}) collective-permute-start(bf16[128,256]{1,0:T(8,128)(2,1)S(1)} %get-tuple-element.31.refs_23_), channel_id=1, source_target_pairs={{0,128},{128,0},{1,129},{129,1},{2,130},{130,2},{3,131},{131,3},{4... | collective-permute-start | bytes 196616 | tf_op jit(solution)/shard_map/ppermute | solution.py:18
  76.6 10.9 %collective-permute-start.15 = (bf16[2,128,256]{2,1,0:T(8,128)(2,1)S(1)}, bf16[2,128,256]{2,1,0:T(8,128)(2,1)S(1)}, u32[]{:S(2)}, u32[]{:S(2)}) collective-permute-start(bf16[2,128,256]{2,1,0:T(8,128)(2,1)S(1)} %pad_maximum_fusion.4), channel_id=1, source_target_pairs={{0,8},{8,0},{1,9},{9,1},{2,10},{10,2},{3,11},{11,3},{4,12},{12,4},... | collective-permute-start | bytes 393224 | tf_op jit(solution)/shard_map/ppermute | solution.py:18
  76.6 12.3 %collective-permute-start.23 = (bf16[2,128,256]{2,1,0:T(8,128)(2,1)S(1)}, bf16[2,128,256]{2,1,0:T(8,128)(2,1)S(1)}, u32[]{:S(2)}, u32[]{:S(2)}) collective-permute-start(bf16[2,128,256]{2,1,0:T(8,128)(2,1)S(1)} %pad_maximum_fusion.8), channel_id=1, source_target_pairs={{0,8},{8,0},{1,9},{9,1},{2,10},{10,2},{3,11},{11,3},{4,12},{12,4},... | collective-permute-start | bytes 393224 | tf_op jit(solution)/shard_map/ppermute | solution.py:18
  80.4 5.8 %collective-permute-start.18 = (bf16[128,256]{1,0:T(8,128)(2,1)S(1)}, bf16[128,256]{1,0:T(8,128)(2,1)S(1)}, u32[]{:S(2)}, u32[]{:S(2)}) collective-permute-start(bf16[128,256]{1,0:T(8,128)(2,1)S(1)} %get-tuple-element.30.refs_20_), channel_id=1, source_target_pairs={{0,128},{128,0},{1,129},{129,1},{2,130},{130,2},{3,131},{131,3},{4... | collective-permute-start | bytes 196616 | tf_op jit(solution)/shard_map/ppermute | solution.py:18
  86.2 2.7 %collective-permute-start.25 = (bf16[2,128,256]{2,1,0:T(8,128)(2,1)}, bf16[2,128,256]{2,1,0:T(8,128)(2,1)S(1)}, u32[]{:S(2)}, u32[]{:S(2)}) collective-permute-start(bf16[2,128,256]{2,1,0:T(8,128)(2,1)} %pad_maximum_fusion.9), channel_id=1, source_target_pairs={{0,8},{8,0},{1,9},{9,1},{2,10},{10,2},{3,11},{11,3},{4,12},{12,4},... | collective-permute-start | bytes 393224 | tf_op jit(solution)/shard_map/ppermute | solution.py:18
  86.9 2.0 %collective-permute-start.17 = (bf16[2,128,256]{2,1,0:T(8,128)(2,1)}, bf16[2,128,256]{2,1,0:T(8,128)(2,1)S(1)}, u32[]{:S(2)}, u32[]{:S(2)}) collective-permute-start(bf16[2,128,256]{2,1,0:T(8,128)(2,1)} %pad_maximum_fusion.5), channel_id=1, source_target_pairs={{0,8},{8,0},{1,9},{9,1},{2,10},{10,2},{3,11},{11,3},{4,12},{12,4},... | collective-permute-start | bytes 393224 | tf_op jit(solution)/shard_map/ppermute | solution.py:18
  87.4 1.6 %collective-permute-start.21 = (bf16[2,128,256]{2,1,0:T(8,128)(2,1)}, bf16[2,128,256]{2,1,0:T(8,128)(2,1)S(1)}, u32[]{:S(2)}, u32[]{:S(2)}) collective-permute-start(bf16[2,128,256]{2,1,0:T(8,128)(2,1)} %pad_maximum_fusion.7), channel_id=1, source_target_pairs={{0,8},{8,0},{1,9},{9,1},{2,10},{10,2},{3,11},{11,3},{4,12},{12,4},... | collective-permute-start | bytes 393224 | tf_op jit(solution)/shard_map/ppermute | solution.py:18
  87.5 1.7 %collective-permute-start.19 = (bf16[2,128,256]{2,1,0:T(8,128)(2,1)}, bf16[2,128,256]{2,1,0:T(8,128)(2,1)S(1)}, u32[]{:S(2)}, u32[]{:S(2)}) collective-permute-start(bf16[2,128,256]{2,1,0:T(8,128)(2,1)} %pad_maximum_fusion.6), channel_id=1, source_target_pairs={{0,8},{8,0},{1,9},{9,1},{2,10},{10,2},{3,11},{11,3},{4,12},{12,4},... | collective-permute-start | bytes 393224 | tf_op jit(solution)/shard_map/ppermute | solution.py:18
  89.1 29.3 %copy-start.1 = (bf16[1,1024,2048]{2,1,0:T(8,128)(2,1)S(1)}, bf16[1,1024,2048]{2,1,0:T(8,128)(2,1)}, u32[]{:S(2)}) copy-start(bf16[1,1024,2048]{2,1,0:T(8,128)(2,1)} %param.14) | copy-start | bytes 12582916
  89.1 29.3 %copy-start.3 = (bf16[1,128,2048]{2,1,0:T(8,128)(2,1)S(1)}, bf16[1,128,2048]{2,1,0:T(8,128)(2,1)}, u32[]{:S(2)}) copy-start(bf16[1,128,2048]{2,1,0:T(8,128)(2,1)} %param.8) | copy-start | bytes 1572868
  119.9 18.0 %collective-permute-start.26 = (bf16[128,2048]{1,0:T(8,128)(2,1)}, bf16[128,2048]{1,0:T(8,128)(2,1)S(1)}, u32[]{:S(2)}, u32[]{:S(2)}) collective-permute-start(bf16[128,2048]{1,0:T(8,128)(2,1)} %shard_map.105), channel_id=1, source_target_pairs={{0,1},{1,2},{2,3},{3,4},{4,5},{5,6},{6,7},{8,9},{9,10},{10,11},{11... | collective-permute-start | bytes 1572872 | tf_op jit(solution)/shard_map/ppermute | solution.py:24

commit v2 on v1

v2 whole, which is shorter than its diff:
```python
import functools

import jax
import jax.numpy as jnp
import numpy as np
from jax import lax
from jax.experimental import pallas as pl
from jax.experimental.pallas import tpu as pltpu
from jax.sharding import Mesh
from jax.sharding import PartitionSpec as P

ZS = 8
EARLY, LATE = (0, 1, 7, 2, 6), (3, 5, 4)
MIB = 1024 * 1024


def shifted(block, axis, distance):
    count = lax.axis_size(axis)
    return lax.ppermute(block, axis, [(i, (i + distance) % count) for i in range(count)])


def passed_along(block, axis, distance):
    devices = range(lax.axis_size(axis))
    route = [(i - distance, i) for i in devices if i - distance in devices]
    return lax.ppermute(block, axis, route)


def params(mib):
    return pltpu.CompilerParams(vmem_limit_bytes=mib * MIB)


def entry_kernel(x_ref, g_ref, w_ref, upper_ref, lower_ref, p_ref):
    half = upper_ref.shape[0]
    for part, n_ref in enumerate((upper_ref, lower_ref)):
        x = x_ref[part * half : (part + 1) * half, :].astype(jnp.float32)
        n_ref[...] = (
            x * lax.rsqrt(jnp.mean(x * x, axis=-1, keepdims=True) + 1e-05) * g_ref[...]
        ).astype(jnp.bfloat16)
    heads, _, wide = p_ref.shape
    width, head_dim = heads * wide // 2, wide // 2
    for h in range(heads):
        p_ref[h, :, :head_dim] = w_ref[:, h * head_dim : (h + 1) * head_dim]
        p_ref[h, :, head_dim:] = w_ref[:, width + h * head_dim : width + (h + 1) * head_dim]


def entry(x, gain, slab, heads):
    rows, columns = slab.shape
    return pl.pallas_call(
        entry_kernel,
        out_shape=[
            *[jax.ShapeDtypeStruct((x.shape[0] // 2, x.shape[1]), jnp.bfloat16)] * 2,
            jax.ShapeDtypeStruct((heads, rows, columns // heads), jnp.bfloat16),
        ],
        compiler_params=params(16),
        cost_estimate=pl.CostEstimate(flops=0, bytes_accessed=3 * x.size * 2, transcendentals=0),
    )(x, gain, slab)


def assemble_kernel(at_ref, own, across, over, both, w_ref):
    rings, rows, _ = own.shape
    yh, core = at_ref[0], at_ref[1]
    for place, part in enumerate((own, across, over, both)):
        half, side = yh ^ (place // 2), core ^ (place % 2)
        for z in range(rings):
            start = half * (2 * rings * rows) + side * rows + z * 2 * rows
            w_ref[pl.ds(pl.multiple_of(start, rows), rows), :] = part[z]


def assembled(at, *parts):
    rings, rows, columns = parts[0].shape
    vmem = pl.BlockSpec(memory_space=pltpu.VMEM)
    return pl.pallas_call(
        assemble_kernel,
        in_specs=[pl.BlockSpec(memory_space=pltpu.SMEM)] + [vmem] * 4,
        out_specs=vmem,
        out_shape=jax.ShapeDtypeStruct((4 * rings * rows, columns), jnp.bfloat16),
        compiler_params=params(16),
        cost_estimate=pl.CostEstimate(flops=0, bytes_accessed=2 * MIB, transcendentals=0),
    )(at, *parts)


def project_kernel(count, temp_ref, *refs):
    blocks, (wq_ref, wkv_ref, q_ref, kv_ref) = refs[:count], refs[count:]
    head_dim = wq_ref.shape[1]
    x = jnp.concatenate([block[...] for block in blocks], axis=0)
    q = jnp.dot(x, wq_ref[...], preferred_element_type=jnp.float32)
    kv = jnp.dot(x, wkv_ref[...], preferred_element_type=jnp.float32)
    k = kv[:, :head_dim]
    q_scale = lax.rsqrt(jnp.mean(q * q, axis=-1, keepdims=True) + 1e-06)
    q_ref[...] = (q * q_scale * temp_ref[0, 0] / head_dim).astype(jnp.bfloat16)
    k_scale = lax.rsqrt(jnp.mean(k * k, axis=-1, keepdims=True) + 1e-06)
    kv_ref[:, :head_dim] = (k * k_scale).astype(jnp.bfloat16)
    kv_ref[:, head_dim:] = kv[:, head_dim:].astype(jnp.bfloat16)


def projected(blocks, wq, wkv, temp):
    rows = sum(b.shape[0] for b in blocks)
    vmem = pl.BlockSpec(memory_space=pltpu.VMEM)
    return pl.pallas_call(
        functools.partial(project_kernel, len(blocks)),
        in_specs=[pl.BlockSpec(memory_space=pltpu.SMEM)] + [vmem] * (len(blocks) + 2),
        out_specs=[vmem, vmem],
        out_shape=[
            jax.ShapeDtypeStruct((rows, wq.shape[1]), jnp.bfloat16),
            jax.ShapeDtypeStruct((rows, wkv.shape[1]), jnp.bfloat16),
        ],
        compiler_params=params(32),
        cost_estimate=pl.CostEstimate(
            flops=2 * rows * 2048 * 384, bytes_accessed=rows * 5632 + 1572864, transcendentals=0
        ),
    )(temp, *blocks, wq, wkv)


def masked_scores(q, keyval, places, qpos, qspan, s_all, column, peak):
    head_dim = q.shape[1]
    s = lax.dot_general(
        q, keyval[:, :head_dim], (((1,), (1,)), ((), ())), preferred_element_type=jnp.float32
    )
    for u, place in enumerate(places):
        lanes = slice(u * 128, (u + 1) * 128)
        part = jnp.where(qpos - place <= qspan, s[:, lanes], -1e30)
        s_all[:, column + u * 128 : column + (u + 1) * 128] = part
        peak = jnp.maximum(peak, part)
    return peak


def mixing(s_all, column, keyval, top, total, mixed):
    rows, head_dim = keyval.shape[0], keyval.shape[1] // 2
    parts = []
    for u in range(rows // 128):
        w = jnp.exp(s_all[:, column + u * 128 : column + (u + 1) * 128] - top)
        total = total + w
        parts.append(w.astype(jnp.bfloat16))
    w = jnp.concatenate(parts, axis=1)
    return total, mixed + jnp.dot(w, keyval[:, head_dim:], preferred_element_type=jnp.float32)


def chunks(segments, kpos_ref, most=512):
    column = 0
    for keyval, place, offsets in segments:
        for start in range(0, keyval.shape[0], most):
            size = min(most, keyval.shape[0] - start)
            places = [
                kpos_ref[place : place + 1, o * 128 : (o + 1) * 128]
                for o in offsets[start // 128 : (start + size) // 128]
            ]
            yield column, keyval, slice(start, start + size), places
            column += size


TILE = 256


def tile_of(t, at_ref, qpos_ref, qspan_ref):
    qpos, qspan = [], []
    for i in range(TILE // 128):
        placed = pl.ds(pl.multiple_of(at_ref[0, t * (TILE // 128) + i] * 128, 128), 128)
        qpos.append(jnp.broadcast_to(qpos_ref[placed, :], (128, 128)))
        qspan.append(jnp.broadcast_to(qspan_ref[placed, :], (128, 128)))
    rows = pl.ds(pl.multiple_of(t * TILE, TILE), TILE)
    return rows, jnp.concatenate(qpos, axis=0), jnp.concatenate(qspan, axis=0)


def weighed(q, peak, segments, kpos_ref, qpos, qspan, s_all):
    for column, keyval, cut, places in chunks(segments, kpos_ref):
        peak = masked_scores(q, keyval[cut, :], places, qpos, qspan, s_all, column, peak)
    top = jnp.broadcast_to(jnp.max(peak, axis=-1, keepdims=True), peak.shape)
    total = jnp.zeros((TILE, 128), jnp.float32)
    mixed = jnp.zeros((TILE, q.shape[1]), jnp.float32)
    for column, keyval, cut, _ in chunks(segments, kpos_ref):
        total, mixed = mixing(s_all, column, keyval[cut, :], top, total, mixed)
    return top, total, mixed


def first_kernel(at_ref, qa, qb, own_a, own_b, ca, ya, xa, qpos_ref, qspan_ref, kpos_ref, q_out, acc, top_out, total_out, s_all):
    early, late = qa.shape[0], qb.shape[0]
    q_out[pl.ds(0, early), :] = qa[...]
    q_out[pl.ds(early, late), :] = qb[...]
    segments = [(own_a, 0, EARLY), (own_b, 0, LATE)]
    segments += [(ca, 1, EARLY), (ya, 2, EARLY), (xa, 3, EARLY)]

    def one_tile(t, _):
        rows, qpos, qspan = tile_of(t, at_ref, qpos_ref, qspan_ref)
        peak = jnp.full((TILE, 128), -1e30, jnp.float32)
        top, total, mixed = weighed(q_out[rows, :], peak, segments, kpos_ref, qpos, qspan, s_all)
        acc[rows, :] = mixed
        total_out[rows, :] = total
        top_out[rows, :] = top
        return 0

    lax.fori_loop(0, (early + late) // TILE, one_tile, 0)


def second_kernel(at_ref, q_ref, acc, top_ref, total_ref, cb, yb, xb, qpos_ref, qspan_ref, kpos_ref, o_ref, s_all):
    segments = [(cb, 1, LATE), (yb, 2, LATE), (xb, 3, LATE)]

    def one_tile(t, _):
        rows, qpos, qspan = tile_of(t, at_ref, qpos_ref, qspan_ref)
        before = top_ref[rows, :]
        top, total, mixed = weighed(q_ref[rows, :], before, segments, kpos_ref, qpos, qspan, s_all)
        kept = jnp.exp(before - top)
        summed = acc[rows, :] * kept + mixed
        weight = jnp.sum(total_ref[rows, :] * kept + total, axis=-1, keepdims=True)
        result = (summed / weight).astype(jnp.bfloat16)
        for i in range(TILE // 128):
            placed = pl.ds(pl.multiple_of(at_ref[1, t * (TILE // 128) + i] * 128, 128), 128)
            o_ref[placed, :] = result[i * 128 : (i + 1) * 128, :]
        return 0

    lax.fori_loop(0, q_ref.shape[0] // TILE, one_tile, 0)


def attended_first(at, queries, own, others, qpos, qspan, kpos):
    early, late = (q.shape[0] for q in queries)
    rows, head_dim = early + late, queries[0].shape[1]
    keys = rows + 3 * early
    wide = jax.ShapeDtypeStruct((rows, head_dim), jnp.float32)
    vmem = pl.BlockSpec(memory_space=pltpu.VMEM)
    return pl.pallas_call(
        first_kernel,
        in_specs=[pl.BlockSpec(memory_space=pltpu.SMEM)] + [vmem] * 10,
        out_specs=[vmem] * 4,
        out_shape=[jax.ShapeDtypeStruct((rows, head_dim), jnp.bfloat16), wide, wide, wide],
        scratch_shapes=[pltpu.VMEM((TILE, keys), jnp.float32)],
        compiler_params=params(24),
        cost_estimate=pl.CostEstimate(
            flops=40 * rows * keys * head_dim, bytes_accessed=4 * keys * head_dim, transcendentals=rows * keys
        ),
    )(at, *queries, *own, *others, qpos, qspan, kpos)


def attended_second(at, state, others, qpos, qspan, kpos):
    rows, head_dim = state[0].shape
    keys = 3 * others[0].shape[0]
    vmem = pl.BlockSpec(memory_space=pltpu.VMEM)
    return pl.pallas_call(
        second_kernel,
        in_specs=[pl.BlockSpec(memory_space=pltpu.SMEM)] + [vmem] * 10,
        out_specs=vmem,
        out_shape=jax.ShapeDtypeStruct((rows, head_dim), jnp.bfloat16),
        scratch_shapes=[pltpu.VMEM((TILE, keys), jnp.float32)],
        compiler_params=params(24),
        cost_estimate=pl.CostEstimate(
            flops=40 * rows * keys * head_dim, bytes_accessed=4 * keys * head_dim, transcendentals=rows * keys
        ),
    )(at, *state, *others, qpos, qspan, kpos)


def output_kernel(m_ref, w_ref, x_ref, o_ref):
    mixed = jnp.concatenate([m_ref[h] for h in range(m_ref.shape[0])], axis=1)
    wide = 512
    for t in range(w_ref.shape[1] // wide):
        lanes = slice(t * wide, (t + 1) * wide)
        added = jnp.dot(mixed, w_ref[:, lanes], preferred_element_type=jnp.float32)
        o_ref[:, lanes] = (x_ref[:, lanes].astype(jnp.float32) + added).astype(jnp.bfloat16)


def outputs(mixed, w_out, x):
    return pl.pallas_call(
        output_kernel,
        out_shape=jax.ShapeDtypeStruct(x.shape, jnp.bfloat16),
        compiler_params=params(24),
        cost_estimate=pl.CostEstimate(
            flops=2 * 128 * 1024 * 2048, bytes_accessed=6 * MIB, transcendentals=0
        ),
    )(mixed, w_out, x)


def per_device(acts, order, doc_ids, gain, w_query, w_keyval, w_out, head_temp):
    inputs = acts[0]
    width = w_query.shape[2]
    heads = head_temp.shape[1]
    head_dim = width // heads
    yh, z, c = (lax.axis_index(a).astype(jnp.int32) for a in ("yh", "z", "c"))

    upper, lower, by_head = entry(inputs, gain, w_keyval[0], heads)

    blocks = {(0, 0): upper, (0, 1): lower}
    for distance in (1, 2, 3):
        for part in (0, 1):
            blocks[-distance, part] = shifted(blocks[1 - distance, part], "z", 1)
            blocks[distance, part] = shifted(blocks[distance - 1, part], "z", -1)
    blocks[4, 0] = shifted(blocks[-3, 0], "z", 1)
    blocks[4, 1] = shifted(blocks[3, 1], "z", -1)

    def rows_of(offset):
        at_offset = offset if offset <= 4 else offset - ZS
        return [blocks[at_offset, 0], blocks[at_offset, 1]]

    own_w = lax.all_to_all(by_head, "z", 0, 0, tiled=True)
    other_w = shifted(own_w, "yh", 1)
    wkv = assembled(jnp.stack([yh, c]), own_w, shifted(own_w, "c", 1), other_w, shifted(other_w, "c", 1))
    wq = lax.dynamic_slice_in_dim(w_query[0], z * head_dim, head_dim, axis=1)
    temp = lax.dynamic_slice_in_dim(head_temp, z, 1, axis=1)

    grid = order.reshape(2, ZS, 2, -1)
    grid = lax.dynamic_slice_in_dim(jnp.concatenate([grid, grid], axis=1), z, ZS, axis=1)
    grid = jnp.where(yh == 0, grid, grid[::-1])
    grid = jnp.where(c == 0, grid, grid[:, :, ::-1])
    kpos = grid.transpose(0, 2, 1, 3).reshape(4, -1)
    begins = jnp.sum(
        (doc_ids[None, :] < jnp.arange(1, 8, dtype=jnp.int32)[:, None]).astype(jnp.int32), axis=1
    )
    own_pos = kpos[0].reshape(-1, 1)
    began = jnp.max(jnp.where(begins[None, :] <= own_pos, begins[None, :], 0), axis=1, keepdims=True)
    lowest = jnp.int32(-(2**31))
    qspan = own_pos - began + lowest
    qpos = own_pos + lowest

    q_early, kv_early = projected(sum([rows_of(o) for o in EARLY], []), wq, wkv, temp)
    q_late, kv_late = projected(sum([rows_of(o) for o in LATE], []), wq, wkv, temp)
    over_early = shifted(kv_early, "yh", 1)
    kv_late, over_later = lax.optimization_barrier((kv_late, over_early))
    others_early = [shifted(kv_early, "c", 1), over_early, shifted(over_later, "c", 1)]
    others_late = [lax.ppermute(kv_late, ("yh", "c"), [(i, i ^ k) for i in range(4)]) for k in (1, 2, 3)]
    offsets = jnp.array(EARLY + LATE, jnp.int32)
    at = jnp.stack([offsets, lax.rem(z + offsets, ZS)])
    state = attended_first(at, [q_early, q_late], [kv_early, kv_late], others_early, qpos, qspan, kpos)
    mixed = attended_second(at, state, others_late, qpos, qspan, kpos)

    mixed = lax.all_to_all(mixed.reshape(ZS, -1, head_dim), "z", 0, 0, tiled=True)
    produced = outputs(mixed, w_out[0], inputs)
    handed = passed_along(produced, ("yl", "x"), 1)
    return (produced[None], handed[None])


def solution(mesh):
    devices = np.asarray(mesh.devices).reshape(2, ZS, 2, 2, 4)
    fine = Mesh(devices, ("yh", "z", "c", "yl", "x"))
    phase, blk = ("yl", "x"), ("yh", "z", "c")
    return jax.shard_map(
        per_device,
        mesh=fine,
        in_specs=(
            P(phase, blk, None),
            P(),
            P(),
            P(phase, None),
            P(phase, None, None),
            P(phase, blk, None),
            P(phase, None, None),
            P(phase, None),
        ),
        out_specs=(P(phase, blk, None), P(phase, blk, None)),
        check_vma=False,
    )
```

time: 139 us -> 118 us (0.85)
  waiting for transfers between devices: 44.2 us -> 32.4 us
  blocking collectives: 19 us -> 15.4 us
  other arithmetic: 4.79 us -> 1.95 us
  Pallas kernels: 21.5 us -> 19.7 us
    ppermute x26 -> x20, waiting for transfers between devices: 23.1 us -> 13.2 us  [shifted(): lax.ppermute(block, axis, [(i, (i + distance) % count) for i in range(cou...]
    pallas_call x8 -> x2, Pallas kernels: 9.49 us -> 5.02 us  [projected(): pl.pallas_call(functools.partial(project_kernel, len(blocks)), in_specs=[...]
    all_to_all x1, waiting for transfers between devices: 6.56 us -> 2.57 us  [per_device(): own_w = lax.all_to_all(by_head, 'z', 0, 0, tiled=True)]
    all_to_all x1, starting transfers between devices: 8.47 us -> 4.51 us  [per_device(): own_w = lax.all_to_all(by_head, 'z', 0, 0, tiled=True)]
    ppermute x0 -> x3, starting transfers between devices: none -> 3.55 us  [per_device(): lax.ppermute(kv_late, ('yh', 'c'), [(i, i ^ k) for i in range(4)])]
    all_to_all x1, blocking collectives: 19 us -> 15.4 us  [per_device(): lax.all_to_all(mixed.reshape(ZS, -1, head_dim), 'z', 0, 0, tiled=True)]
    another operation x12 -> x3, other arithmetic: 2.98 us -> 0.09 us  [the longest x1 0.07 us: per_device(): jnp.stack([yh, c])]
    pallas_call x2 -> x4, Pallas kernels: 10.5 us -> 13.2 us  [the longest x1 7.06 us: attended_first(): pl.pallas_call(first_kernel, in_specs=[pl.BlockSpec(memory_space=pltpu.SM...]
  transfers between devices with their start and end apart: 28 -> 25, of which waited for: 10 -> 9; matrix products, arithmetic and copies ran while one was open for 5% -> 3% of each run, Pallas kernels for 7% -> 11%
where the time goes in v2:
time: 118 us
  starting transfers between devices  41.1 us (35%)
  waiting for transfers between devices  32.4 us (27%)
  Pallas kernels  19.7 us (17%)
  blocking collectives  15.4 us (13%)
  local copies, waits for them, and re-layouts  6.34 us (5%)
  other arithmetic  1.95 us (2%)
    ppermute x20, starting transfers between devices, shifted(): lax.ppermute(block, axis, [(i, (i + distance) % count) for i in range(cou...  29.7 us
    all_to_all x1, blocking collectives, per_device(): lax.all_to_all(mixed.reshape(ZS, -1, head_dim), 'z', 0, 0, tiled=True)  15.4 us
    ppermute x1, waiting for transfers between devices, passed_along(): return lax.ppermute(block, axis, route)  14.8 us
    ppermute x20, waiting for transfers between devices, shifted(): lax.ppermute(block, axis, [(i, (i + distance) % count) for i in range(cou...  13.2 us
    pallas_call x1, Pallas kernels, attended_first(): pl.pallas_call(first_kernel, in_specs=[pl.BlockSpec(memory_space=pltpu.SM...  7.06 us
    pallas_call x2, Pallas kernels, projected(): pl.pallas_call(functools.partial(project_kernel, len(blocks)), in_specs=[...  5.02 us
    all_to_all x1, starting transfers between devices, per_device(): own_w = lax.all_to_all(by_head, 'z', 0, 0, tiled=True)  4.51 us
    unnamed x22, local copies, waits for them, and re-layouts  4.18 us
  transfers between devices with their start and end apart: 25, of which 9 were waited for; matrix products, arithmetic and copies ran while one was open for 3% of the time, Pallas kernels for 11%

profile of v2, /device:TPU:8, one launch (start us, length us, event | category | flops | bytes accessed | tf_op | source)
XLA Modules:
  0.0 117.9 jit_solution(2722337753894827180)
XLA Ops:
  0.7 1.0 copy-done.2
  1.7 0.9 copy-done.4
  2.6 0.7 copy-done.5
  3.3 0.9 shard_map.104
  4.3 5.9 %collective-permute-start = (bf16[64,2048]{1,0:T(8,128)(2,1)S(1)}, bf16[64,2048]{1,0:T(8,128)(2,1)S(1)}, u32[]{:S(2)}, u32[]{:S(2)}) collective-permute-start(bf16[64,2048]{1,0:T(8,128)(2,1)S(1)} %get-tuple-element.15.refs_0_), channel_id=1, source_target_pairs={{0,112},{16,0},{32,16},{48,32},{64,48},{80,64},{96,80},{112,96},{1... | collective-permute-start | bytes 786440 | tf_op jit(solution)/shard_map/ppermute | solution.py:19
  10.1 3.2 %collective-permute-start.1 = (bf16[64,2048]{1,0:T(8,128)(2,1)S(1)}, bf16[64,2048]{1,0:T(8,128)(2,1)S(1)}, u32[]{:S(2)}, u32[]{:S(2)}) collective-permute-start(bf16[64,2048]{1,0:T(8,128)(2,1)S(1)} %get-tuple-element.16.refs_1_), channel_id=1, source_target_pairs={{0,112},{16,0},{32,16},{48,32},{64,48},{80,64},{96,80},{112,96},{1... | collective-permute-start | bytes 786440 | tf_op jit(solution)/shard_map/ppermute | solution.py:19
  13.4 4.5 %all-to-all-start = ((bf16[8,64,256]{2,1,0:T(8,128)(2,1)}), bf16[8,64,256]{2,1,0:T(8,128)(2,1)S(1)}, u32[]{:S(2)}, u32[]{:S(2)}) async-start(bf16[8,64,256]{2,1,0:T(8,128)(2,1)} %get-tuple-element.17), calls=%async_computation | async-start | bytes 524288 | tf_op jit(solution)/shard_map/all_to_all | solution.py:290
  17.9 0.7 fusion
  18.7 3.3 %collective-permute-start.4 = (bf16[64,2048]{1,0:T(8,128)(2,1)S(1)}, bf16[64,2048]{1,0:T(8,128)(2,1)S(1)}, u32[]{:S(2)}, u32[]{:S(2)}) collective-permute-start(bf16[64,2048]{1,0:T(8,128)(2,1)S(1)} %collective-permute-done.refs_2_), channel_id=1, source_target_pairs={{0,112},{16,0},{32,16},{48,32},{64,48},{80,64},{96,80},{112,96},{1... | collective-permute-start | bytes 786440 | tf_op jit(solution)/shard_map/ppermute | solution.py:19
  22.0 3.4 %collective-permute-done.1.refs_3_ = bf16[64,2048]{1,0:T(8,128)(2,1)S(1)} collective-permute-done((bf16[64,2048]{1,0:T(8,128)(2,1)S(1)}, bf16[64,2048]{1,0:T(8,128)(2,1)S(1)}, u32[]{:S(2)}, u32[]{:S(2)}) %collective-permute-start.1) | collective-permute-done | bytes 262176 | tf_op jit(solution)/shard_map/ppermute | solution.py:19
  25.5 3.8 %collective-permute-start.5 = (bf16[64,2048]{1,0:T(8,128)(2,1)S(1)}, bf16[64,2048]{1,0:T(8,128)(2,1)S(1)}, u32[]{:S(2)}, u32[]{:S(2)}) collective-permute-start(bf16[64,2048]{1,0:T(8,128)(2,1)S(1)} %collective-permute-done.1.refs_3_), channel_id=1, source_target_pairs={{0,112},{16,0},{32,16},{48,32},{64,48},{80,64},{96,80},{112,96},{1... | collective-permute-start | bytes 786440 | tf_op jit(solution)/shard_map/ppermute | solution.py:19
  29.3 2.6 %all-to-all-done.own = bf16[8,64,256]{2,1,0:T(8,128)(2,1)S(1)} async-done(((bf16[8,64,256]{2,1,0:T(8,128)(2,1)}), bf16[8,64,256]{2,1,0:T(8,128)(2,1)S(1)}, u32[]{:S(2)}, u32[]{:S(2)}) %all-to-all-start) | async-done | bytes 262176 | tf_op jit(solution)/shard_map/all_to_all | solution.py:290
  31.9 2.3 %collective-permute-start.9 = (bf16[8,64,256]{2,1,0:T(8,128)(2,1)S(1)}, bf16[8,64,256]{2,1,0:T(8,128)(2,1)S(1)}, u32[]{:S(2)}, u32[]{:S(2)}) collective-permute-start(bf16[8,64,256]{2,1,0:T(8,128)(2,1)S(1)} %all-to-all-done.own), channel_id=1, source_target_pairs={{0,128},{128,0},{1,129},{129,1},{2,130},{130,2},{3,131},{131,3},{4... | collective-permute-start | bytes 786440 | tf_op jit(solution)/shard_map/ppermute | solution.py:19
  34.2 0.9 convert_reduce_fusion
  35.1 0.1 collective-permute-start.7
  35.2 0.1 collective-permute-start.8
  35.3 3.3 %collective-permute-done.6.refs_8_ = bf16[64,2048]{1,0:T(8,128)(2,1)S(1)} collective-permute-done((bf16[64,2048]{1,0:T(8,128)(2,1)S(1)}, bf16[64,2048]{1,0:T(8,128)(2,1)S(1)}, u32[]{:S(2)}, u32[]{:S(2)}) %collective-permute-start.6) | collective-permute-done | bytes 262176 | tf_op jit(solution)/shard_map/ppermute | solution.py:19
  38.7 3.2 %collective-permute-start.12 = (bf16[64,2048]{1,0:T(8,128)(2,1)S(1)}, bf16[64,2048]{1,0:T(8,128)(2,1)}, u32[]{:S(2)}, u32[]{:S(2)}) collective-permute-start(bf16[64,2048]{1,0:T(8,128)(2,1)S(1)} %collective-permute-done.5.refs_7_), channel_id=1, source_target_pairs={{0,112},{16,0},{32,16},{48,32},{64,48},{80,64},{96,80},{112,96},{1... | collective-permute-start | bytes 786440 | tf_op jit(solution)/shard_map/ppermute | solution.py:19
  41.9 0.1 pad_add_fusion.1.at_ref
  42.0 0.6 constant_dynamic-slice_fusion.temp_ref
  42.6 1.1 dynamic-slice_bitcast_fusion.refs_10_.refs_6_
  43.7 1.8 %collective-permute-done.7.refs_9_ = bf16[64,2048]{1,0:T(8,128)(2,1)S(1)} collective-permute-done((bf16[64,2048]{1,0:T(8,128)(2,1)S(1)}, bf16[64,2048]{1,0:T(8,128)(2,1)S(1)}, u32[]{:S(2)}, u32[]{:S(2)}) %collective-permute-start.7) | collective-permute-done | bytes 262176 | tf_op jit(solution)/shard_map/ppermute | solution.py:19
  45.5 2.0 %collective-permute-start.14 = (bf16[64,2048]{1,0:T(8,128)(2,1)S(1)}, bf16[64,2048]{1,0:T(8,128)(2,1)S(1)}, u32[]{:S(2)}, u32[]{:S(2)}) collective-permute-start(bf16[64,2048]{1,0:T(8,128)(2,1)S(1)} %collective-permute-done.7.refs_9_), channel_id=1, source_target_pairs={{0,16},{16,32},{32,48},{48,64},{64,80},{80,96},{96,112},{112,0},{1... | collective-permute-start | bytes 786440 | tf_op jit(solution)/shard_map/ppermute | solution.py:19
  47.5 0.9 collective-permute-done.13.refs_2_
  48.4 3.8 %collective-permute-start.16 = (bf16[64,2048]{1,0:T(8,128)(2,1)}, bf16[64,2048]{1,0:T(8,128)(2,1)S(1)}, u32[]{:S(2)}, u32[]{:S(2)}) collective-permute-start(bf16[64,2048]{1,0:T(8,128)(2,1)} %collective-permute-done.12.refs_1_), channel_id=1, source_target_pairs={{0,112},{16,0},{32,16},{48,32},{64,48},{80,64},{96,80},{112,96},{1... | collective-permute-start | bytes 786440 | tf_op jit(solution)/shard_map/ppermute | solution.py:19
  52.2 1.0 shard_map.105.refs_11_.refs_7_
  53.2 2.3 %shard_map.106 = (bf16[640,128]{1,0:T(8,128)(2,1)S(1)}, bf16[640,256]{1,0:T(8,128)(2,1)S(1)}) custom-call(f32[1,1]{1,0:T(1,128)} %constant_dynamic-slice_fusion.temp_ref, bf16[64,2048]{1,0:T(8,128)(2,1)S(1)} %get-tuple-element.15.refs_0_, bf16[64,2048]{1,0:T(8,128)(2,1)S(1)} %get-tuple-element.16.refs_1_, bf16[64,2048]{1,0:T(8,128)(2,1)S(1)} %collective-permute-done.refs_2_, ...), custom_call_target="tpu_custom_call" | custom-call | flops 1006632960 | bytes 5177344 | tf_op jit(solution)/shard_map/pallas_call | solution.py:99
  55.5 0.7 copy-done.6
  56.2 1.8 %collective-permute-start.17 = (bf16[640,256]{1,0:T(8,128)(2,1)S(1)}, bf16[640,256]{1,0:T(8,128)(2,1)S(1)}, u32[]{:S(2)}, u32[]{:S(2)}) collective-permute-start(bf16[640,256]{1,0:T(8,128)(2,1)S(1)} %get-tuple-element.20.own_a), channel_id=1, source_target_pairs={{0,128},{128,0},{1,129},{129,1},{2,130},{130,2},{3,131},{131,3},{4... | collective-permute-start | bytes 983048 | tf_op jit(solution)/shard_map/ppermute | solution.py:19
  58.0 0.1 select_reduce_fusion
  58.1 0.1 collective-permute-start.18
  58.2 1.2 %collective-permute-done.15.refs_4_ = bf16[64,2048]{1,0:T(8,128)(2,1)S(1)} collective-permute-done((bf16[64,2048]{1,0:T(8,128)(2,1)}, bf16[64,2048]{1,0:T(8,128)(2,1)S(1)}, u32[]{:S(2)}, u32[]{:S(2)}) %collective-permute-start.15) | collective-permute-done | bytes 262176 | tf_op jit(solution)/shard_map/ppermute | solution.py:19
  59.5 2.8 %shard_map.107 = (bf16[384,128]{1,0:T(8,128)(2,1)S(1)}, bf16[384,256]{1,0:T(8,128)(2,1)S(1)}) custom-call(f32[1,1]{1,0:T(1,128)} %constant_dynamic-slice_fusion.temp_ref, bf16[64,2048]{1,0:T(8,128)(2,1)S(1)} %collective-permute-done.11.refs_0_, bf16[64,2048]{1,0:T(8,128)(2,1)} %collective-permute-done.12.refs_1_, ...), custom_call_target="tpu_custom_call" | custom-call | flops 603979776 | bytes 3735552 | tf_op jit(solution)/shard_map/pallas_call | solution.py:99
  62.3 2.5 %collective-permute-done.17.ya = bf16[640,256]{1,0:T(8,128)(2,1)S(1)} collective-permute-done((bf16[640,256]{1,0:T(8,128)(2,1)S(1)}, bf16[640,256]{1,0:T(8,128)(2,1)S(1)}, u32[]{:S(2)}, u32[]{:S(2)}) %collective-permute-start.17) | collective-permute-done | bytes 327712 | tf_op jit(solution)/shard_map/ppermute | solution.py:19
  64.8 0.2 copy.23
  65.0 0.2 copy.20
  65.2 0.1 subtract_add_fusion
  65.3 0.6 collective-permute-start.20
  65.9 2.1 %collective-permute-start.21 = (bf16[384,256]{1,0:T(8,128)(2,1)S(1)}, bf16[384,256]{1,0:T(8,128)(2,1)S(1)}, u32[]{:S(2)}, u32[]{:S(2)}) collective-permute-start(bf16[384,256]{1,0:T(8,128)(2,1)S(1)} %get-tuple-element.22.own_b), channel_id=1, source_target_pairs={{0,128},{8,136},{128,0},{136,8},{1,129},{9,137},{129,1},{137,9},{2... | collective-permute-start | bytes 589832 | tf_op jit(solution)/shard_map/ppermute | solution.py:315
  68.0 0.9 collective-permute-start.22
  68.9 7.1 %shard_map.108 = (bf16[1024,128]{1,0:T(8,128)(2,1)S(1)}, f32[1024,128]{1,0:T(8,128)S(1)}, f32[1024,128]{1,0:T(8,128)S(1)}, f32[1024,128]{1,0:T(8,128)S(1)}) custom-call(s32[2,8]{1,0:T(2,128)S(1)} %pad_add_fusion.at_ref, bf16[640,128]{1,0:T(8,128)(2,1)S(1)} %copy-done.7, bf16[384,128]{1,0:T(8,128)(2,1)S(1)} %get-tuple-element.19.qb, ...), custom_call_target="tpu_custom_call" | custom-call | flops 15435038720 | bytes 1507328 | tf_op jit(solution)/shard_map/pallas_call | solution.py:219
  76.0 1.7 %collective-permute-done.22.xb = bf16[384,256]{1,0:T(8,128)(2,1)S(1)} collective-permute-done((bf16[384,256]{1,0:T(8,128)(2,1)S(1)}, bf16[384,256]{1,0:T(8,128)(2,1)S(1)}, u32[]{:S(2)}, u32[]{:S(2)}) %collective-permute-start.22) | collective-permute-done | bytes 196640 | tf_op jit(solution)/shard_map/ppermute | solution.py:315
  77.7 4.1 %shard_map.109 = bf16[1024,128]{1,0:T(8,128)(2,1)S(1)} custom-call(s32[2,8]{1,0:T(2,128)S(1)} %pad_add_fusion.at_ref, bf16[1024,128]{1,0:T(8,128)(2,1)S(1)} %get-tuple-element.24.q_ref, f32[1024,128]{1,0:T(8,128)S(1)} %get-tuple-element.25.acc, f32[1024,128]{1,0:T(8,128)S(1)} %get-tuple-element.26.top_ref, f32[1024,128]{1,0:T(8,128)S(1)} %get-tuple-element.27.total_ref, ...), custom_call_target="tpu_custom_call" | custom-call | flops 6039797760 | bytes 589824 | tf_op jit(solution)/shard_map/pallas_call | solution.py:236
  81.8 15.4 %all_to_all.10.m_ref = bf16[8,128,128]{2,1,0:T(8,128)(2,1)S(1)} all-to-all(bf16[8,128,128]{2,1,0:T(8,128)(2,1)S(1)} %bitcast.28), channel_id=1, replica_groups=mesh['yh'=2,'z'=8,'c'=2,'yl'=2,'x'=4] {'z'}, dimensions={0} | all-to-all | bytes 524288 | tf_op jit(solution)/shard_map/all_to_all | solution.py:321
  97.3 1.6 %shard_map.110 = bf16[128,2048]{1,0:T(8,128)(2,1)} custom-call(bf16[8,128,128]{2,1,0:T(8,128)(2,1)S(1)} %all_to_all.10.m_ref, bf16[1024,2048]{1,0:T(8,128)(2,1)S(1)} %bitcast.24, bf16[128,2048]{1,0:T(8,128)(2,1)S(1)} %bitcast.26), custom_call_target="tpu_custom_call" | custom-call | flops 536870912 | bytes 6291456 | tf_op jit(solution)/shard_map/pallas_call | solution.py:259
  98.9 3.4 %collective-permute-start.23 = (bf16[128,2048]{1,0:T(8,128)(2,1)}, bf16[128,2048]{1,0:T(8,128)(2,1)S(1)}, u32[]{:S(2)}, u32[]{:S(2)}) collective-permute-start(bf16[128,2048]{1,0:T(8,128)(2,1)} %shard_map.110), channel_id=1, source_target_pairs={{0,1},{1,2},{2,3},{3,4},{4,5},{5,6},{6,7},{8,9},{9,10},{10,11},{11... | collective-permute-start | bytes 1572872 | tf_op jit(solution)/shard_map/ppermute | solution.py:25
  102.2 14.8 %collective-permute-done.23 = bf16[128,2048]{1,0:T(8,128)(2,1)S(1)} collective-permute-done((bf16[128,2048]{1,0:T(8,128)(2,1)}, bf16[128,2048]{1,0:T(8,128)(2,1)S(1)}, u32[]{:S(2)}, u32[]{:S(2)}) %collective-permute-start.23) | collective-permute-done | bytes 524320 | tf_op jit(solution)/shard_map/ppermute | solution.py:25
  117.1 0.8 copy.30
  (49 shorter events, 0.2 us)
Async XLA Ops:
  0.6 41.4 %copy-start = (f32[1,8]{1,0:T(1,128)S(1)}, f32[1,8]{1,0:T(1,128)}, u32[]{:S(2)}) copy-start(f32[1,8]{1,0:T(1,128)} %param.16) | copy-start | bytes 100
  0.6 1.0 copy-start.2
  1.7 0.9 copy-start.4
  2.6 0.7 copy-start.5
  4.3 53.8 %copy-start.9 = (s32[8]{0:T(128)S(1)}, s32[8]{0:T(128)}, u32[]{:S(2)}) copy-start(s32[8]{0:T(128)} %constant.36.clone) | copy-start | bytes 100
  4.3 14.5 %collective-permute-start = (bf16[64,2048]{1,0:T(8,128)(2,1)S(1)}, bf16[64,2048]{1,0:T(8,128)(2,1)S(1)}, u32[]{:S(2)}, u32[]{:S(2)}) collective-permute-start(bf16[64,2048]{1,0:T(8,128)(2,1)S(1)} %get-tuple-element.15.refs_0_), channel_id=1, source_target_pairs={{0,112},{16,0},{32,16},{48,32},{64,48},{80,64},{96,80},{112,96},{1... | collective-permute-start | bytes 786440 | tf_op jit(solution)/shard_map/ppermute | solution.py:19
  10.1 19.2 %collective-permute-start.2 = (bf16[64,2048]{1,0:T(8,128)(2,1)S(1)}, bf16[64,2048]{1,0:T(8,128)(2,1)S(1)}, u32[]{:S(2)}, u32[]{:S(2)}) collective-permute-start(bf16[64,2048]{1,0:T(8,128)(2,1)S(1)} %get-tuple-element.15.refs_0_), channel_id=1, source_target_pairs={{0,16},{16,32},{32,48},{48,64},{64,80},{80,96},{96,112},{112,0},{1... | collective-permute-start | bytes 786440 | tf_op jit(solution)/shard_map/ppermute | solution.py:19
  10.1 15.3 %collective-permute-start.1 = (bf16[64,2048]{1,0:T(8,128)(2,1)S(1)}, bf16[64,2048]{1,0:T(8,128)(2,1)S(1)}, u32[]{:S(2)}, u32[]{:S(2)}) collective-permute-start(bf16[64,2048]{1,0:T(8,128)(2,1)S(1)} %get-tuple-element.16.refs_1_), channel_id=1, source_target_pairs={{0,112},{16,0},{32,16},{48,32},{64,48},{80,64},{96,80},{112,96},{1... | collective-permute-start | bytes 786440 | tf_op jit(solution)/shard_map/ppermute | solution.py:19
  13.4 21.8 %collective-permute-start.3 = (bf16[64,2048]{1,0:T(8,128)(2,1)S(1)}, bf16[64,2048]{1,0:T(8,128)(2,1)S(1)}, u32[]{:S(2)}, u32[]{:S(2)}) collective-permute-start(bf16[64,2048]{1,0:T(8,128)(2,1)S(1)} %get-tuple-element.16.refs_1_), channel_id=1, source_target_pairs={{0,16},{16,32},{32,48},{48,64},{64,80},{80,96},{96,112},{112,0},{1... | collective-permute-start | bytes 786440 | tf_op jit(solution)/shard_map/ppermute | solution.py:19
  13.4 18.5 %all-to-all-start = ((bf16[8,64,256]{2,1,0:T(8,128)(2,1)}), bf16[8,64,256]{2,1,0:T(8,128)(2,1)S(1)}, u32[]{:S(2)}, u32[]{:S(2)}) async-start(bf16[8,64,256]{2,1,0:T(8,128)(2,1)} %get-tuple-element.17), calls=%async_computation | async-start | bytes 524288 | tf_op jit(solution)/shard_map/all_to_all | solution.py:290
  18.7 16.5 %collective-permute-start.4 = (bf16[64,2048]{1,0:T(8,128)(2,1)S(1)}, bf16[64,2048]{1,0:T(8,128)(2,1)S(1)}, u32[]{:S(2)}, u32[]{:S(2)}) collective-permute-start(bf16[64,2048]{1,0:T(8,128)(2,1)S(1)} %collective-permute-done.refs_2_), channel_id=1, source_target_pairs={{0,112},{16,0},{32,16},{48,32},{64,48},{80,64},{96,80},{112,96},{1... | collective-permute-start | bytes 786440 | tf_op jit(solution)/shard_map/ppermute | solution.py:19
  25.5 13.2 %collective-permute-start.5 = (bf16[64,2048]{1,0:T(8,128)(2,1)S(1)}, bf16[64,2048]{1,0:T(8,128)(2,1)S(1)}, u32[]{:S(2)}, u32[]{:S(2)}) collective-permute-start(bf16[64,2048]{1,0:T(8,128)(2,1)S(1)} %collective-permute-done.1.refs_3_), channel_id=1, source_target_pairs={{0,112},{16,0},{32,16},{48,32},{64,48},{80,64},{96,80},{112,96},{1... | collective-permute-start | bytes 786440 | tf_op jit(solution)/shard_map/ppermute | solution.py:19
  29.3 9.4 %collective-permute-start.6 = (bf16[64,2048]{1,0:T(8,128)(2,1)S(1)}, bf16[64,2048]{1,0:T(8,128)(2,1)S(1)}, u32[]{:S(2)}, u32[]{:S(2)}) collective-permute-start(bf16[64,2048]{1,0:T(8,128)(2,1)S(1)} %collective-permute-done.2.refs_4_), channel_id=1, source_target_pairs={{0,16},{16,32},{32,48},{48,64},{64,80},{80,96},{96,112},{112,0},{1... | collective-permute-start | bytes 786440 | tf_op jit(solution)/shard_map/ppermute | solution.py:19
  31.9 10.0 %collective-permute-start.9 = (bf16[8,64,256]{2,1,0:T(8,128)(2,1)S(1)}, bf16[8,64,256]{2,1,0:T(8,128)(2,1)S(1)}, u32[]{:S(2)}, u32[]{:S(2)}) collective-permute-start(bf16[8,64,256]{2,1,0:T(8,128)(2,1)S(1)} %all-to-all-done.own), channel_id=1, source_target_pairs={{0,128},{128,0},{1,129},{129,1},{2,130},{130,2},{3,131},{131,3},{4... | collective-permute-start | bytes 786440 | tf_op jit(solution)/shard_map/ppermute | solution.py:19
  35.1 10.3 %collective-permute-start.7 = (bf16[64,2048]{1,0:T(8,128)(2,1)S(1)}, bf16[64,2048]{1,0:T(8,128)(2,1)S(1)}, u32[]{:S(2)}, u32[]{:S(2)}) collective-permute-start(bf16[64,2048]{1,0:T(8,128)(2,1)S(1)} %collective-permute-done.3.refs_5_), channel_id=1, source_target_pairs={{0,16},{16,32},{32,48},{48,64},{64,80},{80,96},{96,112},{112,0},{1... | collective-permute-start | bytes 786440 | tf_op jit(solution)/shard_map/ppermute | solution.py:19
  35.2 10.2 %collective-permute-start.8 = (bf16[8,64,256]{2,1,0:T(8,128)(2,1)S(1)}, bf16[8,64,256]{2,1,0:T(8,128)(2,1)S(1)}, u32[]{:S(2)}, u32[]{:S(2)}) collective-permute-start(bf16[8,64,256]{2,1,0:T(8,128)(2,1)S(1)} %all-to-all-done.own), channel_id=1, source_target_pairs={{0,8},{8,0},{1,9},{9,1},{2,10},{10,2},{3,11},{11,3},{4,12},{12,4},... | collective-permute-start | bytes 786440 | tf_op jit(solution)/shard_map/ppermute | solution.py:19
  38.7 9.7 %collective-permute-start.13 = (bf16[64,2048]{1,0:T(8,128)(2,1)S(1)}, bf16[64,2048]{1,0:T(8,128)(2,1)}, u32[]{:S(2)}, u32[]{:S(2)}) collective-permute-start(bf16[64,2048]{1,0:T(8,128)(2,1)S(1)} %collective-permute-done.6.refs_8_), channel_id=1, source_target_pairs={{0,16},{16,32},{32,48},{48,64},{64,80},{80,96},{96,112},{112,0},{1... | collective-permute-start | bytes 786440 | tf_op jit(solution)/shard_map/ppermute | solution.py:19
  38.7 9.7 %collective-permute-start.12 = (bf16[64,2048]{1,0:T(8,128)(2,1)S(1)}, bf16[64,2048]{1,0:T(8,128)(2,1)}, u32[]{:S(2)}, u32[]{:S(2)}) collective-permute-start(bf16[64,2048]{1,0:T(8,128)(2,1)S(1)} %collective-permute-done.5.refs_7_), channel_id=1, source_target_pairs={{0,112},{16,0},{32,16},{48,32},{64,48},{80,64},{96,80},{112,96},{1... | collective-permute-start | bytes 786440 | tf_op jit(solution)/shard_map/ppermute | solution.py:19
  41.9 10.3 %collective-permute-start.10 = (bf16[8,64,256]{2,1,0:T(8,128)(2,1)S(1)}, bf16[8,64,256]{2,1,0:T(8,128)(2,1)}, u32[]{:S(2)}, u32[]{:S(2)}) collective-permute-start(bf16[8,64,256]{2,1,0:T(8,128)(2,1)S(1)} %collective-permute-done.9.over), channel_id=1, source_target_pairs={{0,8},{8,0},{1,9},{9,1},{2,10},{10,2},{3,11},{11,3},{4,12},{12,4},... | collective-permute-start | bytes 786440 | tf_op jit(solution)/shard_map/ppermute | solution.py:19
  45.4 12.7 %collective-permute-start.11 = (bf16[64,2048]{1,0:T(8,128)(2,1)S(1)}, bf16[64,2048]{1,0:T(8,128)(2,1)S(1)}, u32[]{:S(2)}, u32[]{:S(2)}) collective-permute-start(bf16[64,2048]{1,0:T(8,128)(2,1)S(1)} %collective-permute-done.4.refs_6_), channel_id=1, source_target_pairs={{0,112},{16,0},{32,16},{48,32},{64,48},{80,64},{96,80},{112,96},{1... | collective-permute-start | bytes 786440 | tf_op jit(solution)/shard_map/ppermute | solution.py:19
  45.5 12.8 %collective-permute-start.14 = (bf16[64,2048]{1,0:T(8,128)(2,1)S(1)}, bf16[64,2048]{1,0:T(8,128)(2,1)S(1)}, u32[]{:S(2)}, u32[]{:S(2)}) collective-permute-start(bf16[64,2048]{1,0:T(8,128)(2,1)S(1)} %collective-permute-done.7.refs_9_), channel_id=1, source_target_pairs={{0,16},{16,32},{32,48},{48,64},{64,80},{80,96},{96,112},{112,0},{1... | collective-permute-start | bytes 786440 | tf_op jit(solution)/shard_map/ppermute | solution.py:19
  48.4 11.1 %collective-permute-start.15 = (bf16[64,2048]{1,0:T(8,128)(2,1)}, bf16[64,2048]{1,0:T(8,128)(2,1)S(1)}, u32[]{:S(2)}, u32[]{:S(2)}) collective-permute-start(bf16[64,2048]{1,0:T(8,128)(2,1)} %collective-permute-done.13.refs_2_), channel_id=1, source_target_pairs={{0,16},{16,32},{32,48},{48,64},{64,80},{80,96},{96,112},{112,0},{1... | collective-permute-start | bytes 786440 | tf_op jit(solution)/shard_map/ppermute | solution.py:19
  48.4 11.1 %collective-permute-start.16 = (bf16[64,2048]{1,0:T(8,128)(2,1)}, bf16[64,2048]{1,0:T(8,128)(2,1)S(1)}, u32[]{:S(2)}, u32[]{:S(2)}) collective-permute-start(bf16[64,2048]{1,0:T(8,128)(2,1)} %collective-permute-done.12.refs_1_), channel_id=1, source_target_pairs={{0,112},{16,0},{32,16},{48,32},{64,48},{80,64},{96,80},{112,96},{1... | collective-permute-start | bytes 786440 | tf_op jit(solution)/shard_map/ppermute | solution.py:19
  53.2 11.5 %copy-start.8 = (s32[1,8]{1,0:T(1,128)S(1)}, s32[1,8]{1,0:T(1,128)}, u32[]{:S(2)}) copy-start(s32[1,8]{1,0:T(1,128)} %constant.43) | copy-start | bytes 100
  55.5 0.7 copy-start.6
  56.2 12.7 %copy-start.7 = (bf16[640,128]{1,0:T(8,128)(2,1)S(1)}, bf16[640,128]{1,0:T(8,128)(2,1)}, u32[]{:S(2)}) copy-start(bf16[640,128]{1,0:T(8,128)(2,1)} %copy-done.6) | copy-start | bytes 491524
  56.2 8.6 %collective-permute-start.17 = (bf16[640,256]{1,0:T(8,128)(2,1)S(1)}, bf16[640,256]{1,0:T(8,128)(2,1)S(1)}, u32[]{:S(2)}, u32[]{:S(2)}) collective-permute-start(bf16[640,256]{1,0:T(8,128)(2,1)S(1)} %get-tuple-element.20.own_a), channel_id=1, source_target_pairs={{0,128},{128,0},{1,129},{129,1},{2,130},{130,2},{3,131},{131,3},{4... | collective-permute-start | bytes 983048 | tf_op jit(solution)/shard_map/ppermute | solution.py:19
  58.1 10.7 %collective-permute-start.18 = (bf16[640,256]{1,0:T(8,128)(2,1)S(1)}, bf16[640,256]{1,0:T(8,128)(2,1)S(1)}, u32[]{:S(2)}, u32[]{:S(2)}) collective-permute-start(bf16[640,256]{1,0:T(8,128)(2,1)S(1)} %get-tuple-element.20.own_a), channel_id=1, source_target_pairs={{0,8},{8,0},{1,9},{9,1},{2,10},{10,2},{3,11},{11,3},{4,12},{12,4},... | collective-permute-start | bytes 983048 | tf_op jit(solution)/shard_map/ppermute | solution.py:19
  64.8 4.1 %collective-permute-start.19 = (bf16[640,256]{1,0:T(8,128)(2,1)S(1)}, bf16[640,256]{1,0:T(8,128)(2,1)S(1)}, u32[]{:S(2)}, u32[]{:S(2)}) collective-permute-start(bf16[640,256]{1,0:T(8,128)(2,1)S(1)} %collective-permute-done.17.ya), channel_id=1, source_target_pairs={{0,8},{8,0},{1,9},{9,1},{2,10},{10,2},{3,11},{11,3},{4,12},{12,4},... | collective-permute-start | bytes 983048 | tf_op jit(solution)/shard_map/ppermute | solution.py:19
  65.3 10.6 %collective-permute-start.20 = (bf16[384,256]{1,0:T(8,128)(2,1)S(1)}, bf16[384,256]{1,0:T(8,128)(2,1)S(1)}, u32[]{:S(2)}, u32[]{:S(2)}) collective-permute-start(bf16[384,256]{1,0:T(8,128)(2,1)S(1)} %get-tuple-element.22.own_b), channel_id=1, source_target_pairs={{0,8},{8,0},{128,136},{136,128},{1,9},{9,1},{129,137},{137,129},{2... | collective-permute-start | bytes 589832 | tf_op jit(solution)/shard_map/ppermute | solution.py:315
  65.9 10.0 %collective-permute-start.21 = (bf16[384,256]{1,0:T(8,128)(2,1)S(1)}, bf16[384,256]{1,0:T(8,128)(2,1)S(1)}, u32[]{:S(2)}, u32[]{:S(2)}) collective-permute-start(bf16[384,256]{1,0:T(8,128)(2,1)S(1)} %get-tuple-element.22.own_b), channel_id=1, source_target_pairs={{0,128},{8,136},{128,0},{136,8},{1,129},{9,137},{129,1},{137,9},{2... | collective-permute-start | bytes 589832 | tf_op jit(solution)/shard_map/ppermute | solution.py:315
  68.0 9.7 %collective-permute-start.22 = (bf16[384,256]{1,0:T(8,128)(2,1)S(1)}, bf16[384,256]{1,0:T(8,128)(2,1)S(1)}, u32[]{:S(2)}, u32[]{:S(2)}) collective-permute-start(bf16[384,256]{1,0:T(8,128)(2,1)S(1)} %get-tuple-element.22.own_b), channel_id=1, source_target_pairs={{0,136},{8,128},{128,8},{136,0},{1,137},{9,129},{129,9},{137,1},{2... | collective-permute-start | bytes 589832 | tf_op jit(solution)/shard_map/ppermute | solution.py:315
  77.7 19.6 %copy-start.1 = (bf16[1,1024,2048]{2,1,0:T(8,128)(2,1)S(1)}, bf16[1,1024,2048]{2,1,0:T(8,128)(2,1)}, u32[]{:S(2)}) copy-start(bf16[1,1024,2048]{2,1,0:T(8,128)(2,1)} %param.15) | copy-start | bytes 12582916
  77.7 19.6 %copy-start.3 = (bf16[1,128,2048]{2,1,0:T(8,128)(2,1)S(1)}, bf16[1,128,2048]{2,1,0:T(8,128)(2,1)}, u32[]{:S(2)}) copy-start(bf16[1,128,2048]{2,1,0:T(8,128)(2,1)} %param.9) | copy-start | bytes 1572868
  98.9 18.2 %collective-permute-start.23 = (bf16[128,2048]{1,0:T(8,128)(2,1)}, bf16[128,2048]{1,0:T(8,128)(2,1)S(1)}, u32[]{:S(2)}, u32[]{:S(2)}) collective-permute-start(bf16[128,2048]{1,0:T(8,128)(2,1)} %shard_map.110), channel_id=1, source_target_pairs={{0,1},{1,2},{2,3},{3,4},{4,5},{5,6},{6,7},{8,9},{9,10},{10,11},{11... | collective-permute-start | bytes 1572872 | tf_op jit(solution)/shard_map/ppermute | solution.py:25

commit v3 on v2

--- a/solution.py
+++ b/solution.py
@@ -172,78 +172,44 @@
     return top, total, mixed
 
 
-def first_kernel(at_ref, qa, qb, own_a, own_b, ca, ya, xa, qpos_ref, qspan_ref, kpos_ref, q_out, acc, top_out, total_out, s_all):
+def attend_kernel(at_ref, qa, qb, *refs):
+    parts, (qpos_ref, qspan_ref, kpos_ref, o_ref, q_all, s_all) = refs[:8], refs[8:]
     early, late = qa.shape[0], qb.shape[0]
-    q_out[pl.ds(0, early), :] = qa[...]
-    q_out[pl.ds(early, late), :] = qb[...]
-    segments = [(own_a, 0, EARLY), (own_b, 0, LATE)]
-    segments += [(ca, 1, EARLY), (ya, 2, EARLY), (xa, 3, EARLY)]
+    q_all[pl.ds(0, early), :] = qa[...]
+    q_all[pl.ds(early, late), :] = qb[...]
+    segments = [(parts[i], i, EARLY) for i in range(4)] + [(parts[4 + i], i, LATE) for i in range(4)]
 
     def one_tile(t, _):
         rows, qpos, qspan = tile_of(t, at_ref, qpos_ref, qspan_ref)
         peak = jnp.full((TILE, 128), -1e30, jnp.float32)
-        top, total, mixed = weighed(q_out[rows, :], peak, segments, kpos_ref, qpos, qspan, s_all)
-        acc[rows, :] = mixed
-        total_out[rows, :] = total
-        top_out[rows, :] = top
-        return 0
-
-    lax.fori_loop(0, (early + late) // TILE, one_tile, 0)
-
-
-def second_kernel(at_ref, q_ref, acc, top_ref, total_ref, cb, yb, xb, qpos_ref, qspan_ref, kpos_ref, o_ref, s_all):
-    segments = [(cb, 1, LATE), (yb, 2, LATE), (xb, 3, LATE)]
-
-    def one_tile(t, _):
-        rows, qpos, qspan = tile_of(t, at_ref, qpos_ref, qspan_ref)
-        before = top_ref[rows, :]
-        top, total, mixed = weighed(q_ref[rows, :], before, segments, kpos_ref, qpos, qspan, s_all)
-        kept = jnp.exp(before - top)
-        summed = acc[rows, :] * kept + mixed
-        weight = jnp.sum(total_ref[rows, :] * kept + total, axis=-1, keepdims=True)
-        result = (summed / weight).astype(jnp.bfloat16)
+        _, total, mixed = weighed(q_all[rows, :], peak, segments, kpos_ref, qpos, qspan, s_all)
+        result = (mixed / jnp.sum(total, axis=-1, keepdims=True)).astype(jnp.bfloat16)
         for i in range(TILE // 128):
             placed = pl.ds(pl.multiple_of(at_ref[1, t * (TILE // 128) + i] * 128, 128), 128)
             o_ref[placed, :] = result[i * 128 : (i + 1) * 128, :]
         return 0
 
-    lax.fori_loop(0, q_ref.shape[0] // TILE, one_tile, 0)
-
-
-def attended_first(at, queries, own, others, qpos, qspan, kpos):
-    early, late = (q.shape[0] for q in queries)
-    rows, head_dim = early + late, queries[0].shape[1]
-    keys = rows + 3 * early
-    wide = jax.ShapeDtypeStruct((rows, head_dim), jnp.float32)
+    lax.fori_loop(0, (early + late) // TILE, one_tile, 0)
+
+
+def attended(at, queries, keyvals, qpos, qspan, kpos):
+    rows, head_dim = sum(q.shape[0] for q in queries), queries[0].shape[1]
+    keys = sum(k.shape[0] for k in keyvals)
     vmem = pl.BlockSpec(memory_space=pltpu.VMEM)
     return pl.pallas_call(
-        first_kernel,
-        in_specs=[pl.BlockSpec(memory_space=pltpu.SMEM)] + [vmem] * 10,
-        out_specs=[vmem] * 4,
-        out_shape=[jax.ShapeDtypeStruct((rows, head_dim), jnp.bfloat16), wide, wide, wide],
-        scratch_shapes=[pltpu.VMEM((TILE, keys), jnp.float32)],
+        attend_kernel,
+        in_specs=[pl.BlockSpec(memory_space=pltpu.SMEM)] + [vmem] * 13,
+        out_specs=vmem,
+        out_shape=jax.ShapeDtypeStruct((rows, head_dim), jnp.bfloat16),
+        scratch_shapes=[
+            pltpu.VMEM((rows, head_dim), jnp.bfloat16),
+            pltpu.VMEM((TILE, keys), jnp.float32),
+        ],
         compiler_params=params(24),
         cost_estimate=pl.CostEstimate(
             flops=40 * rows * keys * head_dim, bytes_accessed=4 * keys * head_dim, transcendentals=rows * keys
         ),
-    )(at, *queries, *own, *others, qpos, qspan, kpos)
-
-
-def attended_second(at, state, others, qpos, qspan, kpos):
-    rows, head_dim = state[0].shape
-    keys = 3 * others[0].shape[0]
-    vmem = pl.BlockSpec(memory_space=pltpu.VMEM)
-    return pl.pallas_call(
-        second_kernel,
-        in_specs=[pl.BlockSpec(memory_space=pltpu.SMEM)] + [vmem] * 10,
-        out_specs=vmem,
-        out_shape=jax.ShapeDtypeStruct((rows, head_dim), jnp.bfloat16),
-        scratch_shapes=[pltpu.VMEM((TILE, keys), jnp.float32)],
-        compiler_params=params(24),
-        cost_estimate=pl.CostEstimate(
-            flops=40 * rows * keys * head_dim, bytes_accessed=4 * keys * head_dim, transcendentals=rows * keys
-        ),
-    )(at, *state, *others, qpos, qspan, kpos)
+    )(at, *queries, *keyvals, qpos, qspan, kpos)
 
 
 def output_kernel(m_ref, w_ref, x_ref, o_ref):
@@ -310,13 +276,13 @@
     q_early, kv_early = projected(sum([rows_of(o) for o in EARLY], []), wq, wkv, temp)
     q_late, kv_late = projected(sum([rows_of(o) for o in LATE], []), wq, wkv, temp)
     over_early = shifted(kv_early, "yh", 1)
-    kv_late, over_later = lax.optimization_barrier((kv_late, over_early))
-    others_early = [shifted(kv_early, "c", 1), over_early, shifted(over_later, "c", 1)]
-    others_late = [lax.ppermute(kv_late, ("yh", "c"), [(i, i ^ k) for i in range(4)]) for k in (1, 2, 3)]
+    _, over_later = lax.optimization_barrier((kv_late, over_early))
+    over_late = shifted(kv_late, "yh", 1)
+    keyvals = [kv_early, shifted(kv_early, "c", 1), over_early, shifted(over_later, "c", 1)]
+    keyvals += [kv_late, shifted(kv_late, "c", 1), over_late, shifted(over_late, "c", 1)]
     offsets = jnp.array(EARLY + LATE, jnp.int32)
     at = jnp.stack([offsets, lax.rem(z + offsets, ZS)])
-    state = attended_first(at, [q_early, q_late], [kv_early, kv_late], others_early, qpos, qspan, kpos)
-    mixed = attended_second(at, state, others_late, qpos, qspan, kpos)
+    mixed = attended(at, [q_early, q_late], keyvals, qpos, qspan, kpos)
 
     mixed = lax.all_to_all(mixed.reshape(ZS, -1, head_dim), "z", 0, 0, tiled=True)
     produced = outputs(mixed, w_out[0], inputs)

time: 118 us -> 118 us (level); the launches traced: 118 us -> 116 us
  Pallas kernels: 19.7 us -> 17.8 us
    ppermute x20 -> x23, starting transfers between devices: 29.7 us -> 33.6 us  [shifted(): lax.ppermute(block, axis, [(i, (i + distance) % count) for i in range(cou...]
    ppermute x3 -> x0, starting transfers between devices: 3.55 us -> none  [per_device(): lax.ppermute(kv_late, ('yh', 'c'), [(i, i ^ k) for i in range(4)])]
    ppermute x20 -> x23, waiting for transfers between devices: 13.2 us -> 15.6 us  [shifted(): lax.ppermute(block, axis, [(i, (i + distance) % count) for i in range(cou...]
    pallas_call x2 -> x1, Pallas kernels: 11.2 us -> 9.29 us  [attended(): pl.pallas_call(attend_kernel, in_specs=[pl.BlockSpec(memory_space=pltpu.S...]
    ppermute x3 -> x0, waiting for transfers between devices: 1.73 us -> none  [per_device(): lax.ppermute(kv_late, ('yh', 'c'), [(i, i ^ k) for i in range(4)])]
  transfers between devices with their start and end apart: 25 -> 25, of which waited for: 9 -> 9; matrix products, arithmetic and copies ran while one was open for 3% -> 3% of each run, Pallas kernels for 11% -> 5%
where the time goes in v3:
time: 118 us; the launch traced here: 116 us
  starting transfers between devices  41.5 us (35%)
  waiting for transfers between devices  32.9 us (28%)
  Pallas kernels  17.8 us (15%)
  blocking collectives  14.9 us (13%)
  local copies, waits for them, and re-layouts  6.34 us (5%)
  other arithmetic  1.88 us (2%)
    ppermute x23, starting transfers between devices, shifted(): lax.ppermute(block, axis, [(i, (i + distance) % count) for i in range(cou...  33.6 us
    ppermute x23, waiting for transfers between devices, shifted(): lax.ppermute(block, axis, [(i, (i + distance) % count) for i in range(cou...  15.6 us
    all_to_all x1, blocking collectives, per_device(): lax.all_to_all(mixed.reshape(ZS, -1, head_dim), 'z', 0, 0, tiled=True)  14.9 us
    ppermute x1, waiting for transfers between devices, passed_along(): return lax.ppermute(block, axis, route)  14.7 us
    pallas_call x1, Pallas kernels, attended(): pl.pallas_call(attend_kernel, in_specs=[pl.BlockSpec(memory_space=pltpu.S...  9.29 us
    pallas_call x2, Pallas kernels, projected(): pl.pallas_call(functools.partial(project_kernel, len(blocks)), in_specs=[...  5.02 us
    all_to_all x1, starting transfers between devices, per_device(): own_w = lax.all_to_all(by_head, 'z', 0, 0, tiled=True)  4.51 us
    unnamed x22, local copies, waits for them, and re-layouts  4.18 us
  transfers between devices with their start and end apart: 25, of which 9 were waited for; matrix products, arithmetic and copies ran while one was open for 3% of the time, Pallas kernels for 5%

profile of v3, /device:TPU:8, one launch (start us, length us, event | category | flops | bytes accessed | tf_op | source)
XLA Modules:
  0.0 116.2 jit_solution(12370733757678302099)
XLA Ops:
  0.7 1.0 copy-done.2
  1.7 0.9 copy-done.4
  2.6 0.7 copy-done.5
  3.3 0.9 shard_map.104
  4.3 5.9 %collective-permute-start = (bf16[64,2048]{1,0:T(8,128)(2,1)S(1)}, bf16[64,2048]{1,0:T(8,128)(2,1)S(1)}, u32[]{:S(2)}, u32[]{:S(2)}) collective-permute-start(bf16[64,2048]{1,0:T(8,128)(2,1)S(1)} %get-tuple-element.10.refs_0_), channel_id=1, source_target_pairs={{0,112},{16,0},{32,16},{48,32},{64,48},{80,64},{96,80},{112,96},{1... | collective-permute-start | bytes 786440 | tf_op jit(solution)/shard_map/ppermute | solution.py:19
  10.1 3.2 %collective-permute-start.1 = (bf16[64,2048]{1,0:T(8,128)(2,1)S(1)}, bf16[64,2048]{1,0:T(8,128)(2,1)S(1)}, u32[]{:S(2)}, u32[]{:S(2)}) collective-permute-start(bf16[64,2048]{1,0:T(8,128)(2,1)S(1)} %get-tuple-element.11.refs_1_), channel_id=1, source_target_pairs={{0,112},{16,0},{32,16},{48,32},{64,48},{80,64},{96,80},{112,96},{1... | collective-permute-start | bytes 786440 | tf_op jit(solution)/shard_map/ppermute | solution.py:19
  13.4 4.5 %all-to-all-start = ((bf16[8,64,256]{2,1,0:T(8,128)(2,1)}), bf16[8,64,256]{2,1,0:T(8,128)(2,1)S(1)}, u32[]{:S(2)}, u32[]{:S(2)}) async-start(bf16[8,64,256]{2,1,0:T(8,128)(2,1)} %get-tuple-element.12), calls=%async_computation | async-start | bytes 524288 | tf_op jit(solution)/shard_map/all_to_all | solution.py:256
  17.9 0.7 fusion
  18.7 3.3 %collective-permute-start.4 = (bf16[64,2048]{1,0:T(8,128)(2,1)S(1)}, bf16[64,2048]{1,0:T(8,128)(2,1)S(1)}, u32[]{:S(2)}, u32[]{:S(2)}) collective-permute-start(bf16[64,2048]{1,0:T(8,128)(2,1)S(1)} %collective-permute-done.refs_2_), channel_id=1, source_target_pairs={{0,112},{16,0},{32,16},{48,32},{64,48},{80,64},{96,80},{112,96},{1... | collective-permute-start | bytes 786440 | tf_op jit(solution)/shard_map/ppermute | solution.py:19
  22.0 3.4 %collective-permute-done.1.refs_3_ = bf16[64,2048]{1,0:T(8,128)(2,1)S(1)} collective-permute-done((bf16[64,2048]{1,0:T(8,128)(2,1)S(1)}, bf16[64,2048]{1,0:T(8,128)(2,1)S(1)}, u32[]{:S(2)}, u32[]{:S(2)}) %collective-permute-start.1) | collective-permute-done | bytes 262176 | tf_op jit(solution)/shard_map/ppermute | solution.py:19
  25.5 3.8 %collective-permute-start.5 = (bf16[64,2048]{1,0:T(8,128)(2,1)S(1)}, bf16[64,2048]{1,0:T(8,128)(2,1)S(1)}, u32[]{:S(2)}, u32[]{:S(2)}) collective-permute-start(bf16[64,2048]{1,0:T(8,128)(2,1)S(1)} %collective-permute-done.1.refs_3_), channel_id=1, source_target_pairs={{0,112},{16,0},{32,16},{48,32},{64,48},{80,64},{96,80},{112,96},{1... | collective-permute-start | bytes 786440 | tf_op jit(solution)/shard_map/ppermute | solution.py:19
  29.3 2.6 %all-to-all-done.own = bf16[8,64,256]{2,1,0:T(8,128)(2,1)S(1)} async-done(((bf16[8,64,256]{2,1,0:T(8,128)(2,1)}), bf16[8,64,256]{2,1,0:T(8,128)(2,1)S(1)}, u32[]{:S(2)}, u32[]{:S(2)}) %all-to-all-start) | async-done | bytes 262176 | tf_op jit(solution)/shard_map/all_to_all | solution.py:256
  31.9 2.3 %collective-permute-start.9 = (bf16[8,64,256]{2,1,0:T(8,128)(2,1)S(1)}, bf16[8,64,256]{2,1,0:T(8,128)(2,1)S(1)}, u32[]{:S(2)}, u32[]{:S(2)}) collective-permute-start(bf16[8,64,256]{2,1,0:T(8,128)(2,1)S(1)} %all-to-all-done.own), channel_id=1, source_target_pairs={{0,128},{128,0},{1,129},{129,1},{2,130},{130,2},{3,131},{131,3},{4... | collective-permute-start | bytes 786440 | tf_op jit(solution)/shard_map/ppermute | solution.py:19
  34.2 0.7 fusion.2
  34.9 0.1 collective-permute-start.7
  35.0 0.1 collective-permute-start.8
  35.1 3.9 %collective-permute-done.6.refs_8_ = bf16[64,2048]{1,0:T(8,128)(2,1)S(1)} collective-permute-done((bf16[64,2048]{1,0:T(8,128)(2,1)S(1)}, bf16[64,2048]{1,0:T(8,128)(2,1)S(1)}, u32[]{:S(2)}, u32[]{:S(2)}) %collective-permute-start.6) | collective-permute-done | bytes 262176 | tf_op jit(solution)/shard_map/ppermute | solution.py:19
  39.0 3.2 %collective-permute-start.12 = (bf16[64,2048]{1,0:T(8,128)(2,1)S(1)}, bf16[64,2048]{1,0:T(8,128)(2,1)}, u32[]{:S(2)}, u32[]{:S(2)}) collective-permute-start(bf16[64,2048]{1,0:T(8,128)(2,1)S(1)} %collective-permute-done.5.refs_7_), channel_id=1, source_target_pairs={{0,112},{16,0},{32,16},{48,32},{64,48},{80,64},{96,80},{112,96},{1... | collective-permute-start | bytes 786440 | tf_op jit(solution)/shard_map/ppermute | solution.py:19
  42.2 0.1 pad_add_fusion.1.at_ref
  42.3 0.6 constant_dynamic-slice_fusion.temp_ref
  42.9 1.1 dynamic-slice_bitcast_fusion.refs_10_.refs_6_
  44.0 1.3 %collective-permute-done.7.refs_9_ = bf16[64,2048]{1,0:T(8,128)(2,1)S(1)} collective-permute-done((bf16[64,2048]{1,0:T(8,128)(2,1)S(1)}, bf16[64,2048]{1,0:T(8,128)(2,1)S(1)}, u32[]{:S(2)}, u32[]{:S(2)}) %collective-permute-start.7) | collective-permute-done | bytes 262176 | tf_op jit(solution)/shard_map/ppermute | solution.py:19
  45.3 2.0 %collective-permute-start.14 = (bf16[64,2048]{1,0:T(8,128)(2,1)S(1)}, bf16[64,2048]{1,0:T(8,128)(2,1)S(1)}, u32[]{:S(2)}, u32[]{:S(2)}) collective-permute-start(bf16[64,2048]{1,0:T(8,128)(2,1)S(1)} %collective-permute-done.7.refs_9_), channel_id=1, source_target_pairs={{0,16},{16,32},{32,48},{48,64},{64,80},{80,96},{96,112},{112,0},{1... | collective-permute-start | bytes 786440 | tf_op jit(solution)/shard_map/ppermute | solution.py:19
  47.3 0.9 collective-permute-done.13.refs_2_
  48.2 3.6 %collective-permute-start.16 = (bf16[64,2048]{1,0:T(8,128)(2,1)}, bf16[64,2048]{1,0:T(8,128)(2,1)S(1)}, u32[]{:S(2)}, u32[]{:S(2)}) collective-permute-start(bf16[64,2048]{1,0:T(8,128)(2,1)} %collective-permute-done.12.refs_1_), channel_id=1, source_target_pairs={{0,112},{16,0},{32,16},{48,32},{64,48},{80,64},{96,80},{112,96},{1... | collective-permute-start | bytes 786440 | tf_op jit(solution)/shard_map/ppermute | solution.py:19
  51.9 1.0 shard_map.105.refs_11_.refs_7_
  52.9 2.3 %shard_map.106 = (bf16[640,128]{1,0:T(8,128)(2,1)S(1)}, bf16[640,256]{1,0:T(8,128)(2,1)S(1)}) custom-call(f32[1,1]{1,0:T(1,128)} %constant_dynamic-slice_fusion.temp_ref, bf16[64,2048]{1,0:T(8,128)(2,1)S(1)} %get-tuple-element.10.refs_0_, bf16[64,2048]{1,0:T(8,128)(2,1)S(1)} %get-tuple-element.11.refs_1_, bf16[64,2048]{1,0:T(8,128)(2,1)S(1)} %collective-permute-done.refs_2_, ...), custom_call_target="tpu_custom_call" | custom-call | flops 1006632960 | bytes 5177344 | tf_op jit(solution)/shard_map/pallas_call | solution.py:99
  55.2 0.7 copy-done.6
  55.9 2.2 %collective-permute-start.18 = (bf16[640,256]{1,0:T(8,128)(2,1)S(1)}, bf16[640,256]{1,0:T(8,128)(2,1)S(1)}, u32[]{:S(2)}, u32[]{:S(2)}) collective-permute-start(bf16[640,256]{1,0:T(8,128)(2,1)S(1)} %get-tuple-element.15.refs_0_), channel_id=1, source_target_pairs={{0,128},{128,0},{1,129},{129,1},{2,130},{130,2},{3,131},{131,3},{4... | collective-permute-start | bytes 983048 | tf_op jit(solution)/shard_map/ppermute | solution.py:19
  58.0 0.2 convert_reduce_fusion
  58.3 1.4 %collective-permute-done.15.refs_4_ = bf16[64,2048]{1,0:T(8,128)(2,1)S(1)} collective-permute-done((bf16[64,2048]{1,0:T(8,128)(2,1)}, bf16[64,2048]{1,0:T(8,128)(2,1)S(1)}, u32[]{:S(2)}, u32[]{:S(2)}) %collective-permute-start.15) | collective-permute-done | bytes 262176 | tf_op jit(solution)/shard_map/ppermute | solution.py:19
  59.7 2.8 %shard_map.107 = (bf16[384,128]{1,0:T(8,128)(2,1)S(1)}, bf16[384,256]{1,0:T(8,128)(2,1)S(1)}) custom-call(f32[1,1]{1,0:T(1,128)} %constant_dynamic-slice_fusion.temp_ref, bf16[64,2048]{1,0:T(8,128)(2,1)S(1)} %collective-permute-done.11.refs_0_, bf16[64,2048]{1,0:T(8,128)(2,1)} %collective-permute-done.12.refs_1_, ...), custom_call_target="tpu_custom_call" | custom-call | flops 603979776 | bytes 3735552 | tf_op jit(solution)/shard_map/pallas_call | solution.py:99
  62.5 3.1 %collective-permute-start.21 = (bf16[384,256]{1,0:T(8,128)(2,1)S(1)}, bf16[384,256]{1,0:T(8,128)(2,1)S(1)}, u32[]{:S(2)}, u32[]{:S(2)}) collective-permute-start(bf16[384,256]{1,0:T(8,128)(2,1)S(1)} %get-tuple-element.16.refs_4_), channel_id=1, source_target_pairs={{0,128},{128,0},{1,129},{129,1},{2,130},{130,2},{3,131},{131,3},{4... | collective-permute-start | bytes 589832 | tf_op jit(solution)/shard_map/ppermute | solution.py:19
  65.6 0.1 select_reduce_fusion
  65.7 0.1 collective-permute-start.17
  65.8 0.5 collective-permute-start.19
  66.3 0.2 copy.23
  66.5 0.2 copy.20
  66.7 0.2 collective-permute-start.20
  66.9 3.3 %collective-permute-done.21.refs_6_ = bf16[384,256]{1,0:T(8,128)(2,1)S(1)} collective-permute-done((bf16[384,256]{1,0:T(8,128)(2,1)S(1)}, bf16[384,256]{1,0:T(8,128)(2,1)S(1)}, u32[]{:S(2)}, u32[]{:S(2)}) %collective-permute-start.21) | collective-permute-done | bytes 196640 | tf_op jit(solution)/shard_map/ppermute | solution.py:19
  70.2 0.1 subtract_add_fusion
  70.3 1.3 %collective-permute-done.22.refs_7_ = bf16[384,256]{1,0:T(8,128)(2,1)S(1)} collective-permute-done((bf16[384,256]{1,0:T(8,128)(2,1)S(1)}, bf16[384,256]{1,0:T(8,128)(2,1)S(1)}, u32[]{:S(2)}, u32[]{:S(2)}) %collective-permute-start.22) | collective-permute-done | bytes 196640 | tf_op jit(solution)/shard_map/ppermute | solution.py:19
  71.7 9.3 %shard_map.108 = bf16[1024,128]{1,0:T(8,128)(2,1)S(1)} custom-call(s32[2,8]{1,0:T(2,128)S(1)} %pad_add_fusion.at_ref, bf16[640,128]{1,0:T(8,128)(2,1)S(1)} %copy-done.7, bf16[384,128]{1,0:T(8,128)(2,1)S(1)} %get-tuple-element.14.qb, bf16[640,256]{1,0:T(8,128)(2,1)S(1)} %get-tuple-element.15.refs_0_, bf16[640,256]{1,0:T(8,128)(2,1)S(1)} %collective-permute-done.17.refs_1_, ...), custom_call_target="tpu_custom_call" | custom-call | flops 21474836480 | bytes 2097152 | tf_op jit(solution)/shard_map/pallas_call | solution.py:199
  81.0 14.9 %all_to_all.10.m_ref = bf16[8,128,128]{2,1,0:T(8,128)(2,1)S(1)} all-to-all(bf16[8,128,128]{2,1,0:T(8,128)(2,1)S(1)} %bitcast.28), channel_id=1, replica_groups=mesh['yh'=2,'z'=8,'c'=2,'yl'=2,'x'=4] {'z'}, dimensions={0} | all-to-all | bytes 524288 | tf_op jit(solution)/shard_map/all_to_all | solution.py:287
  95.8 1.6 %shard_map.109 = bf16[128,2048]{1,0:T(8,128)(2,1)} custom-call(bf16[8,128,128]{2,1,0:T(8,128)(2,1)S(1)} %all_to_all.10.m_ref, bf16[1024,2048]{1,0:T(8,128)(2,1)S(1)} %bitcast.24, bf16[128,2048]{1,0:T(8,128)(2,1)S(1)} %bitcast.26), custom_call_target="tpu_custom_call" | custom-call | flops 536870912 | bytes 6291456 | tf_op jit(solution)/shard_map/pallas_call | solution.py:225
  97.4 3.4 %collective-permute-start.23 = (bf16[128,2048]{1,0:T(8,128)(2,1)}, bf16[128,2048]{1,0:T(8,128)(2,1)S(1)}, u32[]{:S(2)}, u32[]{:S(2)}) collective-permute-start(bf16[128,2048]{1,0:T(8,128)(2,1)} %shard_map.109), channel_id=1, source_target_pairs={{0,1},{1,2},{2,3},{3,4},{4,5},{5,6},{6,7},{8,9},{9,10},{10,11},{11... | collective-permute-start | bytes 1572872 | tf_op jit(solution)/shard_map/ppermute | solution.py:25
  100.8 14.7 %collective-permute-done.23 = bf16[128,2048]{1,0:T(8,128)(2,1)S(1)} collective-permute-done((bf16[128,2048]{1,0:T(8,128)(2,1)}, bf16[128,2048]{1,0:T(8,128)(2,1)S(1)}, u32[]{:S(2)}, u32[]{:S(2)}) %collective-permute-start.23) | collective-permute-done | bytes 524320 | tf_op jit(solution)/shard_map/ppermute | solution.py:25
  115.4 0.8 copy.30
  (48 shorter events, 0.2 us)
Async XLA Ops:
  0.6 41.7 %copy-start = (f32[1,8]{1,0:T(1,128)S(1)}, f32[1,8]{1,0:T(1,128)}, u32[]{:S(2)}) copy-start(f32[1,8]{1,0:T(1,128)} %param.16) | copy-start | bytes 100
  0.6 1.0 copy-start.2
  1.7 0.9 copy-start.4
  2.6 0.7 copy-start.5
  4.3 53.8 %copy-start.8 = (s32[4096]{0:T(1024)S(1)}, s32[4096]{0:T(1024)}, u32[]{:S(2)}) copy-start(s32[4096]{0:T(1024)} %param.11) | copy-start | bytes 49156
  4.3 14.5 %collective-permute-start = (bf16[64,2048]{1,0:T(8,128)(2,1)S(1)}, bf16[64,2048]{1,0:T(8,128)(2,1)S(1)}, u32[]{:S(2)}, u32[]{:S(2)}) collective-permute-start(bf16[64,2048]{1,0:T(8,128)(2,1)S(1)} %get-tuple-element.10.refs_0_), channel_id=1, source_target_pairs={{0,112},{16,0},{32,16},{48,32},{64,48},{80,64},{96,80},{112,96},{1... | collective-permute-start | bytes 786440 | tf_op jit(solution)/shard_map/ppermute | solution.py:19
  10.1 19.2 %collective-permute-start.2 = (bf16[64,2048]{1,0:T(8,128)(2,1)S(1)}, bf16[64,2048]{1,0:T(8,128)(2,1)S(1)}, u32[]{:S(2)}, u32[]{:S(2)}) collective-permute-start(bf16[64,2048]{1,0:T(8,128)(2,1)S(1)} %get-tuple-element.10.refs_0_), channel_id=1, source_target_pairs={{0,16},{16,32},{32,48},{48,64},{64,80},{80,96},{96,112},{112,0},{1... | collective-permute-start | bytes 786440 | tf_op jit(solution)/shard_map/ppermute | solution.py:19
  10.1 15.3 %collective-permute-start.1 = (bf16[64,2048]{1,0:T(8,128)(2,1)S(1)}, bf16[64,2048]{1,0:T(8,128)(2,1)S(1)}, u32[]{:S(2)}, u32[]{:S(2)}) collective-permute-start(bf16[64,2048]{1,0:T(8,128)(2,1)S(1)} %get-tuple-element.11.refs_1_), channel_id=1, source_target_pairs={{0,112},{16,0},{32,16},{48,32},{64,48},{80,64},{96,80},{112,96},{1... | collective-permute-start | bytes 786440 | tf_op jit(solution)/shard_map/ppermute | solution.py:19
  13.4 21.5 %collective-permute-start.3 = (bf16[64,2048]{1,0:T(8,128)(2,1)S(1)}, bf16[64,2048]{1,0:T(8,128)(2,1)S(1)}, u32[]{:S(2)}, u32[]{:S(2)}) collective-permute-start(bf16[64,2048]{1,0:T(8,128)(2,1)S(1)} %get-tuple-element.11.refs_1_), channel_id=1, source_target_pairs={{0,16},{16,32},{32,48},{48,64},{64,80},{80,96},{96,112},{112,0},{1... | collective-permute-start | bytes 786440 | tf_op jit(solution)/shard_map/ppermute | solution.py:19
  13.4 18.5 %all-to-all-start = ((bf16[8,64,256]{2,1,0:T(8,128)(2,1)}), bf16[8,64,256]{2,1,0:T(8,128)(2,1)S(1)}, u32[]{:S(2)}, u32[]{:S(2)}) async-start(bf16[8,64,256]{2,1,0:T(8,128)(2,1)} %get-tuple-element.12), calls=%async_computation | async-start | bytes 524288 | tf_op jit(solution)/shard_map/all_to_all | solution.py:256
  18.7 16.2 %collective-permute-start.4 = (bf16[64,2048]{1,0:T(8,128)(2,1)S(1)}, bf16[64,2048]{1,0:T(8,128)(2,1)S(1)}, u32[]{:S(2)}, u32[]{:S(2)}) collective-permute-start(bf16[64,2048]{1,0:T(8,128)(2,1)S(1)} %collective-permute-done.refs_2_), channel_id=1, source_target_pairs={{0,112},{16,0},{32,16},{48,32},{64,48},{80,64},{96,80},{112,96},{1... | collective-permute-start | bytes 786440 | tf_op jit(solution)/shard_map/ppermute | solution.py:19
  25.5 13.5 %collective-permute-start.5 = (bf16[64,2048]{1,0:T(8,128)(2,1)S(1)}, bf16[64,2048]{1,0:T(8,128)(2,1)S(1)}, u32[]{:S(2)}, u32[]{:S(2)}) collective-permute-start(bf16[64,2048]{1,0:T(8,128)(2,1)S(1)} %collective-permute-done.1.refs_3_), channel_id=1, source_target_pairs={{0,112},{16,0},{32,16},{48,32},{64,48},{80,64},{96,80},{112,96},{1... | collective-permute-start | bytes 786440 | tf_op jit(solution)/shard_map/ppermute | solution.py:19
  29.3 9.7 %collective-permute-start.6 = (bf16[64,2048]{1,0:T(8,128)(2,1)S(1)}, bf16[64,2048]{1,0:T(8,128)(2,1)S(1)}, u32[]{:S(2)}, u32[]{:S(2)}) collective-permute-start(bf16[64,2048]{1,0:T(8,128)(2,1)S(1)} %collective-permute-done.2.refs_4_), channel_id=1, source_target_pairs={{0,16},{16,32},{32,48},{48,64},{64,80},{80,96},{96,112},{112,0},{1... | collective-permute-start | bytes 786440 | tf_op jit(solution)/shard_map/ppermute | solution.py:19
  31.9 10.3 %collective-permute-start.9 = (bf16[8,64,256]{2,1,0:T(8,128)(2,1)S(1)}, bf16[8,64,256]{2,1,0:T(8,128)(2,1)S(1)}, u32[]{:S(2)}, u32[]{:S(2)}) collective-permute-start(bf16[8,64,256]{2,1,0:T(8,128)(2,1)S(1)} %all-to-all-done.own), channel_id=1, source_target_pairs={{0,128},{128,0},{1,129},{129,1},{2,130},{130,2},{3,131},{131,3},{4... | collective-permute-start | bytes 786440 | tf_op jit(solution)/shard_map/ppermute | solution.py:19
  34.9 10.4 %collective-permute-start.7 = (bf16[64,2048]{1,0:T(8,128)(2,1)S(1)}, bf16[64,2048]{1,0:T(8,128)(2,1)S(1)}, u32[]{:S(2)}, u32[]{:S(2)}) collective-permute-start(bf16[64,2048]{1,0:T(8,128)(2,1)S(1)} %collective-permute-done.3.refs_5_), channel_id=1, source_target_pairs={{0,16},{16,32},{32,48},{48,64},{64,80},{80,96},{96,112},{112,0},{1... | collective-permute-start | bytes 786440 | tf_op jit(solution)/shard_map/ppermute | solution.py:19
  35.0 10.3 %collective-permute-start.8 = (bf16[8,64,256]{2,1,0:T(8,128)(2,1)S(1)}, bf16[8,64,256]{2,1,0:T(8,128)(2,1)S(1)}, u32[]{:S(2)}, u32[]{:S(2)}) collective-permute-start(bf16[8,64,256]{2,1,0:T(8,128)(2,1)S(1)} %all-to-all-done.own), channel_id=1, source_target_pairs={{0,8},{8,0},{1,9},{9,1},{2,10},{10,2},{3,11},{11,3},{4,12},{12,4},... | collective-permute-start | bytes 786440 | tf_op jit(solution)/shard_map/ppermute | solution.py:19
  39.0 9.2 %collective-permute-start.13 = (bf16[64,2048]{1,0:T(8,128)(2,1)S(1)}, bf16[64,2048]{1,0:T(8,128)(2,1)}, u32[]{:S(2)}, u32[]{:S(2)}) collective-permute-start(bf16[64,2048]{1,0:T(8,128)(2,1)S(1)} %collective-permute-done.6.refs_8_), channel_id=1, source_target_pairs={{0,16},{16,32},{32,48},{48,64},{64,80},{80,96},{96,112},{112,0},{1... | collective-permute-start | bytes 786440 | tf_op jit(solution)/shard_map/ppermute | solution.py:19
  39.0 9.3 %collective-permute-start.12 = (bf16[64,2048]{1,0:T(8,128)(2,1)S(1)}, bf16[64,2048]{1,0:T(8,128)(2,1)}, u32[]{:S(2)}, u32[]{:S(2)}) collective-permute-start(bf16[64,2048]{1,0:T(8,128)(2,1)S(1)} %collective-permute-done.5.refs_7_), channel_id=1, source_target_pairs={{0,112},{16,0},{32,16},{48,32},{64,48},{80,64},{96,80},{112,96},{1... | collective-permute-start | bytes 786440 | tf_op jit(solution)/shard_map/ppermute | solution.py:19
  42.2 9.6 %collective-permute-start.10 = (bf16[8,64,256]{2,1,0:T(8,128)(2,1)S(1)}, bf16[8,64,256]{2,1,0:T(8,128)(2,1)}, u32[]{:S(2)}, u32[]{:S(2)}) collective-permute-start(bf16[8,64,256]{2,1,0:T(8,128)(2,1)S(1)} %collective-permute-done.9.over), channel_id=1, source_target_pairs={{0,8},{8,0},{1,9},{9,1},{2,10},{10,2},{3,11},{11,3},{4,12},{12,4},... | collective-permute-start | bytes 786440 | tf_op jit(solution)/shard_map/ppermute | solution.py:19
  45.3 12.9 %collective-permute-start.11 = (bf16[64,2048]{1,0:T(8,128)(2,1)S(1)}, bf16[64,2048]{1,0:T(8,128)(2,1)S(1)}, u32[]{:S(2)}, u32[]{:S(2)}) collective-permute-start(bf16[64,2048]{1,0:T(8,128)(2,1)S(1)} %collective-permute-done.4.refs_6_), channel_id=1, source_target_pairs={{0,112},{16,0},{32,16},{48,32},{64,48},{80,64},{96,80},{112,96},{1... | collective-permute-start | bytes 786440 | tf_op jit(solution)/shard_map/ppermute | solution.py:19
  45.3 12.9 %collective-permute-start.14 = (bf16[64,2048]{1,0:T(8,128)(2,1)S(1)}, bf16[64,2048]{1,0:T(8,128)(2,1)S(1)}, u32[]{:S(2)}, u32[]{:S(2)}) collective-permute-start(bf16[64,2048]{1,0:T(8,128)(2,1)S(1)} %collective-permute-done.7.refs_9_), channel_id=1, source_target_pairs={{0,16},{16,32},{32,48},{48,64},{64,80},{80,96},{96,112},{112,0},{1... | collective-permute-start | bytes 786440 | tf_op jit(solution)/shard_map/ppermute | solution.py:19
  48.2 11.5 %collective-permute-start.15 = (bf16[64,2048]{1,0:T(8,128)(2,1)}, bf16[64,2048]{1,0:T(8,128)(2,1)S(1)}, u32[]{:S(2)}, u32[]{:S(2)}) collective-permute-start(bf16[64,2048]{1,0:T(8,128)(2,1)} %collective-permute-done.13.refs_2_), channel_id=1, source_target_pairs={{0,16},{16,32},{32,48},{48,64},{64,80},{80,96},{96,112},{112,0},{1... | collective-permute-start | bytes 786440 | tf_op jit(solution)/shard_map/ppermute | solution.py:19
  48.2 11.5 %collective-permute-start.16 = (bf16[64,2048]{1,0:T(8,128)(2,1)}, bf16[64,2048]{1,0:T(8,128)(2,1)S(1)}, u32[]{:S(2)}, u32[]{:S(2)}) collective-permute-start(bf16[64,2048]{1,0:T(8,128)(2,1)} %collective-permute-done.12.refs_1_), channel_id=1, source_target_pairs={{0,112},{16,0},{32,16},{48,32},{64,48},{80,64},{96,80},{112,96},{1... | collective-permute-start | bytes 786440 | tf_op jit(solution)/shard_map/ppermute | solution.py:19
  52.9 13.4 %copy-start.9 = (s32[1,8]{1,0:T(1,128)S(1)}, s32[1,8]{1,0:T(1,128)}, u32[]{:S(2)}) copy-start(s32[1,8]{1,0:T(1,128)} %constant.43) | copy-start | bytes 100
  55.2 0.7 copy-start.6
  55.9 15.8 %copy-start.7 = (bf16[640,128]{1,0:T(8,128)(2,1)S(1)}, bf16[640,128]{1,0:T(8,128)(2,1)}, u32[]{:S(2)}) copy-start(bf16[640,128]{1,0:T(8,128)(2,1)} %copy-done.6) | copy-start | bytes 491524
  55.9 9.9 %collective-permute-start.18 = (bf16[640,256]{1,0:T(8,128)(2,1)S(1)}, bf16[640,256]{1,0:T(8,128)(2,1)S(1)}, u32[]{:S(2)}, u32[]{:S(2)}) collective-permute-start(bf16[640,256]{1,0:T(8,128)(2,1)S(1)} %get-tuple-element.15.refs_0_), channel_id=1, source_target_pairs={{0,128},{128,0},{1,129},{129,1},{2,130},{130,2},{3,131},{131,3},{4... | collective-permute-start | bytes 983048 | tf_op jit(solution)/shard_map/ppermute | solution.py:19
  62.5 7.7 %collective-permute-start.21 = (bf16[384,256]{1,0:T(8,128)(2,1)S(1)}, bf16[384,256]{1,0:T(8,128)(2,1)S(1)}, u32[]{:S(2)}, u32[]{:S(2)}) collective-permute-start(bf16[384,256]{1,0:T(8,128)(2,1)S(1)} %get-tuple-element.16.refs_4_), channel_id=1, source_target_pairs={{0,128},{128,0},{1,129},{129,1},{2,130},{130,2},{3,131},{131,3},{4... | collective-permute-start | bytes 589832 | tf_op jit(solution)/shard_map/ppermute | solution.py:19
  65.7 4.6 %collective-permute-start.17 = (bf16[640,256]{1,0:T(8,128)(2,1)S(1)}, bf16[640,256]{1,0:T(8,128)(2,1)S(1)}, u32[]{:S(2)}, u32[]{:S(2)}) collective-permute-start(bf16[640,256]{1,0:T(8,128)(2,1)S(1)} %get-tuple-element.15.refs_0_), channel_id=1, source_target_pairs={{0,8},{8,0},{1,9},{9,1},{2,10},{10,2},{3,11},{11,3},{4,12},{12,4},... | collective-permute-start | bytes 983048 | tf_op jit(solution)/shard_map/ppermute | solution.py:19
  65.8 5.9 %collective-permute-start.19 = (bf16[640,256]{1,0:T(8,128)(2,1)S(1)}, bf16[640,256]{1,0:T(8,128)(2,1)S(1)}, u32[]{:S(2)}, u32[]{:S(2)}) collective-permute-start(bf16[640,256]{1,0:T(8,128)(2,1)S(1)} %collective-permute-done.18.refs_2_), channel_id=1, source_target_pairs={{0,8},{8,0},{1,9},{9,1},{2,10},{10,2},{3,11},{11,3},{4,12},{12,4},... | collective-permute-start | bytes 983048 | tf_op jit(solution)/shard_map/ppermute | solution.py:19
  66.7 3.5 %collective-permute-start.20 = (bf16[384,256]{1,0:T(8,128)(2,1)S(1)}, bf16[384,256]{1,0:T(8,128)(2,1)S(1)}, u32[]{:S(2)}, u32[]{:S(2)}) collective-permute-start(bf16[384,256]{1,0:T(8,128)(2,1)S(1)} %get-tuple-element.16.refs_4_), channel_id=1, source_target_pairs={{0,8},{8,0},{1,9},{9,1},{2,10},{10,2},{3,11},{11,3},{4,12},{12,4},... | collective-permute-start | bytes 589832 | tf_op jit(solution)/shard_map/ppermute | solution.py:19
  70.2 1.4 %collective-permute-start.22 = (bf16[384,256]{1,0:T(8,128)(2,1)S(1)}, bf16[384,256]{1,0:T(8,128)(2,1)S(1)}, u32[]{:S(2)}, u32[]{:S(2)}) collective-permute-start(bf16[384,256]{1,0:T(8,128)(2,1)S(1)} %collective-permute-done.21.refs_6_), channel_id=1, source_target_pairs={{0,8},{8,0},{1,9},{9,1},{2,10},{10,2},{3,11},{11,3},{4,12},{12,4},... | collective-permute-start | bytes 589832 | tf_op jit(solution)/shard_map/ppermute | solution.py:19
  71.6 24.2 %copy-start.1 = (bf16[1,1024,2048]{2,1,0:T(8,128)(2,1)S(1)}, bf16[1,1024,2048]{2,1,0:T(8,128)(2,1)}, u32[]{:S(2)}) copy-start(bf16[1,1024,2048]{2,1,0:T(8,128)(2,1)} %param.15) | copy-start | bytes 12582916
  71.6 24.2 %copy-start.3 = (bf16[1,128,2048]{2,1,0:T(8,128)(2,1)S(1)}, bf16[1,128,2048]{2,1,0:T(8,128)(2,1)}, u32[]{:S(2)}) copy-start(bf16[1,128,2048]{2,1,0:T(8,128)(2,1)} %param.9) | copy-start | bytes 1572868
  97.4 18.1 %collective-permute-start.23 = (bf16[128,2048]{1,0:T(8,128)(2,1)}, bf16[128,2048]{1,0:T(8,128)(2,1)S(1)}, u32[]{:S(2)}, u32[]{:S(2)}) collective-permute-start(bf16[128,2048]{1,0:T(8,128)(2,1)} %shard_map.109), channel_id=1, source_target_pairs={{0,1},{1,2},{2,3},{3,4},{4,5},{5,6},{6,7},{8,9},{9,10},{10,11},{11... | collective-permute-start | bytes 1572872 | tf_op jit(solution)/shard_map/ppermute | solution.py:25

commit v4 on v3

--- a/solution.py
+++ b/solution.py
@@ -111,11 +111,8 @@
     )(temp, *blocks, wq, wkv)
 
 
-def masked_scores(q, keyval, places, qpos, qspan, s_all, column, peak):
-    head_dim = q.shape[1]
-    s = lax.dot_general(
-        q, keyval[:, :head_dim], (((1,), (1,)), ((), ())), preferred_element_type=jnp.float32
-    )
+def masked_scores(q, keys, places, qpos, qspan, s_all, column, peak):
+    s = lax.dot_general(q, keys, (((1,), (1,)), ((), ())), preferred_element_type=jnp.float32)
     for u, place in enumerate(places):
         lanes = slice(u * 128, (u + 1) * 128)
         part = jnp.where(qpos - place <= qspan, s[:, lanes], -1e30)
@@ -124,28 +121,14 @@
     return peak
 
 
-def mixing(s_all, column, keyval, top, total, mixed):
-    rows, head_dim = keyval.shape[0], keyval.shape[1] // 2
+def mixing(s_all, column, values, top, total, mixed):
     parts = []
-    for u in range(rows // 128):
+    for u in range(values.shape[0] // 128):
         w = jnp.exp(s_all[:, column + u * 128 : column + (u + 1) * 128] - top)
         total = total + w
         parts.append(w.astype(jnp.bfloat16))
     w = jnp.concatenate(parts, axis=1)
-    return total, mixed + jnp.dot(w, keyval[:, head_dim:], preferred_element_type=jnp.float32)
-
-
-def chunks(segments, kpos_ref, most=512):
-    column = 0
-    for keyval, place, offsets in segments:
-        for start in range(0, keyval.shape[0], most):
-            size = min(most, keyval.shape[0] - start)
-            places = [
-                kpos_ref[place : place + 1, o * 128 : (o + 1) * 128]
-                for o in offsets[start // 128 : (start + size) // 128]
-            ]
-            yield column, keyval, slice(start, start + size), places
-            column += size
+    return total, mixed + jnp.dot(w, values, preferred_element_type=jnp.float32)
 
 
 TILE = 256
@@ -161,35 +144,45 @@
     return rows, jnp.concatenate(qpos, axis=0), jnp.concatenate(qspan, axis=0)
 
 
-def weighed(q, peak, segments, kpos_ref, qpos, qspan, s_all):
-    for column, keyval, cut, places in chunks(segments, kpos_ref):
-        peak = masked_scores(q, keyval[cut, :], places, qpos, qspan, s_all, column, peak)
-    top = jnp.broadcast_to(jnp.max(peak, axis=-1, keepdims=True), peak.shape)
-    total = jnp.zeros((TILE, 128), jnp.float32)
-    mixed = jnp.zeros((TILE, q.shape[1]), jnp.float32)
-    for column, keyval, cut, _ in chunks(segments, kpos_ref):
-        total, mixed = mixing(s_all, column, keyval[cut, :], top, total, mixed)
-    return top, total, mixed
-
-
 def attend_kernel(at_ref, qa, qb, *refs):
-    parts, (qpos_ref, qspan_ref, kpos_ref, o_ref, q_all, s_all) = refs[:8], refs[8:]
+    parts, (qpos_ref, qspan_ref, kpos_ref, o_ref, q_all, k_all, v_all, s_all) = refs[:8], refs[8:]
     early, late = qa.shape[0], qb.shape[0]
+    own_rows, head_dim = q_all.shape
     q_all[pl.ds(0, early), :] = qa[...]
     q_all[pl.ds(early, late), :] = qb[...]
-    segments = [(parts[i], i, EARLY) for i in range(4)] + [(parts[4 + i], i, LATE) for i in range(4)]
+    for i in range(4):
+        for part, rows in (
+            (parts[i], pl.ds(i * own_rows, early)),
+            (parts[4 + i], pl.ds(i * own_rows + early, late)),
+        ):
+            k_all[rows, :] = part[:, :head_dim]
+            v_all[rows, :] = part[:, head_dim:]
+    offsets, wide = EARLY + LATE, 512
+    cuts = [slice(start, start + wide) for start in range(0, k_all.shape[0], wide)]
 
     def one_tile(t, _):
         rows, qpos, qspan = tile_of(t, at_ref, qpos_ref, qspan_ref)
+        q = q_all[rows, :]
         peak = jnp.full((TILE, 128), -1e30, jnp.float32)
-        _, total, mixed = weighed(q_all[rows, :], peak, segments, kpos_ref, qpos, qspan, s_all)
+        for cut in cuts:
+            places = []
+            for start in range(cut.start, cut.stop, 128):
+                o = offsets[start % own_rows // 128]
+                origin = start // own_rows
+                places.append(kpos_ref[origin : origin + 1, o * 128 : (o + 1) * 128])
+            peak = masked_scores(q, k_all[cut, :], places, qpos, qspan, s_all, cut.start, peak)
+        top = jnp.broadcast_to(jnp.max(peak, axis=-1, keepdims=True), peak.shape)
+        total = jnp.zeros((TILE, 128), jnp.float32)
+        mixed = jnp.zeros((TILE, head_dim), jnp.float32)
+        for cut in cuts:
+            total, mixed = mixing(s_all, cut.start, v_all[cut, :], top, total, mixed)
         result = (mixed / jnp.sum(total, axis=-1, keepdims=True)).astype(jnp.bfloat16)
         for i in range(TILE // 128):
             placed = pl.ds(pl.multiple_of(at_ref[1, t * (TILE // 128) + i] * 128, 128), 128)
             o_ref[placed, :] = result[i * 128 : (i + 1) * 128, :]
         return 0
 
-    lax.fori_loop(0, (early + late) // TILE, one_tile, 0)
+    lax.fori_loop(0, own_rows // TILE, one_tile, 0)
 
 
 def attended(at, queries, keyvals, qpos, qspan, kpos):
@@ -203,6 +196,8 @@
         out_shape=jax.ShapeDtypeStruct((rows, head_dim), jnp.bfloat16),
         scratch_shapes=[
             pltpu.VMEM((rows, head_dim), jnp.bfloat16),
+            pltpu.VMEM((keys, head_dim), jnp.bfloat16),
+            pltpu.VMEM((keys, head_dim), jnp.bfloat16),
             pltpu.VMEM((TILE, keys), jnp.float32),
         ],
         compiler_params=params(24),

time: 118 us -> 117 us (level)
  no operation moved by 1% of the time
where the time goes in v4:
time: 117 us; the launch traced here: 116 us
  starting transfers between devices  41.5 us (35%)
  waiting for transfers between devices  32.9 us (28%)
  Pallas kernels  17.4 us (15%)
  blocking collectives  14.8 us (13%)
  local copies, waits for them, and re-layouts  6.34 us (5%)
  other arithmetic  1.88 us (2%)
    ppermute x23, starting transfers between devices, shifted(): lax.ppermute(block, axis, [(i, (i + distance) % count) for i in range(cou...  33.6 us
    ppermute x23, waiting for transfers between devices, shifted(): lax.ppermute(block, axis, [(i, (i + distance) % count) for i in range(cou...  15.6 us
    all_to_all x1, blocking collectives, per_device(): lax.all_to_all(mixed.reshape(ZS, -1, head_dim), 'z', 0, 0, tiled=True)  14.8 us
    ppermute x1, waiting for transfers between devices, passed_along(): return lax.ppermute(block, axis, route)  14.6 us
    pallas_call x1, Pallas kernels, attended(): pl.pallas_call(attend_kernel, in_specs=[pl.BlockSpec(memory_space=pltpu.S...  8.89 us
    pallas_call x2, Pallas kernels, projected(): pl.pallas_call(functools.partial(project_kernel, len(blocks)), in_specs=[...  5.02 us
    all_to_all x1, starting transfers between devices, per_device(): own_w = lax.all_to_all(by_head, 'z', 0, 0, tiled=True)  4.51 us
    unnamed x22, local copies, waits for them, and re-layouts  4.18 us
  transfers between devices with their start and end apart: 25, of which 9 were waited for; matrix products, arithmetic and copies ran while one was open for 3% of the time, Pallas kernels for 5%

profile of v4, /device:TPU:8, one launch (start us, length us, event | category | flops | bytes accessed | tf_op | source)
XLA Modules:
  0.0 115.8 jit_solution(1311163505046612127)
XLA Ops:
  0.7 1.0 copy-done.2
  1.7 0.9 copy-done.4
  2.6 0.7 copy-done.5
  3.3 0.9 shard_map.104
  4.3 5.9 %collective-permute-start = (bf16[64,2048]{1,0:T(8,128)(2,1)S(1)}, bf16[64,2048]{1,0:T(8,128)(2,1)S(1)}, u32[]{:S(2)}, u32[]{:S(2)}) collective-permute-start(bf16[64,2048]{1,0:T(8,128)(2,1)S(1)} %get-tuple-element.10.refs_0_), channel_id=1, source_target_pairs={{0,112},{16,0},{32,16},{48,32},{64,48},{80,64},{96,80},{112,96},{1... | collective-permute-start | bytes 786440 | tf_op jit(solution)/shard_map/ppermute | solution.py:19
  10.1 3.2 %collective-permute-start.1 = (bf16[64,2048]{1,0:T(8,128)(2,1)S(1)}, bf16[64,2048]{1,0:T(8,128)(2,1)S(1)}, u32[]{:S(2)}, u32[]{:S(2)}) collective-permute-start(bf16[64,2048]{1,0:T(8,128)(2,1)S(1)} %get-tuple-element.11.refs_1_), channel_id=1, source_target_pairs={{0,112},{16,0},{32,16},{48,32},{64,48},{80,64},{96,80},{112,96},{1... | collective-permute-start | bytes 786440 | tf_op jit(solution)/shard_map/ppermute | solution.py:19
  13.4 4.5 %all-to-all-start = ((bf16[8,64,256]{2,1,0:T(8,128)(2,1)}), bf16[8,64,256]{2,1,0:T(8,128)(2,1)S(1)}, u32[]{:S(2)}, u32[]{:S(2)}) async-start(bf16[8,64,256]{2,1,0:T(8,128)(2,1)} %get-tuple-element.12), calls=%async_computation | async-start | bytes 524288 | tf_op jit(solution)/shard_map/all_to_all | solution.py:251
  17.9 0.7 fusion
  18.7 3.3 %collective-permute-start.4 = (bf16[64,2048]{1,0:T(8,128)(2,1)S(1)}, bf16[64,2048]{1,0:T(8,128)(2,1)S(1)}, u32[]{:S(2)}, u32[]{:S(2)}) collective-permute-start(bf16[64,2048]{1,0:T(8,128)(2,1)S(1)} %collective-permute-done.refs_2_), channel_id=1, source_target_pairs={{0,112},{16,0},{32,16},{48,32},{64,48},{80,64},{96,80},{112,96},{1... | collective-permute-start | bytes 786440 | tf_op jit(solution)/shard_map/ppermute | solution.py:19
  22.0 3.4 %collective-permute-done.1.refs_3_ = bf16[64,2048]{1,0:T(8,128)(2,1)S(1)} collective-permute-done((bf16[64,2048]{1,0:T(8,128)(2,1)S(1)}, bf16[64,2048]{1,0:T(8,128)(2,1)S(1)}, u32[]{:S(2)}, u32[]{:S(2)}) %collective-permute-start.1) | collective-permute-done | bytes 262176 | tf_op jit(solution)/shard_map/ppermute | solution.py:19
  25.5 3.8 %collective-permute-start.5 = (bf16[64,2048]{1,0:T(8,128)(2,1)S(1)}, bf16[64,2048]{1,0:T(8,128)(2,1)S(1)}, u32[]{:S(2)}, u32[]{:S(2)}) collective-permute-start(bf16[64,2048]{1,0:T(8,128)(2,1)S(1)} %collective-permute-done.1.refs_3_), channel_id=1, source_target_pairs={{0,112},{16,0},{32,16},{48,32},{64,48},{80,64},{96,80},{112,96},{1... | collective-permute-start | bytes 786440 | tf_op jit(solution)/shard_map/ppermute | solution.py:19
  29.3 2.6 %all-to-all-done.own = bf16[8,64,256]{2,1,0:T(8,128)(2,1)S(1)} async-done(((bf16[8,64,256]{2,1,0:T(8,128)(2,1)}), bf16[8,64,256]{2,1,0:T(8,128)(2,1)S(1)}, u32[]{:S(2)}, u32[]{:S(2)}) %all-to-all-start) | async-done | bytes 262176 | tf_op jit(solution)/shard_map/all_to_all | solution.py:251
  31.9 2.3 %collective-permute-start.9 = (bf16[8,64,256]{2,1,0:T(8,128)(2,1)S(1)}, bf16[8,64,256]{2,1,0:T(8,128)(2,1)S(1)}, u32[]{:S(2)}, u32[]{:S(2)}) collective-permute-start(bf16[8,64,256]{2,1,0:T(8,128)(2,1)S(1)} %all-to-all-done.own), channel_id=1, source_target_pairs={{0,128},{128,0},{1,129},{129,1},{2,130},{130,2},{3,131},{131,3},{4... | collective-permute-start | bytes 786440 | tf_op jit(solution)/shard_map/ppermute | solution.py:19
  34.2 0.7 fusion.2
  34.9 0.1 collective-permute-start.7
  35.0 0.1 collective-permute-start.8
  35.1 3.9 %collective-permute-done.6.refs_8_ = bf16[64,2048]{1,0:T(8,128)(2,1)S(1)} collective-permute-done((bf16[64,2048]{1,0:T(8,128)(2,1)S(1)}, bf16[64,2048]{1,0:T(8,128)(2,1)S(1)}, u32[]{:S(2)}, u32[]{:S(2)}) %collective-permute-start.6) | collective-permute-done | bytes 262176 | tf_op jit(solution)/shard_map/ppermute | solution.py:19
  39.0 3.2 %collective-permute-start.12 = (bf16[64,2048]{1,0:T(8,128)(2,1)S(1)}, bf16[64,2048]{1,0:T(8,128)(2,1)}, u32[]{:S(2)}, u32[]{:S(2)}) collective-permute-start(bf16[64,2048]{1,0:T(8,128)(2,1)S(1)} %collective-permute-done.5.refs_7_), channel_id=1, source_target_pairs={{0,112},{16,0},{32,16},{48,32},{64,48},{80,64},{96,80},{112,96},{1... | collective-permute-start | bytes 786440 | tf_op jit(solution)/shard_map/ppermute | solution.py:19
  42.2 0.1 pad_add_fusion.1.at_ref
  42.3 0.6 constant_dynamic-slice_fusion.temp_ref
  42.9 1.1 dynamic-slice_bitcast_fusion.refs_10_.refs_6_
  44.0 1.3 %collective-permute-done.7.refs_9_ = bf16[64,2048]{1,0:T(8,128)(2,1)S(1)} collective-permute-done((bf16[64,2048]{1,0:T(8,128)(2,1)S(1)}, bf16[64,2048]{1,0:T(8,128)(2,1)S(1)}, u32[]{:S(2)}, u32[]{:S(2)}) %collective-permute-start.7) | collective-permute-done | bytes 262176 | tf_op jit(solution)/shard_map/ppermute | solution.py:19
  45.3 2.0 %collective-permute-start.14 = (bf16[64,2048]{1,0:T(8,128)(2,1)S(1)}, bf16[64,2048]{1,0:T(8,128)(2,1)S(1)}, u32[]{:S(2)}, u32[]{:S(2)}) collective-permute-start(bf16[64,2048]{1,0:T(8,128)(2,1)S(1)} %collective-permute-done.7.refs_9_), channel_id=1, source_target_pairs={{0,16},{16,32},{32,48},{48,64},{64,80},{80,96},{96,112},{112,0},{1... | collective-permute-start | bytes 786440 | tf_op jit(solution)/shard_map/ppermute | solution.py:19
  47.3 0.9 collective-permute-done.13.refs_2_
  48.2 3.6 %collective-permute-start.16 = (bf16[64,2048]{1,0:T(8,128)(2,1)}, bf16[64,2048]{1,0:T(8,128)(2,1)S(1)}, u32[]{:S(2)}, u32[]{:S(2)}) collective-permute-start(bf16[64,2048]{1,0:T(8,128)(2,1)} %collective-permute-done.12.refs_1_), channel_id=1, source_target_pairs={{0,112},{16,0},{32,16},{48,32},{64,48},{80,64},{96,80},{112,96},{1... | collective-permute-start | bytes 786440 | tf_op jit(solution)/shard_map/ppermute | solution.py:19
  51.9 1.0 shard_map.105.refs_11_.refs_7_
  52.9 2.3 %shard_map.106 = (bf16[640,128]{1,0:T(8,128)(2,1)S(1)}, bf16[640,256]{1,0:T(8,128)(2,1)S(1)}) custom-call(f32[1,1]{1,0:T(1,128)} %constant_dynamic-slice_fusion.temp_ref, bf16[64,2048]{1,0:T(8,128)(2,1)S(1)} %get-tuple-element.10.refs_0_, bf16[64,2048]{1,0:T(8,128)(2,1)S(1)} %get-tuple-element.11.refs_1_, bf16[64,2048]{1,0:T(8,128)(2,1)S(1)} %collective-permute-done.refs_2_, ...), custom_call_target="tpu_custom_call" | custom-call | flops 1006632960 | bytes 5177344 | tf_op jit(solution)/shard_map/pallas_call | solution.py:99
  55.2 0.7 copy-done.6
  55.9 2.2 %collective-permute-start.18 = (bf16[640,256]{1,0:T(8,128)(2,1)S(1)}, bf16[640,256]{1,0:T(8,128)(2,1)S(1)}, u32[]{:S(2)}, u32[]{:S(2)}) collective-permute-start(bf16[640,256]{1,0:T(8,128)(2,1)S(1)} %get-tuple-element.15.refs_0_), channel_id=1, source_target_pairs={{0,128},{128,0},{1,129},{129,1},{2,130},{130,2},{3,131},{131,3},{4... | collective-permute-start | bytes 983048 | tf_op jit(solution)/shard_map/ppermute | solution.py:19
  58.0 0.2 convert_reduce_fusion
  58.3 1.4 %collective-permute-done.15.refs_4_ = bf16[64,2048]{1,0:T(8,128)(2,1)S(1)} collective-permute-done((bf16[64,2048]{1,0:T(8,128)(2,1)}, bf16[64,2048]{1,0:T(8,128)(2,1)S(1)}, u32[]{:S(2)}, u32[]{:S(2)}) %collective-permute-start.15) | collective-permute-done | bytes 262176 | tf_op jit(solution)/shard_map/ppermute | solution.py:19
  59.7 2.8 %shard_map.107 = (bf16[384,128]{1,0:T(8,128)(2,1)S(1)}, bf16[384,256]{1,0:T(8,128)(2,1)S(1)}) custom-call(f32[1,1]{1,0:T(1,128)} %constant_dynamic-slice_fusion.temp_ref, bf16[64,2048]{1,0:T(8,128)(2,1)S(1)} %collective-permute-done.11.refs_0_, bf16[64,2048]{1,0:T(8,128)(2,1)} %collective-permute-done.12.refs_1_, ...), custom_call_target="tpu_custom_call" | custom-call | flops 603979776 | bytes 3735552 | tf_op jit(solution)/shard_map/pallas_call | solution.py:99
  62.5 3.1 %collective-permute-start.21 = (bf16[384,256]{1,0:T(8,128)(2,1)S(1)}, bf16[384,256]{1,0:T(8,128)(2,1)S(1)}, u32[]{:S(2)}, u32[]{:S(2)}) collective-permute-start(bf16[384,256]{1,0:T(8,128)(2,1)S(1)} %get-tuple-element.16.refs_4_), channel_id=1, source_target_pairs={{0,128},{128,0},{1,129},{129,1},{2,130},{130,2},{3,131},{131,3},{4... | collective-permute-start | bytes 589832 | tf_op jit(solution)/shard_map/ppermute | solution.py:19
  65.6 0.1 select_reduce_fusion
  65.7 0.1 collective-permute-start.17
  65.8 0.5 collective-permute-start.19
  66.3 0.2 copy.23
  66.5 0.2 copy.20
  66.7 0.2 collective-permute-start.20
  66.9 3.3 %collective-permute-done.21.refs_6_ = bf16[384,256]{1,0:T(8,128)(2,1)S(1)} collective-permute-done((bf16[384,256]{1,0:T(8,128)(2,1)S(1)}, bf16[384,256]{1,0:T(8,128)(2,1)S(1)}, u32[]{:S(2)}, u32[]{:S(2)}) %collective-permute-start.21) | collective-permute-done | bytes 196640 | tf_op jit(solution)/shard_map/ppermute | solution.py:19
  70.2 0.1 subtract_add_fusion
  70.3 1.3 %collective-permute-done.22.refs_7_ = bf16[384,256]{1,0:T(8,128)(2,1)S(1)} collective-permute-done((bf16[384,256]{1,0:T(8,128)(2,1)S(1)}, bf16[384,256]{1,0:T(8,128)(2,1)S(1)}, u32[]{:S(2)}, u32[]{:S(2)}) %collective-permute-start.22) | collective-permute-done | bytes 196640 | tf_op jit(solution)/shard_map/ppermute | solution.py:19
  71.7 8.9 %shard_map.108 = bf16[1024,128]{1,0:T(8,128)(2,1)S(1)} custom-call(s32[2,8]{1,0:T(2,128)S(1)} %pad_add_fusion.at_ref, bf16[640,128]{1,0:T(8,128)(2,1)S(1)} %copy-done.7, bf16[384,128]{1,0:T(8,128)(2,1)S(1)} %get-tuple-element.14.qb, bf16[640,256]{1,0:T(8,128)(2,1)S(1)} %get-tuple-element.15.refs_0_, bf16[640,256]{1,0:T(8,128)(2,1)S(1)} %collective-permute-done.17.refs_1_, ...), custom_call_target="tpu_custom_call" | custom-call | flops 21474836480 | bytes 2097152 | tf_op jit(solution)/shard_map/pallas_call | solution.py:192
  80.5 14.8 %all_to_all.10.m_ref = bf16[8,128,128]{2,1,0:T(8,128)(2,1)S(1)} all-to-all(bf16[8,128,128]{2,1,0:T(8,128)(2,1)S(1)} %bitcast.28), channel_id=1, replica_groups=mesh['yh'=2,'z'=8,'c'=2,'yl'=2,'x'=4] {'z'}, dimensions={0} | all-to-all | bytes 524288 | tf_op jit(solution)/shard_map/all_to_all | solution.py:282
  95.4 1.6 %shard_map.109 = bf16[128,2048]{1,0:T(8,128)(2,1)} custom-call(bf16[8,128,128]{2,1,0:T(8,128)(2,1)S(1)} %all_to_all.10.m_ref, bf16[1024,2048]{1,0:T(8,128)(2,1)S(1)} %bitcast.24, bf16[128,2048]{1,0:T(8,128)(2,1)S(1)} %bitcast.26), custom_call_target="tpu_custom_call" | custom-call | flops 536870912 | bytes 6291456 | tf_op jit(solution)/shard_map/pallas_call | solution.py:220
  96.9 3.4 %collective-permute-start.23 = (bf16[128,2048]{1,0:T(8,128)(2,1)}, bf16[128,2048]{1,0:T(8,128)(2,1)S(1)}, u32[]{:S(2)}, u32[]{:S(2)}) collective-permute-start(bf16[128,2048]{1,0:T(8,128)(2,1)} %shard_map.109), channel_id=1, source_target_pairs={{0,1},{1,2},{2,3},{3,4},{4,5},{5,6},{6,7},{8,9},{9,10},{10,11},{11... | collective-permute-start | bytes 1572872 | tf_op jit(solution)/shard_map/ppermute | solution.py:25
  100.3 14.6 %collective-permute-done.23 = bf16[128,2048]{1,0:T(8,128)(2,1)S(1)} collective-permute-done((bf16[128,2048]{1,0:T(8,128)(2,1)}, bf16[128,2048]{1,0:T(8,128)(2,1)S(1)}, u32[]{:S(2)}, u32[]{:S(2)}) %collective-permute-start.23) | collective-permute-done | bytes 524320 | tf_op jit(solution)/shard_map/ppermute | solution.py:25
  115.0 0.8 copy.30
  (48 shorter events, 0.2 us)
Async XLA Ops:
  0.6 41.7 %copy-start = (f32[1,8]{1,0:T(1,128)S(1)}, f32[1,8]{1,0:T(1,128)}, u32[]{:S(2)}) copy-start(f32[1,8]{1,0:T(1,128)} %param.16) | copy-start | bytes 100
  0.6 1.0 copy-start.2
  1.7 0.9 copy-start.4
  2.6 0.7 copy-start.5
  4.3 53.8 %copy-start.8 = (s32[4096]{0:T(1024)S(1)}, s32[4096]{0:T(1024)}, u32[]{:S(2)}) copy-start(s32[4096]{0:T(1024)} %param.11) | copy-start | bytes 49156
  4.3 14.5 %collective-permute-start = (bf16[64,2048]{1,0:T(8,128)(2,1)S(1)}, bf16[64,2048]{1,0:T(8,128)(2,1)S(1)}, u32[]{:S(2)}, u32[]{:S(2)}) collective-permute-start(bf16[64,2048]{1,0:T(8,128)(2,1)S(1)} %get-tuple-element.10.refs_0_), channel_id=1, source_target_pairs={{0,112},{16,0},{32,16},{48,32},{64,48},{80,64},{96,80},{112,96},{1... | collective-permute-start | bytes 786440 | tf_op jit(solution)/shard_map/ppermute | solution.py:19
  10.1 19.2 %collective-permute-start.2 = (bf16[64,2048]{1,0:T(8,128)(2,1)S(1)}, bf16[64,2048]{1,0:T(8,128)(2,1)S(1)}, u32[]{:S(2)}, u32[]{:S(2)}) collective-permute-start(bf16[64,2048]{1,0:T(8,128)(2,1)S(1)} %get-tuple-element.10.refs_0_), channel_id=1, source_target_pairs={{0,16},{16,32},{32,48},{48,64},{64,80},{80,96},{96,112},{112,0},{1... | collective-permute-start | bytes 786440 | tf_op jit(solution)/shard_map/ppermute | solution.py:19
  10.1 15.3 %collective-permute-start.1 = (bf16[64,2048]{1,0:T(8,128)(2,1)S(1)}, bf16[64,2048]{1,0:T(8,128)(2,1)S(1)}, u32[]{:S(2)}, u32[]{:S(2)}) collective-permute-start(bf16[64,2048]{1,0:T(8,128)(2,1)S(1)} %get-tuple-element.11.refs_1_), channel_id=1, source_target_pairs={{0,112},{16,0},{32,16},{48,32},{64,48},{80,64},{96,80},{112,96},{1... | collective-permute-start | bytes 786440 | tf_op jit(solution)/shard_map/ppermute | solution.py:19
  13.4 21.5 %collective-permute-start.3 = (bf16[64,2048]{1,0:T(8,128)(2,1)S(1)}, bf16[64,2048]{1,0:T(8,128)(2,1)S(1)}, u32[]{:S(2)}, u32[]{:S(2)}) collective-permute-start(bf16[64,2048]{1,0:T(8,128)(2,1)S(1)} %get-tuple-element.11.refs_1_), channel_id=1, source_target_pairs={{0,16},{16,32},{32,48},{48,64},{64,80},{80,96},{96,112},{112,0},{1... | collective-permute-start | bytes 786440 | tf_op jit(solution)/shard_map/ppermute | solution.py:19
  13.4 18.5 %all-to-all-start = ((bf16[8,64,256]{2,1,0:T(8,128)(2,1)}), bf16[8,64,256]{2,1,0:T(8,128)(2,1)S(1)}, u32[]{:S(2)}, u32[]{:S(2)}) async-start(bf16[8,64,256]{2,1,0:T(8,128)(2,1)} %get-tuple-element.12), calls=%async_computation | async-start | bytes 524288 | tf_op jit(solution)/shard_map/all_to_all | solution.py:251
  18.7 16.2 %collective-permute-start.4 = (bf16[64,2048]{1,0:T(8,128)(2,1)S(1)}, bf16[64,2048]{1,0:T(8,128)(2,1)S(1)}, u32[]{:S(2)}, u32[]{:S(2)}) collective-permute-start(bf16[64,2048]{1,0:T(8,128)(2,1)S(1)} %collective-permute-done.refs_2_), channel_id=1, source_target_pairs={{0,112},{16,0},{32,16},{48,32},{64,48},{80,64},{96,80},{112,96},{1... | collective-permute-start | bytes 786440 | tf_op jit(solution)/shard_map/ppermute | solution.py:19
  25.5 13.5 %collective-permute-start.5 = (bf16[64,2048]{1,0:T(8,128)(2,1)S(1)}, bf16[64,2048]{1,0:T(8,128)(2,1)S(1)}, u32[]{:S(2)}, u32[]{:S(2)}) collective-permute-start(bf16[64,2048]{1,0:T(8,128)(2,1)S(1)} %collective-permute-done.1.refs_3_), channel_id=1, source_target_pairs={{0,112},{16,0},{32,16},{48,32},{64,48},{80,64},{96,80},{112,96},{1... | collective-permute-start | bytes 786440 | tf_op jit(solution)/shard_map/ppermute | solution.py:19
  29.3 9.7 %collective-permute-start.6 = (bf16[64,2048]{1,0:T(8,128)(2,1)S(1)}, bf16[64,2048]{1,0:T(8,128)(2,1)S(1)}, u32[]{:S(2)}, u32[]{:S(2)}) collective-permute-start(bf16[64,2048]{1,0:T(8,128)(2,1)S(1)} %collective-permute-done.2.refs_4_), channel_id=1, source_target_pairs={{0,16},{16,32},{32,48},{48,64},{64,80},{80,96},{96,112},{112,0},{1... | collective-permute-start | bytes 786440 | tf_op jit(solution)/shard_map/ppermute | solution.py:19
  31.9 10.3 %collective-permute-start.9 = (bf16[8,64,256]{2,1,0:T(8,128)(2,1)S(1)}, bf16[8,64,256]{2,1,0:T(8,128)(2,1)S(1)}, u32[]{:S(2)}, u32[]{:S(2)}) collective-permute-start(bf16[8,64,256]{2,1,0:T(8,128)(2,1)S(1)} %all-to-all-done.own), channel_id=1, source_target_pairs={{0,128},{128,0},{1,129},{129,1},{2,130},{130,2},{3,131},{131,3},{4... | collective-permute-start | bytes 786440 | tf_op jit(solution)/shard_map/ppermute | solution.py:19
  34.9 10.4 %collective-permute-start.7 = (bf16[64,2048]{1,0:T(8,128)(2,1)S(1)}, bf16[64,2048]{1,0:T(8,128)(2,1)S(1)}, u32[]{:S(2)}, u32[]{:S(2)}) collective-permute-start(bf16[64,2048]{1,0:T(8,128)(2,1)S(1)} %collective-permute-done.3.refs_5_), channel_id=1, source_target_pairs={{0,16},{16,32},{32,48},{48,64},{64,80},{80,96},{96,112},{112,0},{1... | collective-permute-start | bytes 786440 | tf_op jit(solution)/shard_map/ppermute | solution.py:19
  35.0 10.3 %collective-permute-start.8 = (bf16[8,64,256]{2,1,0:T(8,128)(2,1)S(1)}, bf16[8,64,256]{2,1,0:T(8,128)(2,1)S(1)}, u32[]{:S(2)}, u32[]{:S(2)}) collective-permute-start(bf16[8,64,256]{2,1,0:T(8,128)(2,1)S(1)} %all-to-all-done.own), channel_id=1, source_target_pairs={{0,8},{8,0},{1,9},{9,1},{2,10},{10,2},{3,11},{11,3},{4,12},{12,4},... | collective-permute-start | bytes 786440 | tf_op jit(solution)/shard_map/ppermute | solution.py:19
  39.0 9.2 %collective-permute-start.13 = (bf16[64,2048]{1,0:T(8,128)(2,1)S(1)}, bf16[64,2048]{1,0:T(8,128)(2,1)}, u32[]{:S(2)}, u32[]{:S(2)}) collective-permute-start(bf16[64,2048]{1,0:T(8,128)(2,1)S(1)} %collective-permute-done.6.refs_8_), channel_id=1, source_target_pairs={{0,16},{16,32},{32,48},{48,64},{64,80},{80,96},{96,112},{112,0},{1... | collective-permute-start | bytes 786440 | tf_op jit(solution)/shard_map/ppermute | solution.py:19
  39.0 9.3 %collective-permute-start.12 = (bf16[64,2048]{1,0:T(8,128)(2,1)S(1)}, bf16[64,2048]{1,0:T(8,128)(2,1)}, u32[]{:S(2)}, u32[]{:S(2)}) collective-permute-start(bf16[64,2048]{1,0:T(8,128)(2,1)S(1)} %collective-permute-done.5.refs_7_), channel_id=1, source_target_pairs={{0,112},{16,0},{32,16},{48,32},{64,48},{80,64},{96,80},{112,96},{1... | collective-permute-start | bytes 786440 | tf_op jit(solution)/shard_map/ppermute | solution.py:19
  42.2 9.6 %collective-permute-start.10 = (bf16[8,64,256]{2,1,0:T(8,128)(2,1)S(1)}, bf16[8,64,256]{2,1,0:T(8,128)(2,1)}, u32[]{:S(2)}, u32[]{:S(2)}) collective-permute-start(bf16[8,64,256]{2,1,0:T(8,128)(2,1)S(1)} %collective-permute-done.9.over), channel_id=1, source_target_pairs={{0,8},{8,0},{1,9},{9,1},{2,10},{10,2},{3,11},{11,3},{4,12},{12,4},... | collective-permute-start | bytes 786440 | tf_op jit(solution)/shard_map/ppermute | solution.py:19
  45.3 12.9 %collective-permute-start.11 = (bf16[64,2048]{1,0:T(8,128)(2,1)S(1)}, bf16[64,2048]{1,0:T(8,128)(2,1)S(1)}, u32[]{:S(2)}, u32[]{:S(2)}) collective-permute-start(bf16[64,2048]{1,0:T(8,128)(2,1)S(1)} %collective-permute-done.4.refs_6_), channel_id=1, source_target_pairs={{0,112},{16,0},{32,16},{48,32},{64,48},{80,64},{96,80},{112,96},{1... | collective-permute-start | bytes 786440 | tf_op jit(solution)/shard_map/ppermute | solution.py:19
  45.3 12.9 %collective-permute-start.14 = (bf16[64,2048]{1,0:T(8,128)(2,1)S(1)}, bf16[64,2048]{1,0:T(8,128)(2,1)S(1)}, u32[]{:S(2)}, u32[]{:S(2)}) collective-permute-start(bf16[64,2048]{1,0:T(8,128)(2,1)S(1)} %collective-permute-done.7.refs_9_), channel_id=1, source_target_pairs={{0,16},{16,32},{32,48},{48,64},{64,80},{80,96},{96,112},{112,0},{1... | collective-permute-start | bytes 786440 | tf_op jit(solution)/shard_map/ppermute | solution.py:19
  48.2 11.5 %collective-permute-start.15 = (bf16[64,2048]{1,0:T(8,128)(2,1)}, bf16[64,2048]{1,0:T(8,128)(2,1)S(1)}, u32[]{:S(2)}, u32[]{:S(2)}) collective-permute-start(bf16[64,2048]{1,0:T(8,128)(2,1)} %collective-permute-done.13.refs_2_), channel_id=1, source_target_pairs={{0,16},{16,32},{32,48},{48,64},{64,80},{80,96},{96,112},{112,0},{1... | collective-permute-start | bytes 786440 | tf_op jit(solution)/shard_map/ppermute | solution.py:19
  48.2 11.5 %collective-permute-start.16 = (bf16[64,2048]{1,0:T(8,128)(2,1)}, bf16[64,2048]{1,0:T(8,128)(2,1)S(1)}, u32[]{:S(2)}, u32[]{:S(2)}) collective-permute-start(bf16[64,2048]{1,0:T(8,128)(2,1)} %collective-permute-done.12.refs_1_), channel_id=1, source_target_pairs={{0,112},{16,0},{32,16},{48,32},{64,48},{80,64},{96,80},{112,96},{1... | collective-permute-start | bytes 786440 | tf_op jit(solution)/shard_map/ppermute | solution.py:19
  52.9 13.4 %copy-start.9 = (s32[1,8]{1,0:T(1,128)S(1)}, s32[1,8]{1,0:T(1,128)}, u32[]{:S(2)}) copy-start(s32[1,8]{1,0:T(1,128)} %constant.43) | copy-start | bytes 100
  55.2 0.7 copy-start.6
  55.9 15.8 %copy-start.7 = (bf16[640,128]{1,0:T(8,128)(2,1)S(1)}, bf16[640,128]{1,0:T(8,128)(2,1)}, u32[]{:S(2)}) copy-start(bf16[640,128]{1,0:T(8,128)(2,1)} %copy-done.6) | copy-start | bytes 491524
  55.9 9.9 %collective-permute-start.18 = (bf16[640,256]{1,0:T(8,128)(2,1)S(1)}, bf16[640,256]{1,0:T(8,128)(2,1)S(1)}, u32[]{:S(2)}, u32[]{:S(2)}) collective-permute-start(bf16[640,256]{1,0:T(8,128)(2,1)S(1)} %get-tuple-element.15.refs_0_), channel_id=1, source_target_pairs={{0,128},{128,0},{1,129},{129,1},{2,130},{130,2},{3,131},{131,3},{4... | collective-permute-start | bytes 983048 | tf_op jit(solution)/shard_map/ppermute | solution.py:19
  62.5 7.7 %collective-permute-start.21 = (bf16[384,256]{1,0:T(8,128)(2,1)S(1)}, bf16[384,256]{1,0:T(8,128)(2,1)S(1)}, u32[]{:S(2)}, u32[]{:S(2)}) collective-permute-start(bf16[384,256]{1,0:T(8,128)(2,1)S(1)} %get-tuple-element.16.refs_4_), channel_id=1, source_target_pairs={{0,128},{128,0},{1,129},{129,1},{2,130},{130,2},{3,131},{131,3},{4... | collective-permute-start | bytes 589832 | tf_op jit(solution)/shard_map/ppermute | solution.py:19
  65.7 4.6 %collective-permute-start.17 = (bf16[640,256]{1,0:T(8,128)(2,1)S(1)}, bf16[640,256]{1,0:T(8,128)(2,1)S(1)}, u32[]{:S(2)}, u32[]{:S(2)}) collective-permute-start(bf16[640,256]{1,0:T(8,128)(2,1)S(1)} %get-tuple-element.15.refs_0_), channel_id=1, source_target_pairs={{0,8},{8,0},{1,9},{9,1},{2,10},{10,2},{3,11},{11,3},{4,12},{12,4},... | collective-permute-start | bytes 983048 | tf_op jit(solution)/shard_map/ppermute | solution.py:19
  65.8 5.9 %collective-permute-start.19 = (bf16[640,256]{1,0:T(8,128)(2,1)S(1)}, bf16[640,256]{1,0:T(8,128)(2,1)S(1)}, u32[]{:S(2)}, u32[]{:S(2)}) collective-permute-start(bf16[640,256]{1,0:T(8,128)(2,1)S(1)} %collective-permute-done.18.refs_2_), channel_id=1, source_target_pairs={{0,8},{8,0},{1,9},{9,1},{2,10},{10,2},{3,11},{11,3},{4,12},{12,4},... | collective-permute-start | bytes 983048 | tf_op jit(solution)/shard_map/ppermute | solution.py:19
  66.7 3.5 %collective-permute-start.20 = (bf16[384,256]{1,0:T(8,128)(2,1)S(1)}, bf16[384,256]{1,0:T(8,128)(2,1)S(1)}, u32[]{:S(2)}, u32[]{:S(2)}) collective-permute-start(bf16[384,256]{1,0:T(8,128)(2,1)S(1)} %get-tuple-element.16.refs_4_), channel_id=1, source_target_pairs={{0,8},{8,0},{1,9},{9,1},{2,10},{10,2},{3,11},{11,3},{4,12},{12,4},... | collective-permute-start | bytes 589832 | tf_op jit(solution)/shard_map/ppermute | solution.py:19
  70.2 1.4 %collective-permute-start.22 = (bf16[384,256]{1,0:T(8,128)(2,1)S(1)}, bf16[384,256]{1,0:T(8,128)(2,1)S(1)}, u32[]{:S(2)}, u32[]{:S(2)}) collective-permute-start(bf16[384,256]{1,0:T(8,128)(2,1)S(1)} %collective-permute-done.21.refs_6_), channel_id=1, source_target_pairs={{0,8},{8,0},{1,9},{9,1},{2,10},{10,2},{3,11},{11,3},{4,12},{12,4},... | collective-permute-start | bytes 589832 | tf_op jit(solution)/shard_map/ppermute | solution.py:19
  71.6 23.8 %copy-start.1 = (bf16[1,1024,2048]{2,1,0:T(8,128)(2,1)S(1)}, bf16[1,1024,2048]{2,1,0:T(8,128)(2,1)}, u32[]{:S(2)}) copy-start(bf16[1,1024,2048]{2,1,0:T(8,128)(2,1)} %param.15) | copy-start | bytes 12582916
  71.6 23.8 %copy-start.3 = (bf16[1,128,2048]{2,1,0:T(8,128)(2,1)S(1)}, bf16[1,128,2048]{2,1,0:T(8,128)(2,1)}, u32[]{:S(2)}) copy-start(bf16[1,128,2048]{2,1,0:T(8,128)(2,1)} %param.9) | copy-start | bytes 1572868
  96.9 18.0 %collective-permute-start.23 = (bf16[128,2048]{1,0:T(8,128)(2,1)}, bf16[128,2048]{1,0:T(8,128)(2,1)S(1)}, u32[]{:S(2)}, u32[]{:S(2)}) collective-permute-start(bf16[128,2048]{1,0:T(8,128)(2,1)} %shard_map.109), channel_id=1, source_target_pairs={{0,1},{1,2},{2,3},{3,4},{4,5},{5,6},{6,7},{8,9},{9,10},{10,11},{11... | collective-permute-start | bytes 1572872 | tf_op jit(solution)/shard_map/ppermute | solution.py:25

commit v5 on v4

--- a/solution.py
+++ b/solution.py
@@ -29,13 +29,22 @@
     return pltpu.CompilerParams(vmem_limit_bytes=mib * MIB)
 
 
-def entry_kernel(x_ref, g_ref, w_ref, upper_ref, lower_ref, p_ref):
+def entry_kernel(x_any, g_any, w_any, upper_ref, lower_ref, p_ref, x_ref, g_ref, w_ref, sems):
+    copies = [
+        pltpu.make_async_copy(source, target, sems.at[i])
+        for i, (source, target) in enumerate(((x_any, x_ref), (g_any, g_ref), (w_any, w_ref)))
+    ]
+    for copy in copies:
+        copy.start()
+    copies[0].wait()
+    copies[1].wait()
     half = upper_ref.shape[0]
     for part, n_ref in enumerate((upper_ref, lower_ref)):
         x = x_ref[part * half : (part + 1) * half, :].astype(jnp.float32)
         n_ref[...] = (
             x * lax.rsqrt(jnp.mean(x * x, axis=-1, keepdims=True) + 1e-05) * g_ref[...]
         ).astype(jnp.bfloat16)
+    copies[2].wait()
     heads, _, wide = p_ref.shape
     width, head_dim = heads * wide // 2, wide // 2
     for h in range(heads):
@@ -45,13 +54,22 @@
 
 def entry(x, gain, slab, heads):
     rows, columns = slab.shape
+    vmem = pl.BlockSpec(memory_space=pltpu.VMEM)
     return pl.pallas_call(
         entry_kernel,
+        in_specs=[pl.BlockSpec(memory_space=pltpu.HBM)] * 3,
+        out_specs=[vmem] * 3,
         out_shape=[
             *[jax.ShapeDtypeStruct((x.shape[0] // 2, x.shape[1]), jnp.bfloat16)] * 2,
             jax.ShapeDtypeStruct((heads, rows, columns // heads), jnp.bfloat16),
         ],
-        compiler_params=params(16),
+        scratch_shapes=[
+            pltpu.VMEM(x.shape, x.dtype),
+            pltpu.VMEM(gain.shape, gain.dtype),
+            pltpu.VMEM(slab.shape, slab.dtype),
+            pltpu.SemaphoreType.DMA((3,)),
+        ],
+        compiler_params=params(54),
         cost_estimate=pl.CostEstimate(flops=0, bytes_accessed=3 * x.size * 2, transcendentals=0),
     )(x, gain, slab)
 

time: 117 us -> 116 us (level)
    pallas_call x1, Pallas kernels: 0.92 us -> 2.16 us  [entry(): pl.pallas_call(entry_kernel, in_specs=[pl.BlockSpec(memory_space=pltpu.HB...]
    unnamed x22 -> x20, local copies, waits for them, and re-layouts: 4.18 us -> 3.39 us
  transfers between devices with their start and end apart: 25 -> 25, of which waited for: 9 -> 10; matrix products, arithmetic and copies ran while one was open for 3% -> 4% of each run, Pallas kernels for 5% -> 5%
where the time goes in v5:
time: 116 us; the launch traced here: 115 us
  starting transfers between devices  41.4 us (36%)
  waiting for transfers between devices  31.8 us (27%)
  Pallas kernels  18.1 us (16%)
  blocking collectives  14.9 us (13%)
  local copies, waits for them, and re-layouts  5.61 us (5%)
  other arithmetic  1.88 us (2%)
    ppermute x23, starting transfers between devices, shifted(): lax.ppermute(block, axis, [(i, (i + distance) % count) for i in range(cou...  33.5 us
    all_to_all x1, blocking collectives, per_device(): lax.all_to_all(mixed.reshape(ZS, -1, head_dim), 'z', 0, 0, tiled=True)  14.9 us
    ppermute x23, waiting for transfers between devices, shifted(): lax.ppermute(block, axis, [(i, (i + distance) % count) for i in range(cou...  14.7 us
    ppermute x1, waiting for transfers between devices, passed_along(): return lax.ppermute(block, axis, route)  14.6 us
    pallas_call x1, Pallas kernels, attended(): pl.pallas_call(attend_kernel, in_specs=[pl.BlockSpec(memory_space=pltpu.S...  8.87 us
    pallas_call x2, Pallas kernels, projected(): pl.pallas_call(functools.partial(project_kernel, len(blocks)), in_specs=[...  4.9 us
    all_to_all x1, starting transfers between devices, per_device(): own_w = lax.all_to_all(by_head, 'z', 0, 0, tiled=True)  4.51 us
    ppermute x1, starting transfers between devices, passed_along(): return lax.ppermute(block, axis, route)  3.39 us
  transfers between devices with their start and end apart: 25, of which 10 were waited for; matrix products, arithmetic and copies ran while one was open for 4% of the time, Pallas kernels for 5%

profile of v5, /device:TPU:8, one launch (start us, length us, event | category | flops | bytes accessed | tf_op | source)
XLA Modules:
  0.0 114.6 jit_solution(17636052739179114389)
XLA Ops:
  0.6 2.2 %shard_map.104 = (bf16[64,2048]{1,0:T(8,128)(2,1)}, bf16[64,2048]{1,0:T(8,128)(2,1)}, bf16[8,64,256]{2,1,0:T(8,128)(2,1)}) custom-call(bf16[128,2048]{1,0:T(8,128)(2,1)} %bitcast.25, f32[1,2048]{1,0:T(1,128)} %g_any.1, bf16[64,2048]{1,0:T(8,128)(2,1)} %bitcast.32), custom_call_target="tpu_custom_call" | custom-call | bytes 1572864 | tf_op jit(solution)/shard_map/pallas_call | solution.py:58
  2.8 5.9 %collective-permute-start = (bf16[64,2048]{1,0:T(8,128)(2,1)}, bf16[64,2048]{1,0:T(8,128)(2,1)S(1)}, u32[]{:S(2)}, u32[]{:S(2)}) collective-permute-start(bf16[64,2048]{1,0:T(8,128)(2,1)} %get-tuple-element.10.refs_0_), channel_id=1, source_target_pairs={{0,112},{16,0},{32,16},{48,32},{64,48},{80,64},{96,80},{112,96},{1... | collective-permute-start | bytes 786440 | tf_op jit(solution)/shard_map/ppermute | solution.py:19
  8.8 3.2 %collective-permute-start.1 = (bf16[64,2048]{1,0:T(8,128)(2,1)}, bf16[64,2048]{1,0:T(8,128)(2,1)S(1)}, u32[]{:S(2)}, u32[]{:S(2)}) collective-permute-start(bf16[64,2048]{1,0:T(8,128)(2,1)} %get-tuple-element.11.refs_1_), channel_id=1, source_target_pairs={{0,112},{16,0},{32,16},{48,32},{64,48},{80,64},{96,80},{112,96},{1... | collective-permute-start | bytes 786440 | tf_op jit(solution)/shard_map/ppermute | solution.py:19
  12.0 4.5 %all-to-all-start = ((bf16[8,64,256]{2,1,0:T(8,128)(2,1)}), bf16[8,64,256]{2,1,0:T(8,128)(2,1)S(1)}, u32[]{:S(2)}, u32[]{:S(2)}) async-start(bf16[8,64,256]{2,1,0:T(8,128)(2,1)} %get-tuple-element.12), calls=%async_computation | async-start | bytes 524288 | tf_op jit(solution)/shard_map/all_to_all | solution.py:269
  16.5 0.7 fusion
  17.4 3.3 %collective-permute-start.4 = (bf16[64,2048]{1,0:T(8,128)(2,1)S(1)}, bf16[64,2048]{1,0:T(8,128)(2,1)S(1)}, u32[]{:S(2)}, u32[]{:S(2)}) collective-permute-start(bf16[64,2048]{1,0:T(8,128)(2,1)S(1)} %collective-permute-done.refs_2_), channel_id=1, source_target_pairs={{0,112},{16,0},{32,16},{48,32},{64,48},{80,64},{96,80},{112,96},{1... | collective-permute-start | bytes 786440 | tf_op jit(solution)/shard_map/ppermute | solution.py:19
  20.7 3.7 %collective-permute-done.1.refs_3_ = bf16[64,2048]{1,0:T(8,128)(2,1)S(1)} collective-permute-done((bf16[64,2048]{1,0:T(8,128)(2,1)}, bf16[64,2048]{1,0:T(8,128)(2,1)S(1)}, u32[]{:S(2)}, u32[]{:S(2)}) %collective-permute-start.1) | collective-permute-done | bytes 262176 | tf_op jit(solution)/shard_map/ppermute | solution.py:19
  24.4 3.7 %collective-permute-start.5 = (bf16[64,2048]{1,0:T(8,128)(2,1)S(1)}, bf16[64,2048]{1,0:T(8,128)(2,1)S(1)}, u32[]{:S(2)}, u32[]{:S(2)}) collective-permute-start(bf16[64,2048]{1,0:T(8,128)(2,1)S(1)} %collective-permute-done.1.refs_3_), channel_id=1, source_target_pairs={{0,112},{16,0},{32,16},{48,32},{64,48},{80,64},{96,80},{112,96},{1... | collective-permute-start | bytes 786440 | tf_op jit(solution)/shard_map/ppermute | solution.py:19
  28.2 2.6 %all-to-all-done.own = bf16[8,64,256]{2,1,0:T(8,128)(2,1)S(1)} async-done(((bf16[8,64,256]{2,1,0:T(8,128)(2,1)}), bf16[8,64,256]{2,1,0:T(8,128)(2,1)S(1)}, u32[]{:S(2)}, u32[]{:S(2)}) %all-to-all-start) | async-done | bytes 262176 | tf_op jit(solution)/shard_map/all_to_all | solution.py:269
  30.8 2.3 %collective-permute-start.9 = (bf16[8,64,256]{2,1,0:T(8,128)(2,1)S(1)}, bf16[8,64,256]{2,1,0:T(8,128)(2,1)S(1)}, u32[]{:S(2)}, u32[]{:S(2)}) collective-permute-start(bf16[8,64,256]{2,1,0:T(8,128)(2,1)S(1)} %all-to-all-done.own), channel_id=1, source_target_pairs={{0,128},{128,0},{1,129},{129,1},{2,130},{130,2},{3,131},{131,3},{4... | collective-permute-start | bytes 786440 | tf_op jit(solution)/shard_map/ppermute | solution.py:19
  33.0 0.7 fusion.2
  33.7 0.1 collective-permute-start.7
  33.9 0.1 collective-permute-start.8
  34.0 3.9 %collective-permute-done.6.refs_8_ = bf16[64,2048]{1,0:T(8,128)(2,1)S(1)} collective-permute-done((bf16[64,2048]{1,0:T(8,128)(2,1)S(1)}, bf16[64,2048]{1,0:T(8,128)(2,1)S(1)}, u32[]{:S(2)}, u32[]{:S(2)}) %collective-permute-start.6) | collective-permute-done | bytes 262176 | tf_op jit(solution)/shard_map/ppermute | solution.py:19
  37.8 3.2 %collective-permute-start.12 = (bf16[64,2048]{1,0:T(8,128)(2,1)S(1)}, bf16[64,2048]{1,0:T(8,128)(2,1)}, u32[]{:S(2)}, u32[]{:S(2)}) collective-permute-start(bf16[64,2048]{1,0:T(8,128)(2,1)S(1)} %collective-permute-done.5.refs_7_), channel_id=1, source_target_pairs={{0,112},{16,0},{32,16},{48,32},{64,48},{80,64},{96,80},{112,96},{1... | collective-permute-start | bytes 786440 | tf_op jit(solution)/shard_map/ppermute | solution.py:19
  41.1 0.1 pad_add_fusion.1.at_ref
  41.2 0.6 constant_dynamic-slice_fusion.temp_ref
  41.8 1.1 dynamic-slice_bitcast_fusion.refs_10_.refs_6_
  42.9 1.3 %collective-permute-done.7.refs_9_ = bf16[64,2048]{1,0:T(8,128)(2,1)S(1)} collective-permute-done((bf16[64,2048]{1,0:T(8,128)(2,1)S(1)}, bf16[64,2048]{1,0:T(8,128)(2,1)S(1)}, u32[]{:S(2)}, u32[]{:S(2)}) %collective-permute-start.7) | collective-permute-done | bytes 262176 | tf_op jit(solution)/shard_map/ppermute | solution.py:19
  44.2 2.0 %collective-permute-start.14 = (bf16[64,2048]{1,0:T(8,128)(2,1)S(1)}, bf16[64,2048]{1,0:T(8,128)(2,1)S(1)}, u32[]{:S(2)}, u32[]{:S(2)}) collective-permute-start(bf16[64,2048]{1,0:T(8,128)(2,1)S(1)} %collective-permute-done.7.refs_9_), channel_id=1, source_target_pairs={{0,16},{16,32},{32,48},{48,64},{64,80},{80,96},{96,112},{112,0},{1... | collective-permute-start | bytes 786440 | tf_op jit(solution)/shard_map/ppermute | solution.py:19
  46.2 0.8 collective-permute-done.13.refs_2_
  47.0 3.6 %collective-permute-start.16 = (bf16[64,2048]{1,0:T(8,128)(2,1)}, bf16[64,2048]{1,0:T(8,128)(2,1)S(1)}, u32[]{:S(2)}, u32[]{:S(2)}) collective-permute-start(bf16[64,2048]{1,0:T(8,128)(2,1)} %collective-permute-done.12.refs_1_), channel_id=1, source_target_pairs={{0,112},{16,0},{32,16},{48,32},{64,48},{80,64},{96,80},{112,96},{1... | collective-permute-start | bytes 786440 | tf_op jit(solution)/shard_map/ppermute | solution.py:19
  50.6 0.6 shard_map.105.refs_11_.refs_7_
  51.3 0.9 copy-done.3
  52.2 0.9 copy-done.4
  53.2 2.2 %shard_map.106 = (bf16[640,128]{1,0:T(8,128)(2,1)S(1)}, bf16[640,256]{1,0:T(8,128)(2,1)S(1)}) custom-call(f32[1,1]{1,0:T(1,128)} %constant_dynamic-slice_fusion.temp_ref, bf16[64,2048]{1,0:T(8,128)(2,1)S(1)} %copy-done.3, bf16[64,2048]{1,0:T(8,128)(2,1)S(1)} %copy-done.4, bf16[64,2048]{1,0:T(8,128)(2,1)S(1)} %collective-permute-done.refs_2_, ...), custom_call_target="tpu_custom_call" | custom-call | flops 1006632960 | bytes 5177344 | tf_op jit(solution)/shard_map/pallas_call | solution.py:117
  55.4 0.7 copy-done.5
  56.1 2.2 %collective-permute-start.18 = (bf16[640,256]{1,0:T(8,128)(2,1)S(1)}, bf16[640,256]{1,0:T(8,128)(2,1)S(1)}, u32[]{:S(2)}, u32[]{:S(2)}) collective-permute-start(bf16[640,256]{1,0:T(8,128)(2,1)S(1)} %get-tuple-element.15.refs_0_), channel_id=1, source_target_pairs={{0,128},{128,0},{1,129},{129,1},{2,130},{130,2},{3,131},{131,3},{4... | collective-permute-start | bytes 983048 | tf_op jit(solution)/shard_map/ppermute | solution.py:19
  58.3 0.2 convert_reduce_fusion
  58.5 0.1 collective-permute-done.15.refs_4_
  58.6 2.7 %shard_map.107 = (bf16[384,128]{1,0:T(8,128)(2,1)S(1)}, bf16[384,256]{1,0:T(8,128)(2,1)S(1)}) custom-call(f32[1,1]{1,0:T(1,128)} %constant_dynamic-slice_fusion.temp_ref, bf16[64,2048]{1,0:T(8,128)(2,1)S(1)} %collective-permute-done.11.refs_0_, bf16[64,2048]{1,0:T(8,128)(2,1)} %collective-permute-done.12.refs_1_, ...), custom_call_target="tpu_custom_call" | custom-call | flops 603979776 | bytes 3735552 | tf_op jit(solution)/shard_map/pallas_call | solution.py:117
  61.3 3.1 %collective-permute-start.21 = (bf16[384,256]{1,0:T(8,128)(2,1)S(1)}, bf16[384,256]{1,0:T(8,128)(2,1)S(1)}, u32[]{:S(2)}, u32[]{:S(2)}) collective-permute-start(bf16[384,256]{1,0:T(8,128)(2,1)S(1)} %get-tuple-element.16.refs_4_), channel_id=1, source_target_pairs={{0,128},{128,0},{1,129},{129,1},{2,130},{130,2},{3,131},{131,3},{4... | collective-permute-start | bytes 589832 | tf_op jit(solution)/shard_map/ppermute | solution.py:19
  64.4 0.1 select_reduce_fusion
  64.5 0.1 collective-permute-start.17
  64.6 0.1 collective-permute-done.18.refs_2_
  64.7 0.4 collective-permute-start.19
  65.1 0.2 copy.23
  65.3 0.2 copy.20
  65.5 0.2 collective-permute-start.20
  65.8 3.3 %collective-permute-done.21.refs_6_ = bf16[384,256]{1,0:T(8,128)(2,1)S(1)} collective-permute-done((bf16[384,256]{1,0:T(8,128)(2,1)S(1)}, bf16[384,256]{1,0:T(8,128)(2,1)S(1)}, u32[]{:S(2)}, u32[]{:S(2)}) %collective-permute-start.21) | collective-permute-done | bytes 196640 | tf_op jit(solution)/shard_map/ppermute | solution.py:19
  69.1 0.1 subtract_add_fusion
  69.2 1.3 %collective-permute-done.22.refs_7_ = bf16[384,256]{1,0:T(8,128)(2,1)S(1)} collective-permute-done((bf16[384,256]{1,0:T(8,128)(2,1)S(1)}, bf16[384,256]{1,0:T(8,128)(2,1)S(1)}, u32[]{:S(2)}, u32[]{:S(2)}) %collective-permute-start.22) | collective-permute-done | bytes 196640 | tf_op jit(solution)/shard_map/ppermute | solution.py:19
  70.6 8.9 %shard_map.108 = bf16[1024,128]{1,0:T(8,128)(2,1)S(1)} custom-call(s32[2,8]{1,0:T(2,128)S(1)} %pad_add_fusion.at_ref, bf16[640,128]{1,0:T(8,128)(2,1)S(1)} %copy-done.6, bf16[384,128]{1,0:T(8,128)(2,1)S(1)} %get-tuple-element.14.qb, bf16[640,256]{1,0:T(8,128)(2,1)S(1)} %get-tuple-element.15.refs_0_, bf16[640,256]{1,0:T(8,128)(2,1)S(1)} %collective-permute-done.17.refs_1_, ...), custom_call_target="tpu_custom_call" | custom-call | flops 21474836480 | bytes 2097152 | tf_op jit(solution)/shard_map/pallas_call | solution.py:210
  79.4 14.9 %all_to_all.10.m_ref = bf16[8,128,128]{2,1,0:T(8,128)(2,1)S(1)} all-to-all(bf16[8,128,128]{2,1,0:T(8,128)(2,1)S(1)} %bitcast.27), channel_id=1, replica_groups=mesh['yh'=2,'z'=8,'c'=2,'yl'=2,'x'=4] {'z'}, dimensions={0} | all-to-all | bytes 524288 | tf_op jit(solution)/shard_map/all_to_all | solution.py:300
  94.3 1.6 %shard_map.109 = bf16[128,2048]{1,0:T(8,128)(2,1)} custom-call(bf16[8,128,128]{2,1,0:T(8,128)(2,1)S(1)} %all_to_all.10.m_ref, bf16[1024,2048]{1,0:T(8,128)(2,1)S(1)} %bitcast.24, bf16[128,2048]{1,0:T(8,128)(2,1)S(1)} %bitcast.26), custom_call_target="tpu_custom_call" | custom-call | flops 536870912 | bytes 6291456 | tf_op jit(solution)/shard_map/pallas_call | solution.py:238
  95.9 3.4 %collective-permute-start.23 = (bf16[128,2048]{1,0:T(8,128)(2,1)}, bf16[128,2048]{1,0:T(8,128)(2,1)S(1)}, u32[]{:S(2)}, u32[]{:S(2)}) collective-permute-start(bf16[128,2048]{1,0:T(8,128)(2,1)} %shard_map.109), channel_id=1, source_target_pairs={{0,1},{1,2},{2,3},{3,4},{4,5},{5,6},{6,7},{8,9},{9,10},{10,11},{11... | collective-permute-start | bytes 1572872 | tf_op jit(solution)/shard_map/ppermute | solution.py:25
  99.3 14.6 %collective-permute-done.23 = bf16[128,2048]{1,0:T(8,128)(2,1)S(1)} collective-permute-done((bf16[128,2048]{1,0:T(8,128)(2,1)}, bf16[128,2048]{1,0:T(8,128)(2,1)S(1)}, u32[]{:S(2)}, u32[]{:S(2)}) %collective-permute-start.23) | collective-permute-done | bytes 524320 | tf_op jit(solution)/shard_map/ppermute | solution.py:25
  113.8 0.8 copy.30
  (46 shorter events, 0.2 us)
Async XLA Ops:
  0.6 40.5 %copy-start = (f32[1,8]{1,0:T(1,128)S(1)}, f32[1,8]{1,0:T(1,128)}, u32[]{:S(2)}) copy-start(f32[1,8]{1,0:T(1,128)} %param.16) | copy-start | bytes 100
  2.8 55.5 %copy-start.7 = (s32[4096]{0:T(1024)S(1)}, s32[4096]{0:T(1024)}, u32[]{:S(2)}) copy-start(s32[4096]{0:T(1024)} %param.11) | copy-start | bytes 49156
  2.8 14.5 %collective-permute-start = (bf16[64,2048]{1,0:T(8,128)(2,1)}, bf16[64,2048]{1,0:T(8,128)(2,1)S(1)}, u32[]{:S(2)}, u32[]{:S(2)}) collective-permute-start(bf16[64,2048]{1,0:T(8,128)(2,1)} %get-tuple-element.10.refs_0_), channel_id=1, source_target_pairs={{0,112},{16,0},{32,16},{48,32},{64,48},{80,64},{96,80},{112,96},{1... | collective-permute-start | bytes 786440 | tf_op jit(solution)/shard_map/ppermute | solution.py:19
  8.8 19.4 %collective-permute-start.2 = (bf16[64,2048]{1,0:T(8,128)(2,1)}, bf16[64,2048]{1,0:T(8,128)(2,1)S(1)}, u32[]{:S(2)}, u32[]{:S(2)}) collective-permute-start(bf16[64,2048]{1,0:T(8,128)(2,1)} %get-tuple-element.10.refs_0_), channel_id=1, source_target_pairs={{0,16},{16,32},{32,48},{48,64},{64,80},{80,96},{96,112},{112,0},{1... | collective-permute-start | bytes 786440 | tf_op jit(solution)/shard_map/ppermute | solution.py:19
  8.8 15.7 %collective-permute-start.1 = (bf16[64,2048]{1,0:T(8,128)(2,1)}, bf16[64,2048]{1,0:T(8,128)(2,1)S(1)}, u32[]{:S(2)}, u32[]{:S(2)}) collective-permute-start(bf16[64,2048]{1,0:T(8,128)(2,1)} %get-tuple-element.11.refs_1_), channel_id=1, source_target_pairs={{0,112},{16,0},{32,16},{48,32},{64,48},{80,64},{96,80},{112,96},{1... | collective-permute-start | bytes 786440 | tf_op jit(solution)/shard_map/ppermute | solution.py:19
  12.0 21.7 %collective-permute-start.3 = (bf16[64,2048]{1,0:T(8,128)(2,1)}, bf16[64,2048]{1,0:T(8,128)(2,1)S(1)}, u32[]{:S(2)}, u32[]{:S(2)}) collective-permute-start(bf16[64,2048]{1,0:T(8,128)(2,1)} %get-tuple-element.11.refs_1_), channel_id=1, source_target_pairs={{0,16},{16,32},{32,48},{48,64},{64,80},{80,96},{96,112},{112,0},{1... | collective-permute-start | bytes 786440 | tf_op jit(solution)/shard_map/ppermute | solution.py:19
  12.0 18.8 %all-to-all-start = ((bf16[8,64,256]{2,1,0:T(8,128)(2,1)}), bf16[8,64,256]{2,1,0:T(8,128)(2,1)S(1)}, u32[]{:S(2)}, u32[]{:S(2)}) async-start(bf16[8,64,256]{2,1,0:T(8,128)(2,1)} %get-tuple-element.12), calls=%async_computation | async-start | bytes 524288 | tf_op jit(solution)/shard_map/all_to_all | solution.py:269
  17.4 16.5 %collective-permute-start.4 = (bf16[64,2048]{1,0:T(8,128)(2,1)S(1)}, bf16[64,2048]{1,0:T(8,128)(2,1)S(1)}, u32[]{:S(2)}, u32[]{:S(2)}) collective-permute-start(bf16[64,2048]{1,0:T(8,128)(2,1)S(1)} %collective-permute-done.refs_2_), channel_id=1, source_target_pairs={{0,112},{16,0},{32,16},{48,32},{64,48},{80,64},{96,80},{112,96},{1... | collective-permute-start | bytes 786440 | tf_op jit(solution)/shard_map/ppermute | solution.py:19
  24.4 13.4 %collective-permute-start.5 = (bf16[64,2048]{1,0:T(8,128)(2,1)S(1)}, bf16[64,2048]{1,0:T(8,128)(2,1)S(1)}, u32[]{:S(2)}, u32[]{:S(2)}) collective-permute-start(bf16[64,2048]{1,0:T(8,128)(2,1)S(1)} %collective-permute-done.1.refs_3_), channel_id=1, source_target_pairs={{0,112},{16,0},{32,16},{48,32},{64,48},{80,64},{96,80},{112,96},{1... | collective-permute-start | bytes 786440 | tf_op jit(solution)/shard_map/ppermute | solution.py:19
  28.2 9.7 %collective-permute-start.6 = (bf16[64,2048]{1,0:T(8,128)(2,1)S(1)}, bf16[64,2048]{1,0:T(8,128)(2,1)S(1)}, u32[]{:S(2)}, u32[]{:S(2)}) collective-permute-start(bf16[64,2048]{1,0:T(8,128)(2,1)S(1)} %collective-permute-done.2.refs_4_), channel_id=1, source_target_pairs={{0,16},{16,32},{32,48},{48,64},{64,80},{80,96},{96,112},{112,0},{1... | collective-permute-start | bytes 786440 | tf_op jit(solution)/shard_map/ppermute | solution.py:19
  30.8 10.3 %collective-permute-start.9 = (bf16[8,64,256]{2,1,0:T(8,128)(2,1)S(1)}, bf16[8,64,256]{2,1,0:T(8,128)(2,1)S(1)}, u32[]{:S(2)}, u32[]{:S(2)}) collective-permute-start(bf16[8,64,256]{2,1,0:T(8,128)(2,1)S(1)} %all-to-all-done.own), channel_id=1, source_target_pairs={{0,128},{128,0},{1,129},{129,1},{2,130},{130,2},{3,131},{131,3},{4... | collective-permute-start | bytes 786440 | tf_op jit(solution)/shard_map/ppermute | solution.py:19
  33.7 10.4 %collective-permute-start.7 = (bf16[64,2048]{1,0:T(8,128)(2,1)S(1)}, bf16[64,2048]{1,0:T(8,128)(2,1)S(1)}, u32[]{:S(2)}, u32[]{:S(2)}) collective-permute-start(bf16[64,2048]{1,0:T(8,128)(2,1)S(1)} %collective-permute-done.3.refs_5_), channel_id=1, source_target_pairs={{0,16},{16,32},{32,48},{48,64},{64,80},{80,96},{96,112},{112,0},{1... | collective-permute-start | bytes 786440 | tf_op jit(solution)/shard_map/ppermute | solution.py:19
  33.9 10.3 %collective-permute-start.8 = (bf16[8,64,256]{2,1,0:T(8,128)(2,1)S(1)}, bf16[8,64,256]{2,1,0:T(8,128)(2,1)S(1)}, u32[]{:S(2)}, u32[]{:S(2)}) collective-permute-start(bf16[8,64,256]{2,1,0:T(8,128)(2,1)S(1)} %all-to-all-done.own), channel_id=1, source_target_pairs={{0,8},{8,0},{1,9},{9,1},{2,10},{10,2},{3,11},{11,3},{4,12},{12,4},... | collective-permute-start | bytes 786440 | tf_op jit(solution)/shard_map/ppermute | solution.py:19
  37.8 9.1 %collective-permute-start.13 = (bf16[64,2048]{1,0:T(8,128)(2,1)S(1)}, bf16[64,2048]{1,0:T(8,128)(2,1)S(1)}, u32[]{:S(2)}, u32[]{:S(2)}) collective-permute-start(bf16[64,2048]{1,0:T(8,128)(2,1)S(1)} %collective-permute-done.6.refs_8_), channel_id=1, source_target_pairs={{0,16},{16,32},{32,48},{48,64},{64,80},{80,96},{96,112},{112,0},{1... | collective-permute-start | bytes 786440 | tf_op jit(solution)/shard_map/ppermute | solution.py:19
  37.8 9.1 %collective-permute-start.12 = (bf16[64,2048]{1,0:T(8,128)(2,1)S(1)}, bf16[64,2048]{1,0:T(8,128)(2,1)}, u32[]{:S(2)}, u32[]{:S(2)}) collective-permute-start(bf16[64,2048]{1,0:T(8,128)(2,1)S(1)} %collective-permute-done.5.refs_7_), channel_id=1, source_target_pairs={{0,112},{16,0},{32,16},{48,32},{64,48},{80,64},{96,80},{112,96},{1... | collective-permute-start | bytes 786440 | tf_op jit(solution)/shard_map/ppermute | solution.py:19
  41.1 9.5 %collective-permute-start.10 = (bf16[8,64,256]{2,1,0:T(8,128)(2,1)S(1)}, bf16[8,64,256]{2,1,0:T(8,128)(2,1)S(1)}, u32[]{:S(2)}, u32[]{:S(2)}) collective-permute-start(bf16[8,64,256]{2,1,0:T(8,128)(2,1)S(1)} %collective-permute-done.9.over), channel_id=1, source_target_pairs={{0,8},{8,0},{1,9},{9,1},{2,10},{10,2},{3,11},{11,3},{4,12},{12,4},... | collective-permute-start | bytes 786440 | tf_op jit(solution)/shard_map/ppermute | solution.py:19
  44.2 14.3 %collective-permute-start.11 = (bf16[64,2048]{1,0:T(8,128)(2,1)S(1)}, bf16[64,2048]{1,0:T(8,128)(2,1)S(1)}, u32[]{:S(2)}, u32[]{:S(2)}) collective-permute-start(bf16[64,2048]{1,0:T(8,128)(2,1)S(1)} %collective-permute-done.4.refs_6_), channel_id=1, source_target_pairs={{0,112},{16,0},{32,16},{48,32},{64,48},{80,64},{96,80},{112,96},{1... | collective-permute-start | bytes 786440 | tf_op jit(solution)/shard_map/ppermute | solution.py:19
  44.2 14.3 %collective-permute-start.14 = (bf16[64,2048]{1,0:T(8,128)(2,1)S(1)}, bf16[64,2048]{1,0:T(8,128)(2,1)S(1)}, u32[]{:S(2)}, u32[]{:S(2)}) collective-permute-start(bf16[64,2048]{1,0:T(8,128)(2,1)S(1)} %collective-permute-done.7.refs_9_), channel_id=1, source_target_pairs={{0,16},{16,32},{32,48},{48,64},{64,80},{80,96},{96,112},{112,0},{1... | collective-permute-start | bytes 786440 | tf_op jit(solution)/shard_map/ppermute | solution.py:19
  47.0 11.7 %collective-permute-start.15 = (bf16[64,2048]{1,0:T(8,128)(2,1)S(1)}, bf16[64,2048]{1,0:T(8,128)(2,1)S(1)}, u32[]{:S(2)}, u32[]{:S(2)}) collective-permute-start(bf16[64,2048]{1,0:T(8,128)(2,1)S(1)} %collective-permute-done.13.refs_2_), channel_id=1, source_target_pairs={{0,16},{16,32},{32,48},{48,64},{64,80},{80,96},{96,112},{112,0},{1... | collective-permute-start | bytes 786440 | tf_op jit(solution)/shard_map/ppermute | solution.py:19
  47.0 11.6 %collective-permute-start.16 = (bf16[64,2048]{1,0:T(8,128)(2,1)}, bf16[64,2048]{1,0:T(8,128)(2,1)S(1)}, u32[]{:S(2)}, u32[]{:S(2)}) collective-permute-start(bf16[64,2048]{1,0:T(8,128)(2,1)} %collective-permute-done.12.refs_1_), channel_id=1, source_target_pairs={{0,112},{16,0},{32,16},{48,32},{64,48},{80,64},{96,80},{112,96},{1... | collective-permute-start | bytes 786440 | tf_op jit(solution)/shard_map/ppermute | solution.py:19
  51.3 1.0 copy-start.3
  52.2 0.9 copy-start.4
  53.2 11.9 %copy-start.8 = (s32[1,8]{1,0:T(1,128)S(1)}, s32[1,8]{1,0:T(1,128)}, u32[]{:S(2)}) copy-start(s32[1,8]{1,0:T(1,128)} %constant.43) | copy-start | bytes 100
  55.4 0.7 copy-start.5
  56.1 14.5 %copy-start.6 = (bf16[640,128]{1,0:T(8,128)(2,1)S(1)}, bf16[640,128]{1,0:T(8,128)(2,1)}, u32[]{:S(2)}) copy-start(bf16[640,128]{1,0:T(8,128)(2,1)} %copy-done.5) | copy-start | bytes 491524
  56.1 8.6 %collective-permute-start.18 = (bf16[640,256]{1,0:T(8,128)(2,1)S(1)}, bf16[640,256]{1,0:T(8,128)(2,1)S(1)}, u32[]{:S(2)}, u32[]{:S(2)}) collective-permute-start(bf16[640,256]{1,0:T(8,128)(2,1)S(1)} %get-tuple-element.15.refs_0_), channel_id=1, source_target_pairs={{0,128},{128,0},{1,129},{129,1},{2,130},{130,2},{3,131},{131,3},{4... | collective-permute-start | bytes 983048 | tf_op jit(solution)/shard_map/ppermute | solution.py:19
  61.3 7.8 %collective-permute-start.21 = (bf16[384,256]{1,0:T(8,128)(2,1)S(1)}, bf16[384,256]{1,0:T(8,128)(2,1)S(1)}, u32[]{:S(2)}, u32[]{:S(2)}) collective-permute-start(bf16[384,256]{1,0:T(8,128)(2,1)S(1)} %get-tuple-element.16.refs_4_), channel_id=1, source_target_pairs={{0,128},{128,0},{1,129},{129,1},{2,130},{130,2},{3,131},{131,3},{4... | collective-permute-start | bytes 589832 | tf_op jit(solution)/shard_map/ppermute | solution.py:19
  64.5 4.7 %collective-permute-start.17 = (bf16[640,256]{1,0:T(8,128)(2,1)S(1)}, bf16[640,256]{1,0:T(8,128)(2,1)S(1)}, u32[]{:S(2)}, u32[]{:S(2)}) collective-permute-start(bf16[640,256]{1,0:T(8,128)(2,1)S(1)} %get-tuple-element.15.refs_0_), channel_id=1, source_target_pairs={{0,8},{8,0},{1,9},{9,1},{2,10},{10,2},{3,11},{11,3},{4,12},{12,4},... | collective-permute-start | bytes 983048 | tf_op jit(solution)/shard_map/ppermute | solution.py:19
  64.7 5.9 %collective-permute-start.19 = (bf16[640,256]{1,0:T(8,128)(2,1)S(1)}, bf16[640,256]{1,0:T(8,128)(2,1)S(1)}, u32[]{:S(2)}, u32[]{:S(2)}) collective-permute-start(bf16[640,256]{1,0:T(8,128)(2,1)S(1)} %collective-permute-done.18.refs_2_), channel_id=1, source_target_pairs={{0,8},{8,0},{1,9},{9,1},{2,10},{10,2},{3,11},{11,3},{4,12},{12,4},... | collective-permute-start | bytes 983048 | tf_op jit(solution)/shard_map/ppermute | solution.py:19
  65.5 3.6 %collective-permute-start.20 = (bf16[384,256]{1,0:T(8,128)(2,1)S(1)}, bf16[384,256]{1,0:T(8,128)(2,1)S(1)}, u32[]{:S(2)}, u32[]{:S(2)}) collective-permute-start(bf16[384,256]{1,0:T(8,128)(2,1)S(1)} %get-tuple-element.16.refs_4_), channel_id=1, source_target_pairs={{0,8},{8,0},{1,9},{9,1},{2,10},{10,2},{3,11},{11,3},{4,12},{12,4},... | collective-permute-start | bytes 589832 | tf_op jit(solution)/shard_map/ppermute | solution.py:19
  69.1 1.4 %collective-permute-start.22 = (bf16[384,256]{1,0:T(8,128)(2,1)S(1)}, bf16[384,256]{1,0:T(8,128)(2,1)S(1)}, u32[]{:S(2)}, u32[]{:S(2)}) collective-permute-start(bf16[384,256]{1,0:T(8,128)(2,1)S(1)} %collective-permute-done.21.refs_6_), channel_id=1, source_target_pairs={{0,8},{8,0},{1,9},{9,1},{2,10},{10,2},{3,11},{11,3},{4,12},{12,4},... | collective-permute-start | bytes 589832 | tf_op jit(solution)/shard_map/ppermute | solution.py:19
  70.5 23.8 %copy-start.1 = (bf16[1,1024,2048]{2,1,0:T(8,128)(2,1)S(1)}, bf16[1,1024,2048]{2,1,0:T(8,128)(2,1)}, u32[]{:S(2)}) copy-start(bf16[1,1024,2048]{2,1,0:T(8,128)(2,1)} %param.15) | copy-start | bytes 12582916
  70.6 23.8 %copy-start.2 = (bf16[1,128,2048]{2,1,0:T(8,128)(2,1)S(1)}, bf16[1,128,2048]{2,1,0:T(8,128)(2,1)}, u32[]{:S(2)}) copy-start(bf16[1,128,2048]{2,1,0:T(8,128)(2,1)} %param.9) | copy-start | bytes 1572868
  95.9 18.0 %collective-permute-start.23 = (bf16[128,2048]{1,0:T(8,128)(2,1)}, bf16[128,2048]{1,0:T(8,128)(2,1)S(1)}, u32[]{:S(2)}, u32[]{:S(2)}) collective-permute-start(bf16[128,2048]{1,0:T(8,128)(2,1)} %shard_map.109), channel_id=1, source_target_pairs={{0,1},{1,2},{2,3},{3,4},{4,5},{5,6},{6,7},{8,9},{9,10},{10,11},{11... | collective-permute-start | bytes 1572872 | tf_op jit(solution)/shard_map/ppermute | solution.py:25

commit v6 on v5

--- a/solution.py
+++ b/solution.py
@@ -162,67 +162,91 @@
     return rows, jnp.concatenate(qpos, axis=0), jnp.concatenate(qspan, axis=0)
 
 
-def attend_kernel(at_ref, qa, qb, *refs):
-    parts, (qpos_ref, qspan_ref, kpos_ref, o_ref, q_all, k_all, v_all, s_all) = refs[:8], refs[8:]
-    early, late = qa.shape[0], qb.shape[0]
-    own_rows, head_dim = q_all.shape
-    q_all[pl.ds(0, early), :] = qa[...]
-    q_all[pl.ds(early, late), :] = qb[...]
-    for i in range(4):
-        for part, rows in (
-            (parts[i], pl.ds(i * own_rows, early)),
-            (parts[4 + i], pl.ds(i * own_rows + early, late)),
-        ):
+def laid_out(parts, k_all, v_all):
+    head_dim, start = k_all.shape[1], 0
+    for early, late in parts:
+        for part in (early, late):
+            rows = pl.ds(start, part.shape[0])
             k_all[rows, :] = part[:, :head_dim]
             v_all[rows, :] = part[:, head_dim:]
+            start += part.shape[0]
+
+
+def weighed(q, peak, first, kpos_ref, qpos, qspan, k_all, v_all, s_all):
     offsets, wide = EARLY + LATE, 512
     cuts = [slice(start, start + wide) for start in range(0, k_all.shape[0], wide)]
+    for cut in cuts:
+        places = []
+        for start in range(cut.start, cut.stop, 128):
+            origin, block = divmod(start // 128, len(offsets))
+            origin, o = origin + first, offsets[block]
+            places.append(kpos_ref[origin : origin + 1, o * 128 : (o + 1) * 128])
+        peak = masked_scores(q, k_all[cut, :], places, qpos, qspan, s_all, cut.start, peak)
+    top = jnp.broadcast_to(jnp.max(peak, axis=-1, keepdims=True), peak.shape)
+    total = jnp.zeros((TILE, 128), jnp.float32)
+    mixed = jnp.zeros((TILE, q.shape[1]), jnp.float32)
+    for cut in cuts:
+        total, mixed = mixing(s_all, cut.start, v_all[cut, :], top, total, mixed)
+    return top, total, mixed
+
+
+def own_kernel(at_ref, qa, qb, early, late, qpos_ref, qspan_ref, kpos_ref, q_out, acc, top_out, total_out, k_all, v_all, s_all):
+    q_out[pl.ds(0, qa.shape[0]), :] = qa[...]
+    q_out[pl.ds(qa.shape[0], qb.shape[0]), :] = qb[...]
+    laid_out([(early, late)], k_all, v_all)
 
     def one_tile(t, _):
         rows, qpos, qspan = tile_of(t, at_ref, qpos_ref, qspan_ref)
-        q = q_all[rows, :]
         peak = jnp.full((TILE, 128), -1e30, jnp.float32)
-        for cut in cuts:
-            places = []
-            for start in range(cut.start, cut.stop, 128):
-                o = offsets[start % own_rows // 128]
-                origin = start // own_rows
-                places.append(kpos_ref[origin : origin + 1, o * 128 : (o + 1) * 128])
-            peak = masked_scores(q, k_all[cut, :], places, qpos, qspan, s_all, cut.start, peak)
-        top = jnp.broadcast_to(jnp.max(peak, axis=-1, keepdims=True), peak.shape)
-        total = jnp.zeros((TILE, 128), jnp.float32)
-        mixed = jnp.zeros((TILE, head_dim), jnp.float32)
-        for cut in cuts:
-            total, mixed = mixing(s_all, cut.start, v_all[cut, :], top, total, mixed)
-        result = (mixed / jnp.sum(total, axis=-1, keepdims=True)).astype(jnp.bfloat16)
+        top, total, mixed = weighed(q_out[rows, :], peak, 0, kpos_ref, qpos, qspan, k_all, v_all, s_all)
+        acc[rows, :] = mixed
+        total_out[rows, :] = total
+        top_out[rows, :] = top
+        return 0
+
+    lax.fori_loop(0, q_out.shape[0] // TILE, one_tile, 0)
+
+
+def others_kernel(at_ref, q_ref, acc, top_ref, total_ref, *refs):
+    parts, (qpos_ref, qspan_ref, kpos_ref, o_ref, k_all, v_all, s_all) = refs[:6], refs[6:]
+    laid_out(list(zip(parts[:3], parts[3:])), k_all, v_all)
+
+    def one_tile(t, _):
+        rows, qpos, qspan = tile_of(t, at_ref, qpos_ref, qspan_ref)
+        before = top_ref[rows, :]
+        top, total, mixed = weighed(
+            q_ref[rows, :], before, 1, kpos_ref, qpos, qspan, k_all, v_all, s_all
+        )
+        kept = jnp.exp(before - top)
+        weight = jnp.sum(total_ref[rows, :] * kept + total, axis=-1, keepdims=True)
+        result = ((acc[rows, :] * kept + mixed) / weight).astype(jnp.bfloat16)
         for i in range(TILE // 128):
             placed = pl.ds(pl.multiple_of(at_ref[1, t * (TILE // 128) + i] * 128, 128), 128)
             o_ref[placed, :] = result[i * 128 : (i + 1) * 128, :]
         return 0
 
-    lax.fori_loop(0, own_rows // TILE, one_tile, 0)
-
-
-def attended(at, queries, keyvals, qpos, qspan, kpos):
-    rows, head_dim = sum(q.shape[0] for q in queries), queries[0].shape[1]
-    keys = sum(k.shape[0] for k in keyvals)
+    lax.fori_loop(0, q_ref.shape[0] // TILE, one_tile, 0)
+
+
+def attended(kernel, out_shape, keys, at, *operands):
+    head_dim = 128
+    rows = operands[0].shape[0]
     vmem = pl.BlockSpec(memory_space=pltpu.VMEM)
     return pl.pallas_call(
-        attend_kernel,
-        in_specs=[pl.BlockSpec(memory_space=pltpu.SMEM)] + [vmem] * 13,
-        out_specs=vmem,
-        out_shape=jax.ShapeDtypeStruct((rows, head_dim), jnp.bfloat16),
+        kernel,
+        in_specs=[pl.BlockSpec(memory_space=pltpu.SMEM)] + [vmem] * len(operands),
+        out_specs=[vmem] * len(out_shape),
+        out_shape=out_shape,
         scratch_shapes=[
-            pltpu.VMEM((rows, head_dim), jnp.bfloat16),
             pltpu.VMEM((keys, head_dim), jnp.bfloat16),
             pltpu.VMEM((keys, head_dim), jnp.bfloat16),
             pltpu.VMEM((TILE, keys), jnp.float32),
         ],
-        compiler_params=params(24),
+        compiler_params=params(16),
         cost_estimate=pl.CostEstimate(
-            flops=40 * rows * keys * head_dim, bytes_accessed=4 * keys * head_dim, transcendentals=rows * keys
+            flops=24 * rows * keys * head_dim, bytes_accessed=4 * keys * head_dim, transcendentals=rows * keys
         ),
-    )(at, *queries, *keyvals, qpos, qspan, kpos)
+    )(at, *operands)
 
 
 def output_kernel(m_ref, w_ref, x_ref, o_ref):
@@ -291,12 +315,17 @@
     over_early = shifted(kv_early, "yh", 1)
     _, over_later = lax.optimization_barrier((kv_late, over_early))
     over_late = shifted(kv_late, "yh", 1)
-    keyvals = [kv_early, shifted(kv_early, "c", 1), over_early, shifted(over_later, "c", 1)]
-    keyvals += [kv_late, shifted(kv_late, "c", 1), over_late, shifted(over_late, "c", 1)]
     offsets = jnp.array(EARLY + LATE, jnp.int32)
     at = jnp.stack([offsets, lax.rem(z + offsets, ZS)])
-    mixed = attended(at, [q_early, q_late], keyvals, qpos, qspan, kpos)
-
+    rows = q_early.shape[0] + q_late.shape[0]
+    narrow = jax.ShapeDtypeStruct((rows, head_dim), jnp.bfloat16)
+    wide = jax.ShapeDtypeStruct((rows, head_dim), jnp.float32)
+    where = (qpos, qspan, kpos)
+    state = attended(own_kernel, [narrow] + [wide] * 3, rows, at, q_early, q_late, kv_early, kv_late, *where)
+    _, over_last = lax.optimization_barrier((state[0], over_late))
+    others = [shifted(kv_early, "c", 1), over_early, shifted(over_later, "c", 1)]
+    others += [shifted(kv_late, "c", 1), over_late, shifted(over_last, "c", 1)]
+    (mixed,) = attended(others_kernel, [narrow], 3 * rows, at, *state, *others, *where)
     mixed = lax.all_to_all(mixed.reshape(ZS, -1, head_dim), "z", 0, 0, tiled=True)
     produced = outputs(mixed, w_out[0], inputs)
     handed = passed_along(produced, ("yl", "x"), 1)

time: 116 us -> 117 us (level); the launches traced: 115 us -> 117 us
  waiting for transfers between devices: 31.8 us -> 35.1 us
  starting transfers between devices: 41.4 us -> 39.6 us
  local copies, waits for them, and re-layouts: 5.61 us -> 3.82 us
  Pallas kernels: 18.1 us -> 19.4 us
    ppermute x23, waiting for transfers between devices: 14.7 us -> 17.9 us  [shifted(): lax.ppermute(block, axis, [(i, (i + distance) % count) for i in range(cou...]
    unnamed x20 -> x16, local copies, waits for them, and re-layouts: 3.39 us -> 0.84 us
    pallas_call x1 -> x2, Pallas kernels: 8.87 us -> 11.1 us  [attended(): pl.pallas_call(kernel, in_specs=[pl.BlockSpec(memory_space=pltpu.SMEM)] +...]
    ppermute x23, starting transfers between devices: 33.5 us -> 31.7 us  [shifted(): lax.ppermute(block, axis, [(i, (i + distance) % count) for i in range(cou...]
  transfers between devices with their start and end apart: 25 -> 25, of which waited for: 10 -> 8; matrix products, arithmetic and copies ran while one was open for 4% -> 5% of each run, Pallas kernels for 5% -> 7%
where the time goes in v6:
time: 117 us
  starting transfers between devices  39.6 us (34%)
  waiting for transfers between devices  35.1 us (30%)
  Pallas kernels  19.4 us (17%)
  blocking collectives  15.1 us (13%)
  local copies, waits for them, and re-layouts  3.82 us (3%)
  other arithmetic  3 us (3%)
    ppermute x23, starting transfers between devices, shifted(): lax.ppermute(block, axis, [(i, (i + distance) % count) for i in range(cou...  31.7 us
    ppermute x23, waiting for transfers between devices, shifted(): lax.ppermute(block, axis, [(i, (i + distance) % count) for i in range(cou...  17.9 us
    all_to_all x1, blocking collectives, per_device(): lax.all_to_all(mixed.reshape(ZS, -1, head_dim), 'z', 0, 0, tiled=True)  15.1 us
    ppermute x1, waiting for transfers between devices, passed_along(): return lax.ppermute(block, axis, route)  14.7 us
    pallas_call x2, Pallas kernels, attended(): pl.pallas_call(kernel, in_specs=[pl.BlockSpec(memory_space=pltpu.SMEM)] +...  11.1 us
    all_to_all x1, starting transfers between devices, per_device(): own_w = lax.all_to_all(by_head, 'z', 0, 0, tiled=True)  4.51 us
    pallas_call x2, Pallas kernels, projected(): pl.pallas_call(functools.partial(project_kernel, len(blocks)), in_specs=[...  3.94 us
    ppermute x1, starting transfers between devices, passed_along(): return lax.ppermute(block, axis, route)  3.38 us
  transfers between devices with their start and end apart: 25, of which 8 were waited for; matrix products, arithmetic and copies ran while one was open for 5% of the time, Pallas kernels for 7%

profile of v6, /device:TPU:8, one launch (start us, length us, event | category | flops | bytes accessed | tf_op | source)
XLA Modules:
  0.0 116.9 jit_solution(16925490713460384933)
XLA Ops:
  0.6 0.0 copy-start
  0.6 2.2 %shard_map.104 = (bf16[64,2048]{1,0:T(8,128)(2,1)}, bf16[64,2048]{1,0:T(8,128)(2,1)}, bf16[8,64,256]{2,1,0:T(8,128)(2,1)}) custom-call(bf16[128,2048]{1,0:T(8,128)(2,1)} %bitcast.25, f32[1,2048]{1,0:T(1,128)} %g_any.1, bf16[64,2048]{1,0:T(8,128)(2,1)} %bitcast.33), custom_call_target="tpu_custom_call" | custom-call | bytes 1572864 | tf_op jit(solution)/shard_map/pallas_call | solution.py:58
  2.8 0.0 copy-start.3
  2.8 5.9 %collective-permute-start = (bf16[64,2048]{1,0:T(8,128)(2,1)}, bf16[64,2048]{1,0:T(8,128)(2,1)S(1)}, u32[]{:S(2)}, u32[]{:S(2)}) collective-permute-start(bf16[64,2048]{1,0:T(8,128)(2,1)} %get-tuple-element.15.refs_0_), channel_id=1, source_target_pairs={{0,112},{16,0},{32,16},{48,32},{64,48},{80,64},{96,80},{112,96},{1... | collective-permute-start | bytes 786440 | tf_op jit(solution)/shard_map/ppermute | solution.py:19
  8.8 3.2 %collective-permute-start.1 = (bf16[64,2048]{1,0:T(8,128)(2,1)}, bf16[64,2048]{1,0:T(8,128)(2,1)S(1)}, u32[]{:S(2)}, u32[]{:S(2)}) collective-permute-start(bf16[64,2048]{1,0:T(8,128)(2,1)} %get-tuple-element.16.refs_1_), channel_id=1, source_target_pairs={{0,112},{16,0},{32,16},{48,32},{64,48},{80,64},{96,80},{112,96},{1... | collective-permute-start | bytes 786440 | tf_op jit(solution)/shard_map/ppermute | solution.py:19
  12.0 4.5 %all-to-all-start = ((bf16[8,64,256]{2,1,0:T(8,128)(2,1)}), bf16[8,64,256]{2,1,0:T(8,128)(2,1)S(1)}, u32[]{:S(2)}, u32[]{:S(2)}) async-start(bf16[8,64,256]{2,1,0:T(8,128)(2,1)} %get-tuple-element.17), calls=%async_computation | async-start | bytes 524288 | tf_op jit(solution)/shard_map/all_to_all | solution.py:293
  16.5 0.7 fusion
  17.4 0.9 convert_reduce_fusion
  18.4 0.1 select_reduce_fusion
  18.5 3.3 %collective-permute-start.4 = (bf16[64,2048]{1,0:T(8,128)(2,1)S(1)}, bf16[64,2048]{1,0:T(8,128)(2,1)S(1)}, u32[]{:S(2)}, u32[]{:S(2)}) collective-permute-start(bf16[64,2048]{1,0:T(8,128)(2,1)S(1)} %collective-permute-done.refs_2_), channel_id=1, source_target_pairs={{0,112},{16,0},{32,16},{48,32},{64,48},{80,64},{96,80},{112,96},{1... | collective-permute-start | bytes 786440 | tf_op jit(solution)/shard_map/ppermute | solution.py:19
  21.8 2.7 %collective-permute-done.1.refs_3_ = bf16[64,2048]{1,0:T(8,128)(2,1)S(1)} collective-permute-done((bf16[64,2048]{1,0:T(8,128)(2,1)}, bf16[64,2048]{1,0:T(8,128)(2,1)S(1)}, u32[]{:S(2)}, u32[]{:S(2)}) %collective-permute-start.1) | collective-permute-done | bytes 262176 | tf_op jit(solution)/shard_map/ppermute | solution.py:19
  24.4 3.8 %collective-permute-start.5 = (bf16[64,2048]{1,0:T(8,128)(2,1)S(1)}, bf16[64,2048]{1,0:T(8,128)(2,1)S(1)}, u32[]{:S(2)}, u32[]{:S(2)}) collective-permute-start(bf16[64,2048]{1,0:T(8,128)(2,1)S(1)} %collective-permute-done.1.refs_3_), channel_id=1, source_target_pairs={{0,112},{16,0},{32,16},{48,32},{64,48},{80,64},{96,80},{112,96},{1... | collective-permute-start | bytes 786440 | tf_op jit(solution)/shard_map/ppermute | solution.py:19
  28.3 2.5 %all-to-all-done.own = bf16[8,64,256]{2,1,0:T(8,128)(2,1)S(1)} async-done(((bf16[8,64,256]{2,1,0:T(8,128)(2,1)}), bf16[8,64,256]{2,1,0:T(8,128)(2,1)S(1)}, u32[]{:S(2)}, u32[]{:S(2)}) %all-to-all-start) | async-done | bytes 262176 | tf_op jit(solution)/shard_map/all_to_all | solution.py:293
  30.8 2.3 %collective-permute-start.9 = (bf16[8,64,256]{2,1,0:T(8,128)(2,1)S(1)}, bf16[8,64,256]{2,1,0:T(8,128)(2,1)S(1)}, u32[]{:S(2)}, u32[]{:S(2)}) collective-permute-start(bf16[8,64,256]{2,1,0:T(8,128)(2,1)S(1)} %all-to-all-done.own), channel_id=1, source_target_pairs={{0,128},{128,0},{1,129},{129,1},{2,130},{130,2},{3,131},{131,3},{4... | collective-permute-start | bytes 786440 | tf_op jit(solution)/shard_map/ppermute | solution.py:19
  33.1 0.1 pad_add_fusion.1.at_ref
  33.1 0.2 copy.23
  33.4 1.0 copy.20
  34.4 0.6 constant_dynamic-slice_fusion.temp_ref
  35.0 1.1 dynamic-slice_bitcast_fusion.refs_10_.refs_6_
  36.1 0.0 copy-start.6
  36.1 0.1 collective-permute-start.7
  36.2 0.1 collective-permute-start.8
  36.3 0.8 collective-permute-start.13
  37.1 3.6 %collective-permute-start.12 = (bf16[64,2048]{1,0:T(8,128)(2,1)S(1)}, bf16[64,2048]{1,0:T(8,128)(2,1)S(1)}, u32[]{:S(2)}, u32[]{:S(2)}) collective-permute-start(bf16[64,2048]{1,0:T(8,128)(2,1)S(1)} %collective-permute-done.5.refs_7_), channel_id=1, source_target_pairs={{0,112},{16,0},{32,16},{48,32},{64,48},{80,64},{96,80},{112,96},{1... | collective-permute-start | bytes 786440 | tf_op jit(solution)/shard_map/ppermute | solution.py:19
  40.7 1.1 subtract_add_fusion
  41.9 4.6 %collective-permute-done.7.refs_9_ = bf16[64,2048]{1,0:T(8,128)(2,1)S(1)} collective-permute-done((bf16[64,2048]{1,0:T(8,128)(2,1)S(1)}, bf16[64,2048]{1,0:T(8,128)(2,1)S(1)}, u32[]{:S(2)}, u32[]{:S(2)}) %collective-permute-start.7) | collective-permute-done | bytes 262176 | tf_op jit(solution)/shard_map/ppermute | solution.py:19
  46.4 2.0 %collective-permute-start.14 = (bf16[64,2048]{1,0:T(8,128)(2,1)S(1)}, bf16[64,2048]{1,0:T(8,128)(2,1)S(1)}, u32[]{:S(2)}, u32[]{:S(2)}) collective-permute-start(bf16[64,2048]{1,0:T(8,128)(2,1)S(1)} %collective-permute-done.7.refs_9_), channel_id=1, source_target_pairs={{0,16},{16,32},{32,48},{48,64},{64,80},{80,96},{96,112},{112,0},{1... | collective-permute-start | bytes 786440 | tf_op jit(solution)/shard_map/ppermute | solution.py:19
  48.4 3.1 %collective-permute-done.13.refs_2_ = bf16[64,2048]{1,0:T(8,128)(2,1)S(1)} collective-permute-done((bf16[64,2048]{1,0:T(8,128)(2,1)S(1)}, bf16[64,2048]{1,0:T(8,128)(2,1)S(1)}, u32[]{:S(2)}, u32[]{:S(2)}) %collective-permute-start.13) | collective-permute-done | bytes 262176 | tf_op jit(solution)/shard_map/ppermute | solution.py:19
  51.6 3.2 %collective-permute-start.16 = (bf16[64,2048]{1,0:T(8,128)(2,1)S(1)}, bf16[64,2048]{1,0:T(8,128)(2,1)S(1)}, u32[]{:S(2)}, u32[]{:S(2)}) collective-permute-start(bf16[64,2048]{1,0:T(8,128)(2,1)S(1)} %collective-permute-done.12.refs_1_), channel_id=1, source_target_pairs={{0,112},{16,0},{32,16},{48,32},{64,48},{80,64},{96,80},{112,96},{1... | collective-permute-start | bytes 786440 | tf_op jit(solution)/shard_map/ppermute | solution.py:19
  54.8 0.6 shard_map.105.refs_11_.refs_7_
  55.5 0.0 copy-start.5
  55.5 2.2 %shard_map.106 = (bf16[640,128]{1,0:T(8,128)(2,1)S(1)}, bf16[640,256]{1,0:T(8,128)(2,1)S(1)}) custom-call(f32[1,1]{1,0:T(1,128)} %constant_dynamic-slice_fusion.temp_ref, bf16[64,2048]{1,0:T(8,128)(2,1)S(1)} %copy-done.3, bf16[64,2048]{1,0:T(8,128)(2,1)S(1)} %copy-done.4, bf16[64,2048]{1,0:T(8,128)(2,1)S(1)} %collective-permute-done.refs_2_, ...), custom_call_target="tpu_custom_call" | custom-call | flops 1006632960 | bytes 5177344 | tf_op jit(solution)/shard_map/pallas_call | solution.py:117
  57.8 0.7 collective-permute-start.18
  58.5 2.0 %collective-permute-done.15.refs_4_ = bf16[64,2048]{1,0:T(8,128)(2,1)S(1)} collective-permute-done((bf16[64,2048]{1,0:T(8,128)(2,1)S(1)}, bf16[64,2048]{1,0:T(8,128)(2,1)S(1)}, u32[]{:S(2)}, u32[]{:S(2)}) %collective-permute-start.15) | collective-permute-done | bytes 262176 | tf_op jit(solution)/shard_map/ppermute | solution.py:19
  60.5 1.7 %shard_map.107 = (bf16[384,128]{1,0:T(8,128)(2,1)S(1)}, bf16[384,256]{1,0:T(8,128)(2,1)S(1)}) custom-call(f32[1,1]{1,0:T(1,128)} %constant_dynamic-slice_fusion.temp_ref, bf16[64,2048]{1,0:T(8,128)(2,1)S(1)} %collective-permute-done.11.refs_0_, bf16[64,2048]{1,0:T(8,128)(2,1)S(1)} %collective-permute-done.12.refs_1_, ...), custom_call_target="tpu_custom_call" | custom-call | flops 603979776 | bytes 3735552 | tf_op jit(solution)/shard_map/pallas_call | solution.py:117
  62.2 1.3 %collective-permute-start.21 = (bf16[384,256]{1,0:T(8,128)(2,1)S(1)}, bf16[384,256]{1,0:T(8,128)(2,1)S(1)}, u32[]{:S(2)}, u32[]{:S(2)}) collective-permute-start(bf16[384,256]{1,0:T(8,128)(2,1)S(1)} %get-tuple-element.21.late), channel_id=1, source_target_pairs={{0,128},{128,0},{1,129},{129,1},{2,130},{130,2},{3,131},{131,3},{4... | collective-permute-start | bytes 589832 | tf_op jit(solution)/shard_map/ppermute | solution.py:19
  63.5 0.1 collective-permute-start.17
  63.6 0.5 collective-permute-start.20
  64.1 4.4 %collective-permute-done.18.refs_1_ = bf16[640,256]{1,0:T(8,128)(2,1)S(1)} collective-permute-done((bf16[640,256]{1,0:T(8,128)(2,1)S(1)}, bf16[640,256]{1,0:T(8,128)(2,1)S(1)}, u32[]{:S(2)}, u32[]{:S(2)}) %collective-permute-start.18) | collective-permute-done | bytes 327712 | tf_op jit(solution)/shard_map/ppermute | solution.py:19
  68.5 3.6 %shard_map.108 = (bf16[1024,128]{1,0:T(8,128)(2,1)S(1)}, f32[1024,128]{1,0:T(8,128)S(1)}, f32[1024,128]{1,0:T(8,128)S(1)}, f32[1024,128]{1,0:T(8,128)S(1)}) custom-call(s32[2,8]{1,0:T(2,128)S(1)} %pad_add_fusion.at_ref, bf16[640,128]{1,0:T(8,128)(2,1)S(1)} %get-tuple-element.18.qa, bf16[384,128]{1,0:T(8,128)(2,1)S(1)} %get-tuple-element.19.qb, ...), custom_call_target="tpu_custom_call" | custom-call | flops 2013265920 | bytes 524288 | tf_op jit(solution)/shard_map/pallas_call | solution.py:235
  72.1 0.6 collective-permute-start.22
  72.7 1.1 collective-permute-done.22.refs_5_
  73.8 7.6 %shard_map.109 = bf16[1024,128]{1,0:T(8,128)(2,1)S(1)} custom-call(s32[2,8]{1,0:T(2,128)S(1)} %pad_add_fusion.at_ref, bf16[1024,128]{1,0:T(8,128)(2,1)S(1)} %get-tuple-element.22.q_ref, f32[1024,128]{1,0:T(8,128)S(1)} %get-tuple-element.23.acc, f32[1024,128]{1,0:T(8,128)S(1)} %get-tuple-element.24.top_ref, f32[1024,128]{1,0:T(8,128)S(1)} %get-tuple-element.25.total_ref, ...), custom_call_target="tpu_custom_call" | custom-call | flops 9663676416 | bytes 1572864 | tf_op jit(solution)/shard_map/pallas_call | solution.py:235
  81.4 15.1 %all_to_all.10.m_ref = bf16[8,128,128]{2,1,0:T(8,128)(2,1)S(1)} all-to-all(bf16[8,128,128]{2,1,0:T(8,128)(2,1)S(1)} %bitcast.27), channel_id=1, replica_groups=mesh['yh'=2,'z'=8,'c'=2,'yl'=2,'x'=4] {'z'}, dimensions={0} | all-to-all | bytes 524288 | tf_op jit(solution)/shard_map/all_to_all | solution.py:329
  96.5 1.5 %shard_map.110 = bf16[128,2048]{1,0:T(8,128)(2,1)} custom-call(bf16[8,128,128]{2,1,0:T(8,128)(2,1)S(1)} %all_to_all.10.m_ref, bf16[1024,2048]{1,0:T(8,128)(2,1)S(1)} %bitcast.24, bf16[128,2048]{1,0:T(8,128)(2,1)S(1)} %bitcast.26), custom_call_target="tpu_custom_call" | custom-call | flops 536870912 | bytes 6291456 | tf_op jit(solution)/shard_map/pallas_call | solution.py:262
  98.0 3.4 %collective-permute-start.23 = (bf16[128,2048]{1,0:T(8,128)(2,1)}, bf16[128,2048]{1,0:T(8,128)(2,1)S(1)}, u32[]{:S(2)}, u32[]{:S(2)}) collective-permute-start(bf16[128,2048]{1,0:T(8,128)(2,1)} %shard_map.110), channel_id=1, source_target_pairs={{0,1},{1,2},{2,3},{3,4},{4,5},{5,6},{6,7},{8,9},{9,10},{10,11},{11... | collective-permute-start | bytes 1572872 | tf_op jit(solution)/shard_map/ppermute | solution.py:25
  101.4 14.7 %collective-permute-done.23 = bf16[128,2048]{1,0:T(8,128)(2,1)S(1)} collective-permute-done((bf16[128,2048]{1,0:T(8,128)(2,1)}, bf16[128,2048]{1,0:T(8,128)(2,1)S(1)}, u32[]{:S(2)}, u32[]{:S(2)}) %collective-permute-start.23) | collective-permute-done | bytes 524320 | tf_op jit(solution)/shard_map/ppermute | solution.py:25
  116.1 0.8 copy.30
  (43 shorter events, 0.2 us)
Async XLA Ops:
  0.6 33.8 %copy-start = (f32[1,8]{1,0:T(1,128)S(1)}, f32[1,8]{1,0:T(1,128)}, u32[]{:S(2)}) copy-start(f32[1,8]{1,0:T(1,128)} %param.16) | copy-start | bytes 100
  2.8 52.6 %copy-start.3 = (bf16[64,2048]{1,0:T(8,128)(2,1)S(1)}, bf16[64,2048]{1,0:T(8,128)(2,1)}, u32[]{:S(2)}) copy-start(bf16[64,2048]{1,0:T(8,128)(2,1)} %get-tuple-element.15.refs_0_) | copy-start | bytes 786436
  2.8 52.6 %copy-start.4 = (bf16[64,2048]{1,0:T(8,128)(2,1)S(1)}, bf16[64,2048]{1,0:T(8,128)(2,1)}, u32[]{:S(2)}) copy-start(bf16[64,2048]{1,0:T(8,128)(2,1)} %get-tuple-element.16.refs_1_) | copy-start | bytes 786436
  2.8 15.6 %collective-permute-start = (bf16[64,2048]{1,0:T(8,128)(2,1)}, bf16[64,2048]{1,0:T(8,128)(2,1)S(1)}, u32[]{:S(2)}, u32[]{:S(2)}) collective-permute-start(bf16[64,2048]{1,0:T(8,128)(2,1)} %get-tuple-element.15.refs_0_), channel_id=1, source_target_pairs={{0,112},{16,0},{32,16},{48,32},{64,48},{80,64},{96,80},{112,96},{1... | collective-permute-start | bytes 786440 | tf_op jit(solution)/shard_map/ppermute | solution.py:19
  8.8 19.5 %collective-permute-start.2 = (bf16[64,2048]{1,0:T(8,128)(2,1)}, bf16[64,2048]{1,0:T(8,128)(2,1)S(1)}, u32[]{:S(2)}, u32[]{:S(2)}) collective-permute-start(bf16[64,2048]{1,0:T(8,128)(2,1)} %get-tuple-element.15.refs_0_), channel_id=1, source_target_pairs={{0,16},{16,32},{32,48},{48,64},{64,80},{80,96},{96,112},{112,0},{1... | collective-permute-start | bytes 786440 | tf_op jit(solution)/shard_map/ppermute | solution.py:19
  8.8 15.7 %collective-permute-start.1 = (bf16[64,2048]{1,0:T(8,128)(2,1)}, bf16[64,2048]{1,0:T(8,128)(2,1)S(1)}, u32[]{:S(2)}, u32[]{:S(2)}) collective-permute-start(bf16[64,2048]{1,0:T(8,128)(2,1)} %get-tuple-element.16.refs_1_), channel_id=1, source_target_pairs={{0,112},{16,0},{32,16},{48,32},{64,48},{80,64},{96,80},{112,96},{1... | collective-permute-start | bytes 786440 | tf_op jit(solution)/shard_map/ppermute | solution.py:19
  12.0 24.1 %collective-permute-start.3 = (bf16[64,2048]{1,0:T(8,128)(2,1)}, bf16[64,2048]{1,0:T(8,128)(2,1)S(1)}, u32[]{:S(2)}, u32[]{:S(2)}) collective-permute-start(bf16[64,2048]{1,0:T(8,128)(2,1)} %get-tuple-element.16.refs_1_), channel_id=1, source_target_pairs={{0,16},{16,32},{32,48},{48,64},{64,80},{80,96},{96,112},{112,0},{1... | collective-permute-start | bytes 786440 | tf_op jit(solution)/shard_map/ppermute | solution.py:19
  12.0 18.8 %all-to-all-start = ((bf16[8,64,256]{2,1,0:T(8,128)(2,1)}), bf16[8,64,256]{2,1,0:T(8,128)(2,1)S(1)}, u32[]{:S(2)}, u32[]{:S(2)}) async-start(bf16[8,64,256]{2,1,0:T(8,128)(2,1)} %get-tuple-element.17), calls=%async_computation | async-start | bytes 524288 | tf_op jit(solution)/shard_map/all_to_all | solution.py:293
  18.5 17.8 %collective-permute-start.4 = (bf16[64,2048]{1,0:T(8,128)(2,1)S(1)}, bf16[64,2048]{1,0:T(8,128)(2,1)S(1)}, u32[]{:S(2)}, u32[]{:S(2)}) collective-permute-start(bf16[64,2048]{1,0:T(8,128)(2,1)S(1)} %collective-permute-done.refs_2_), channel_id=1, source_target_pairs={{0,112},{16,0},{32,16},{48,32},{64,48},{80,64},{96,80},{112,96},{1... | collective-permute-start | bytes 786440 | tf_op jit(solution)/shard_map/ppermute | solution.py:19
  24.4 12.7 %collective-permute-start.5 = (bf16[64,2048]{1,0:T(8,128)(2,1)S(1)}, bf16[64,2048]{1,0:T(8,128)(2,1)S(1)}, u32[]{:S(2)}, u32[]{:S(2)}) collective-permute-start(bf16[64,2048]{1,0:T(8,128)(2,1)S(1)} %collective-permute-done.1.refs_3_), channel_id=1, source_target_pairs={{0,112},{16,0},{32,16},{48,32},{64,48},{80,64},{96,80},{112,96},{1... | collective-permute-start | bytes 786440 | tf_op jit(solution)/shard_map/ppermute | solution.py:19
  28.3 8.0 %collective-permute-start.6 = (bf16[64,2048]{1,0:T(8,128)(2,1)S(1)}, bf16[64,2048]{1,0:T(8,128)(2,1)S(1)}, u32[]{:S(2)}, u32[]{:S(2)}) collective-permute-start(bf16[64,2048]{1,0:T(8,128)(2,1)S(1)} %collective-permute-done.2.refs_4_), channel_id=1, source_target_pairs={{0,16},{16,32},{32,48},{48,64},{64,80},{80,96},{96,112},{112,0},{1... | collective-permute-start | bytes 786440 | tf_op jit(solution)/shard_map/ppermute | solution.py:19
  30.8 9.9 %collective-permute-start.9 = (bf16[8,64,256]{2,1,0:T(8,128)(2,1)S(1)}, bf16[8,64,256]{2,1,0:T(8,128)(2,1)S(1)}, u32[]{:S(2)}, u32[]{:S(2)}) collective-permute-start(bf16[8,64,256]{2,1,0:T(8,128)(2,1)S(1)} %all-to-all-done.own), channel_id=1, source_target_pairs={{0,128},{128,0},{1,129},{129,1},{2,130},{130,2},{3,131},{131,3},{4... | collective-permute-start | bytes 786440 | tf_op jit(solution)/shard_map/ppermute | solution.py:19
  36.1 22.4 %copy-start.6 = (s32[8]{0:T(128)S(1)}, s32[8]{0:T(128)}, u32[]{:S(2)}) copy-start(s32[8]{0:T(128)} %constant.36.clone) | copy-start | bytes 100
  36.1 10.3 %collective-permute-start.7 = (bf16[64,2048]{1,0:T(8,128)(2,1)S(1)}, bf16[64,2048]{1,0:T(8,128)(2,1)S(1)}, u32[]{:S(2)}, u32[]{:S(2)}) collective-permute-start(bf16[64,2048]{1,0:T(8,128)(2,1)S(1)} %collective-permute-done.3.refs_5_), channel_id=1, source_target_pairs={{0,16},{16,32},{32,48},{48,64},{64,80},{80,96},{96,112},{112,0},{1... | collective-permute-start | bytes 786440 | tf_op jit(solution)/shard_map/ppermute | solution.py:19
  36.2 10.2 %collective-permute-start.8 = (bf16[8,64,256]{2,1,0:T(8,128)(2,1)S(1)}, bf16[8,64,256]{2,1,0:T(8,128)(2,1)S(1)}, u32[]{:S(2)}, u32[]{:S(2)}) collective-permute-start(bf16[8,64,256]{2,1,0:T(8,128)(2,1)S(1)} %all-to-all-done.own), channel_id=1, source_target_pairs={{0,8},{8,0},{1,9},{9,1},{2,10},{10,2},{3,11},{11,3},{4,12},{12,4},... | collective-permute-start | bytes 786440 | tf_op jit(solution)/shard_map/ppermute | solution.py:19
  36.3 15.3 %collective-permute-start.13 = (bf16[64,2048]{1,0:T(8,128)(2,1)S(1)}, bf16[64,2048]{1,0:T(8,128)(2,1)S(1)}, u32[]{:S(2)}, u32[]{:S(2)}) collective-permute-start(bf16[64,2048]{1,0:T(8,128)(2,1)S(1)} %collective-permute-done.6.refs_8_), channel_id=1, source_target_pairs={{0,16},{16,32},{32,48},{48,64},{64,80},{80,96},{96,112},{112,0},{1... | collective-permute-start | bytes 786440 | tf_op jit(solution)/shard_map/ppermute | solution.py:19
  37.1 14.5 %collective-permute-start.12 = (bf16[64,2048]{1,0:T(8,128)(2,1)S(1)}, bf16[64,2048]{1,0:T(8,128)(2,1)S(1)}, u32[]{:S(2)}, u32[]{:S(2)}) collective-permute-start(bf16[64,2048]{1,0:T(8,128)(2,1)S(1)} %collective-permute-done.5.refs_7_), channel_id=1, source_target_pairs={{0,112},{16,0},{32,16},{48,32},{64,48},{80,64},{96,80},{112,96},{1... | collective-permute-start | bytes 786440 | tf_op jit(solution)/shard_map/ppermute | solution.py:19
  40.7 14.1 %collective-permute-start.10 = (bf16[8,64,256]{2,1,0:T(8,128)(2,1)S(1)}, bf16[8,64,256]{2,1,0:T(8,128)(2,1)S(1)}, u32[]{:S(2)}, u32[]{:S(2)}) collective-permute-start(bf16[8,64,256]{2,1,0:T(8,128)(2,1)S(1)} %collective-permute-done.9.over), channel_id=1, source_target_pairs={{0,8},{8,0},{1,9},{9,1},{2,10},{10,2},{3,11},{11,3},{4,12},{12,4},... | collective-permute-start | bytes 786440 | tf_op jit(solution)/shard_map/ppermute | solution.py:19
  46.4 12.1 %collective-permute-start.11 = (bf16[64,2048]{1,0:T(8,128)(2,1)S(1)}, bf16[64,2048]{1,0:T(8,128)(2,1)S(1)}, u32[]{:S(2)}, u32[]{:S(2)}) collective-permute-start(bf16[64,2048]{1,0:T(8,128)(2,1)S(1)} %collective-permute-done.4.refs_6_), channel_id=1, source_target_pairs={{0,112},{16,0},{32,16},{48,32},{64,48},{80,64},{96,80},{112,96},{1... | collective-permute-start | bytes 786440 | tf_op jit(solution)/shard_map/ppermute | solution.py:19
  46.4 12.1 %collective-permute-start.14 = (bf16[64,2048]{1,0:T(8,128)(2,1)S(1)}, bf16[64,2048]{1,0:T(8,128)(2,1)S(1)}, u32[]{:S(2)}, u32[]{:S(2)}) collective-permute-start(bf16[64,2048]{1,0:T(8,128)(2,1)S(1)} %collective-permute-done.7.refs_9_), channel_id=1, source_target_pairs={{0,16},{16,32},{32,48},{48,64},{64,80},{80,96},{96,112},{112,0},{1... | collective-permute-start | bytes 786440 | tf_op jit(solution)/shard_map/ppermute | solution.py:19
  51.6 8.9 %collective-permute-start.15 = (bf16[64,2048]{1,0:T(8,128)(2,1)S(1)}, bf16[64,2048]{1,0:T(8,128)(2,1)S(1)}, u32[]{:S(2)}, u32[]{:S(2)}) collective-permute-start(bf16[64,2048]{1,0:T(8,128)(2,1)S(1)} %collective-permute-done.13.refs_2_), channel_id=1, source_target_pairs={{0,16},{16,32},{32,48},{48,64},{64,80},{80,96},{96,112},{112,0},{1... | collective-permute-start | bytes 786440 | tf_op jit(solution)/shard_map/ppermute | solution.py:19
  51.6 8.9 %collective-permute-start.16 = (bf16[64,2048]{1,0:T(8,128)(2,1)S(1)}, bf16[64,2048]{1,0:T(8,128)(2,1)S(1)}, u32[]{:S(2)}, u32[]{:S(2)}) collective-permute-start(bf16[64,2048]{1,0:T(8,128)(2,1)S(1)} %collective-permute-done.12.refs_1_), channel_id=1, source_target_pairs={{0,112},{16,0},{32,16},{48,32},{64,48},{80,64},{96,80},{112,96},{1... | collective-permute-start | bytes 786440 | tf_op jit(solution)/shard_map/ppermute | solution.py:19
  55.5 8.0 %copy-start.5 = (s32[1,8]{1,0:T(1,128)S(1)}, s32[1,8]{1,0:T(1,128)}, u32[]{:S(2)}) copy-start(s32[1,8]{1,0:T(1,128)} %constant.43) | copy-start | bytes 100
  57.8 10.8 %collective-permute-start.18 = (bf16[640,256]{1,0:T(8,128)(2,1)S(1)}, bf16[640,256]{1,0:T(8,128)(2,1)S(1)}, u32[]{:S(2)}, u32[]{:S(2)}) collective-permute-start(bf16[640,256]{1,0:T(8,128)(2,1)S(1)} %get-tuple-element.20.early), channel_id=1, source_target_pairs={{0,128},{128,0},{1,129},{129,1},{2,130},{130,2},{3,131},{131,3},{4... | collective-permute-start | bytes 983048 | tf_op jit(solution)/shard_map/ppermute | solution.py:19
  62.2 9.9 %collective-permute-start.21 = (bf16[384,256]{1,0:T(8,128)(2,1)S(1)}, bf16[384,256]{1,0:T(8,128)(2,1)S(1)}, u32[]{:S(2)}, u32[]{:S(2)}) collective-permute-start(bf16[384,256]{1,0:T(8,128)(2,1)S(1)} %get-tuple-element.21.late), channel_id=1, source_target_pairs={{0,128},{128,0},{1,129},{129,1},{2,130},{130,2},{3,131},{131,3},{4... | collective-permute-start | bytes 589832 | tf_op jit(solution)/shard_map/ppermute | solution.py:19
  63.5 9.2 %collective-permute-start.17 = (bf16[640,256]{1,0:T(8,128)(2,1)S(1)}, bf16[640,256]{1,0:T(8,128)(2,1)S(1)}, u32[]{:S(2)}, u32[]{:S(2)}) collective-permute-start(bf16[640,256]{1,0:T(8,128)(2,1)S(1)} %get-tuple-element.20.early), channel_id=1, source_target_pairs={{0,8},{8,0},{1,9},{9,1},{2,10},{10,2},{3,11},{11,3},{4,12},{12,4},... | collective-permute-start | bytes 983048 | tf_op jit(solution)/shard_map/ppermute | solution.py:19
  63.6 9.1 %collective-permute-start.20 = (bf16[384,256]{1,0:T(8,128)(2,1)S(1)}, bf16[384,256]{1,0:T(8,128)(2,1)S(1)}, u32[]{:S(2)}, u32[]{:S(2)}) collective-permute-start(bf16[384,256]{1,0:T(8,128)(2,1)S(1)} %get-tuple-element.21.late), channel_id=1, source_target_pairs={{0,8},{8,0},{1,9},{9,1},{2,10},{10,2},{3,11},{11,3},{4,12},{12,4},... | collective-permute-start | bytes 589832 | tf_op jit(solution)/shard_map/ppermute | solution.py:19
  68.5 5.2 %collective-permute-start.19 = (bf16[640,256]{1,0:T(8,128)(2,1)S(1)}, bf16[640,256]{1,0:T(8,128)(2,1)S(1)}, u32[]{:S(2)}, u32[]{:S(2)}) collective-permute-start(bf16[640,256]{1,0:T(8,128)(2,1)S(1)} %collective-permute-done.18.refs_1_), channel_id=1, source_target_pairs={{0,8},{8,0},{1,9},{9,1},{2,10},{10,2},{3,11},{11,3},{4,12},{12,4},... | collective-permute-start | bytes 983048 | tf_op jit(solution)/shard_map/ppermute | solution.py:19
  72.1 1.7 %collective-permute-start.22 = (bf16[384,256]{1,0:T(8,128)(2,1)S(1)}, bf16[384,256]{1,0:T(8,128)(2,1)S(1)}, u32[]{:S(2)}, u32[]{:S(2)}) collective-permute-start(bf16[384,256]{1,0:T(8,128)(2,1)S(1)} %collective-permute-done.21.refs_4_), channel_id=1, source_target_pairs={{0,8},{8,0},{1,9},{9,1},{2,10},{10,2},{3,11},{11,3},{4,12},{12,4},... | collective-permute-start | bytes 589832 | tf_op jit(solution)/shard_map/ppermute | solution.py:19
  73.8 22.7 %copy-start.1 = (bf16[1,1024,2048]{2,1,0:T(8,128)(2,1)S(1)}, bf16[1,1024,2048]{2,1,0:T(8,128)(2,1)}, u32[]{:S(2)}) copy-start(bf16[1,1024,2048]{2,1,0:T(8,128)(2,1)} %param.15) | copy-start | bytes 12582916
  73.8 22.7 %copy-start.2 = (bf16[1,128,2048]{2,1,0:T(8,128)(2,1)S(1)}, bf16[1,128,2048]{2,1,0:T(8,128)(2,1)}, u32[]{:S(2)}) copy-start(bf16[1,128,2048]{2,1,0:T(8,128)(2,1)} %param.9) | copy-start | bytes 1572868
  98.0 18.1 %collective-permute-start.23 = (bf16[128,2048]{1,0:T(8,128)(2,1)}, bf16[128,2048]{1,0:T(8,128)(2,1)S(1)}, u32[]{:S(2)}, u32[]{:S(2)}) collective-permute-start(bf16[128,2048]{1,0:T(8,128)(2,1)} %shard_map.110), channel_id=1, source_target_pairs={{0,1},{1,2},{2,3},{3,4},{4,5},{5,6},{6,7},{8,9},{9,10},{10,11},{11... | collective-permute-start | bytes 1572872 | tf_op jit(solution)/shard_map/ppermute | solution.py:25

commit v7 on v5

--- a/solution.py
+++ b/solution.py
@@ -225,19 +225,26 @@
     )(at, *queries, *keyvals, qpos, qspan, kpos)
 
 
-def output_kernel(m_ref, w_ref, x_ref, o_ref):
+def output_kernel(m_ref, w_ref, x_ref, o_ref, upper_ref, lower_ref):
     mixed = jnp.concatenate([m_ref[h] for h in range(m_ref.shape[0])], axis=1)
     wide = 512
     for t in range(w_ref.shape[1] // wide):
         lanes = slice(t * wide, (t + 1) * wide)
         added = jnp.dot(mixed, w_ref[:, lanes], preferred_element_type=jnp.float32)
-        o_ref[:, lanes] = (x_ref[:, lanes].astype(jnp.float32) + added).astype(jnp.bfloat16)
+        made = (x_ref[:, lanes].astype(jnp.float32) + added).astype(jnp.bfloat16)
+        half = made.shape[0] // 2
+        o_ref[:, lanes] = made
+        upper_ref[:, lanes] = made[:half]
+        lower_ref[:, lanes] = made[half:]
 
 
 def outputs(mixed, w_out, x):
     return pl.pallas_call(
         output_kernel,
-        out_shape=jax.ShapeDtypeStruct(x.shape, jnp.bfloat16),
+        out_shape=[
+            jax.ShapeDtypeStruct(x.shape, jnp.bfloat16),
+            *[jax.ShapeDtypeStruct((x.shape[0] // 2, x.shape[1]), jnp.bfloat16)] * 2,
+        ],
         compiler_params=params(24),
         cost_estimate=pl.CostEstimate(
             flops=2 * 128 * 1024 * 2048, bytes_accessed=6 * MIB, transcendentals=0
@@ -298,8 +305,8 @@
     mixed = attended(at, [q_early, q_late], keyvals, qpos, qspan, kpos)
 
     mixed = lax.all_to_all(mixed.reshape(ZS, -1, head_dim), "z", 0, 0, tiled=True)
-    produced = outputs(mixed, w_out[0], inputs)
-    handed = passed_along(produced, ("yl", "x"), 1)
+    produced, *halves = outputs(mixed, w_out[0], inputs)
+    handed = jnp.concatenate([passed_along(rows, ("yl", "x"), 1) for rows in halves])
     return (produced[None], handed[None])
 
 

time: 116 us -> 116 us (level)
  waiting for transfers between devices: 31.8 us -> 28.2 us
  starting transfers between devices: 41.4 us -> 44.9 us
    ppermute x1 -> x2, waiting for transfers between devices: 14.6 us -> 11 us  [passed_along(): return lax.ppermute(block, axis, route)]
    ppermute x1 -> x2, starting transfers between devices: 3.39 us -> 6.78 us  [passed_along(): return lax.ppermute(block, axis, route)]
    unnamed x20 -> x19, local copies, waits for them, and re-layouts: 3.39 us -> 2.6 us
  transfers between devices with their start and end apart: 25 -> 26, of which waited for: 10 -> 11; matrix products, arithmetic and copies ran while one was open for 4% -> 4% of each run, Pallas kernels for 5% -> 5%
where the time goes in v7:
time: 116 us; the launch traced here: 114 us
  starting transfers between devices  44.9 us (39%)
  waiting for transfers between devices  28.2 us (24%)
  Pallas kernels  18.1 us (16%)
  blocking collectives  14.9 us (13%)
  local copies, waits for them, and re-layouts  4.81 us (4%)
  other arithmetic  2.72 us (2%)
    ppermute x23, starting transfers between devices, shifted(): lax.ppermute(block, axis, [(i, (i + distance) % count) for i in range(cou...  33.6 us
    all_to_all x1, blocking collectives, per_device(): lax.all_to_all(mixed.reshape(ZS, -1, head_dim), 'z', 0, 0, tiled=True)  14.9 us
    ppermute x23, waiting for transfers between devices, shifted(): lax.ppermute(block, axis, [(i, (i + distance) % count) for i in range(cou...  14.6 us
    ppermute x2, waiting for transfers between devices, passed_along(): return lax.ppermute(block, axis, route)  11 us
    pallas_call x1, Pallas kernels, attended(): pl.pallas_call(attend_kernel, in_specs=[pl.BlockSpec(memory_space=pltpu.S...  8.87 us
    ppermute x2, starting transfers between devices, passed_along(): return lax.ppermute(block, axis, route)  6.78 us
    pallas_call x2, Pallas kernels, projected(): pl.pallas_call(functools.partial(project_kernel, len(blocks)), in_specs=[...  4.89 us
    all_to_all x1, starting transfers between devices, per_device(): own_w = lax.all_to_all(by_head, 'z', 0, 0, tiled=True)  4.51 us
  transfers between devices with their start and end apart: 26, of which 11 were waited for; matrix products, arithmetic and copies ran while one was open for 4% of the time, Pallas kernels for 5%

profile of v7, /device:TPU:8, one launch (start us, length us, event | category | flops | bytes accessed | tf_op | source)
XLA Modules:
  0.0 114.5 jit_solution(12207388499376524996)
XLA Ops:
  0.6 2.2 %shard_map.104 = (bf16[64,2048]{1,0:T(8,128)(2,1)}, bf16[64,2048]{1,0:T(8,128)(2,1)}, bf16[8,64,256]{2,1,0:T(8,128)(2,1)}) custom-call(bf16[128,2048]{1,0:T(8,128)(2,1)} %bitcast.26, f32[1,2048]{1,0:T(1,128)} %g_any.1, bf16[64,2048]{1,0:T(8,128)(2,1)} %bitcast.31), custom_call_target="tpu_custom_call" | custom-call | bytes 1572864 | tf_op jit(solution)/shard_map/pallas_call | solution.py:58
  2.8 5.9 %collective-permute-start = (bf16[64,2048]{1,0:T(8,128)(2,1)}, bf16[64,2048]{1,0:T(8,128)(2,1)S(1)}, u32[]{:S(2)}, u32[]{:S(2)}) collective-permute-start(bf16[64,2048]{1,0:T(8,128)(2,1)} %get-tuple-element.13.refs_0_), channel_id=1, source_target_pairs={{0,112},{16,0},{32,16},{48,32},{64,48},{80,64},{96,80},{112,96},{1... | collective-permute-start | bytes 786440 | tf_op jit(solution)/shard_map/ppermute | solution.py:19
  8.8 3.2 %collective-permute-start.1 = (bf16[64,2048]{1,0:T(8,128)(2,1)}, bf16[64,2048]{1,0:T(8,128)(2,1)S(1)}, u32[]{:S(2)}, u32[]{:S(2)}) collective-permute-start(bf16[64,2048]{1,0:T(8,128)(2,1)} %get-tuple-element.14.refs_1_), channel_id=1, source_target_pairs={{0,112},{16,0},{32,16},{48,32},{64,48},{80,64},{96,80},{112,96},{1... | collective-permute-start | bytes 786440 | tf_op jit(solution)/shard_map/ppermute | solution.py:19
  12.0 4.5 %all-to-all-start = ((bf16[8,64,256]{2,1,0:T(8,128)(2,1)}), bf16[8,64,256]{2,1,0:T(8,128)(2,1)S(1)}, u32[]{:S(2)}, u32[]{:S(2)}) async-start(bf16[8,64,256]{2,1,0:T(8,128)(2,1)} %get-tuple-element.15), calls=%async_computation | async-start | bytes 524288 | tf_op jit(solution)/shard_map/all_to_all | solution.py:276
  16.5 0.7 fusion
  17.4 3.3 %collective-permute-start.4 = (bf16[64,2048]{1,0:T(8,128)(2,1)S(1)}, bf16[64,2048]{1,0:T(8,128)(2,1)S(1)}, u32[]{:S(2)}, u32[]{:S(2)}) collective-permute-start(bf16[64,2048]{1,0:T(8,128)(2,1)S(1)} %collective-permute-done.refs_2_), channel_id=1, source_target_pairs={{0,112},{16,0},{32,16},{48,32},{64,48},{80,64},{96,80},{112,96},{1... | collective-permute-start | bytes 786440 | tf_op jit(solution)/shard_map/ppermute | solution.py:19
  20.7 3.7 %collective-permute-done.1.refs_3_ = bf16[64,2048]{1,0:T(8,128)(2,1)S(1)} collective-permute-done((bf16[64,2048]{1,0:T(8,128)(2,1)}, bf16[64,2048]{1,0:T(8,128)(2,1)S(1)}, u32[]{:S(2)}, u32[]{:S(2)}) %collective-permute-start.1) | collective-permute-done | bytes 262176 | tf_op jit(solution)/shard_map/ppermute | solution.py:19
  24.4 3.7 %collective-permute-start.5 = (bf16[64,2048]{1,0:T(8,128)(2,1)S(1)}, bf16[64,2048]{1,0:T(8,128)(2,1)S(1)}, u32[]{:S(2)}, u32[]{:S(2)}) collective-permute-start(bf16[64,2048]{1,0:T(8,128)(2,1)S(1)} %collective-permute-done.1.refs_3_), channel_id=1, source_target_pairs={{0,112},{16,0},{32,16},{48,32},{64,48},{80,64},{96,80},{112,96},{1... | collective-permute-start | bytes 786440 | tf_op jit(solution)/shard_map/ppermute | solution.py:19
  28.2 2.6 %all-to-all-done.own = bf16[8,64,256]{2,1,0:T(8,128)(2,1)S(1)} async-done(((bf16[8,64,256]{2,1,0:T(8,128)(2,1)}), bf16[8,64,256]{2,1,0:T(8,128)(2,1)S(1)}, u32[]{:S(2)}, u32[]{:S(2)}) %all-to-all-start) | async-done | bytes 262176 | tf_op jit(solution)/shard_map/all_to_all | solution.py:276
  30.8 2.3 %collective-permute-start.9 = (bf16[8,64,256]{2,1,0:T(8,128)(2,1)S(1)}, bf16[8,64,256]{2,1,0:T(8,128)(2,1)S(1)}, u32[]{:S(2)}, u32[]{:S(2)}) collective-permute-start(bf16[8,64,256]{2,1,0:T(8,128)(2,1)S(1)} %all-to-all-done.own), channel_id=1, source_target_pairs={{0,128},{128,0},{1,129},{129,1},{2,130},{130,2},{3,131},{131,3},{4... | collective-permute-start | bytes 786440 | tf_op jit(solution)/shard_map/ppermute | solution.py:19
  33.1 0.7 fusion.2
  33.7 0.1 collective-permute-start.7
  33.9 0.1 collective-permute-start.8
  34.0 3.9 %collective-permute-done.6.refs_8_ = bf16[64,2048]{1,0:T(8,128)(2,1)S(1)} collective-permute-done((bf16[64,2048]{1,0:T(8,128)(2,1)S(1)}, bf16[64,2048]{1,0:T(8,128)(2,1)S(1)}, u32[]{:S(2)}, u32[]{:S(2)}) %collective-permute-start.6) | collective-permute-done | bytes 262176 | tf_op jit(solution)/shard_map/ppermute | solution.py:19
  37.8 3.2 %collective-permute-start.12 = (bf16[64,2048]{1,0:T(8,128)(2,1)S(1)}, bf16[64,2048]{1,0:T(8,128)(2,1)}, u32[]{:S(2)}, u32[]{:S(2)}) collective-permute-start(bf16[64,2048]{1,0:T(8,128)(2,1)S(1)} %collective-permute-done.5.refs_7_), channel_id=1, source_target_pairs={{0,112},{16,0},{32,16},{48,32},{64,48},{80,64},{96,80},{112,96},{1... | collective-permute-start | bytes 786440 | tf_op jit(solution)/shard_map/ppermute | solution.py:19
  41.2 0.6 constant_dynamic-slice_fusion.temp_ref
  41.8 1.1 dynamic-slice_bitcast_fusion.refs_10_.refs_6_
  42.9 1.3 %collective-permute-done.7.refs_9_ = bf16[64,2048]{1,0:T(8,128)(2,1)S(1)} collective-permute-done((bf16[64,2048]{1,0:T(8,128)(2,1)S(1)}, bf16[64,2048]{1,0:T(8,128)(2,1)S(1)}, u32[]{:S(2)}, u32[]{:S(2)}) %collective-permute-start.7) | collective-permute-done | bytes 262176 | tf_op jit(solution)/shard_map/ppermute | solution.py:19
  44.2 2.0 %collective-permute-start.14 = (bf16[64,2048]{1,0:T(8,128)(2,1)S(1)}, bf16[64,2048]{1,0:T(8,128)(2,1)S(1)}, u32[]{:S(2)}, u32[]{:S(2)}) collective-permute-start(bf16[64,2048]{1,0:T(8,128)(2,1)S(1)} %collective-permute-done.7.refs_9_), channel_id=1, source_target_pairs={{0,16},{16,32},{32,48},{48,64},{64,80},{80,96},{96,112},{112,0},{1... | collective-permute-start | bytes 786440 | tf_op jit(solution)/shard_map/ppermute | solution.py:19
  46.2 0.8 collective-permute-done.13.refs_2_
  47.0 3.7 %collective-permute-start.16 = (bf16[64,2048]{1,0:T(8,128)(2,1)}, bf16[64,2048]{1,0:T(8,128)(2,1)S(1)}, u32[]{:S(2)}, u32[]{:S(2)}) collective-permute-start(bf16[64,2048]{1,0:T(8,128)(2,1)} %collective-permute-done.12.refs_1_), channel_id=1, source_target_pairs={{0,112},{16,0},{32,16},{48,32},{64,48},{80,64},{96,80},{112,96},{1... | collective-permute-start | bytes 786440 | tf_op jit(solution)/shard_map/ppermute | solution.py:19
  50.6 0.6 shard_map.105.refs_11_.refs_7_
  51.3 0.9 copy-done.3
  52.2 0.9 copy-done.4
  53.2 2.2 %shard_map.106 = (bf16[640,128]{1,0:T(8,128)(2,1)S(1)}, bf16[640,256]{1,0:T(8,128)(2,1)S(1)}) custom-call(f32[1,1]{1,0:T(1,128)} %constant_dynamic-slice_fusion.temp_ref, bf16[64,2048]{1,0:T(8,128)(2,1)S(1)} %copy-done.3, bf16[64,2048]{1,0:T(8,128)(2,1)S(1)} %copy-done.4, bf16[64,2048]{1,0:T(8,128)(2,1)S(1)} %collective-permute-done.refs_2_, ...), custom_call_target="tpu_custom_call" | custom-call | flops 1006632960 | bytes 5177344 | tf_op jit(solution)/shard_map/pallas_call | solution.py:117
  55.5 0.7 copy-done.5
  56.1 2.2 %collective-permute-start.18 = (bf16[640,256]{1,0:T(8,128)(2,1)S(1)}, bf16[640,256]{1,0:T(8,128)(2,1)S(1)}, u32[]{:S(2)}, u32[]{:S(2)}) collective-permute-start(bf16[640,256]{1,0:T(8,128)(2,1)S(1)} %get-tuple-element.18.refs_0_), channel_id=1, source_target_pairs={{0,128},{128,0},{1,129},{129,1},{2,130},{130,2},{3,131},{131,3},{4... | collective-permute-start | bytes 983048 | tf_op jit(solution)/shard_map/ppermute | solution.py:19
  58.3 0.2 convert_reduce_fusion
  58.5 0.1 collective-permute-done.15.refs_4_
  58.6 2.7 %shard_map.107 = (bf16[384,128]{1,0:T(8,128)(2,1)S(1)}, bf16[384,256]{1,0:T(8,128)(2,1)S(1)}) custom-call(f32[1,1]{1,0:T(1,128)} %constant_dynamic-slice_fusion.temp_ref, bf16[64,2048]{1,0:T(8,128)(2,1)S(1)} %collective-permute-done.11.refs_0_, bf16[64,2048]{1,0:T(8,128)(2,1)} %collective-permute-done.12.refs_1_, ...), custom_call_target="tpu_custom_call" | custom-call | flops 603979776 | bytes 3735552 | tf_op jit(solution)/shard_map/pallas_call | solution.py:117
  61.3 3.1 %collective-permute-start.21 = (bf16[384,256]{1,0:T(8,128)(2,1)S(1)}, bf16[384,256]{1,0:T(8,128)(2,1)S(1)}, u32[]{:S(2)}, u32[]{:S(2)}) collective-permute-start(bf16[384,256]{1,0:T(8,128)(2,1)S(1)} %get-tuple-element.19.refs_4_), channel_id=1, source_target_pairs={{0,128},{128,0},{1,129},{129,1},{2,130},{130,2},{3,131},{131,3},{4... | collective-permute-start | bytes 589832 | tf_op jit(solution)/shard_map/ppermute | solution.py:19
  64.4 0.1 select_reduce_fusion
  64.5 0.1 collective-permute-start.17
  64.6 0.1 collective-permute-done.18.refs_2_
  64.7 0.4 collective-permute-start.19
  65.1 0.2 copy.23
  65.3 0.2 copy.20
  65.6 0.2 collective-permute-start.20
  65.8 3.4 %collective-permute-done.21.refs_6_ = bf16[384,256]{1,0:T(8,128)(2,1)S(1)} collective-permute-done((bf16[384,256]{1,0:T(8,128)(2,1)S(1)}, bf16[384,256]{1,0:T(8,128)(2,1)S(1)}, u32[]{:S(2)}, u32[]{:S(2)}) %collective-permute-start.21) | collective-permute-done | bytes 196640 | tf_op jit(solution)/shard_map/ppermute | solution.py:19
  69.2 1.3 %collective-permute-done.22.refs_7_ = bf16[384,256]{1,0:T(8,128)(2,1)S(1)} collective-permute-done((bf16[384,256]{1,0:T(8,128)(2,1)S(1)}, bf16[384,256]{1,0:T(8,128)(2,1)S(1)}, u32[]{:S(2)}, u32[]{:S(2)}) %collective-permute-start.22) | collective-permute-done | bytes 196640 | tf_op jit(solution)/shard_map/ppermute | solution.py:19
  70.6 8.9 %shard_map.108 = bf16[1024,128]{1,0:T(8,128)(2,1)S(1)} custom-call(s32[2,8]{1,0:T(2,128)S(1)} %pad_add_fusion.at_ref, bf16[640,128]{1,0:T(8,128)(2,1)S(1)} %copy-done.6, bf16[384,128]{1,0:T(8,128)(2,1)S(1)} %get-tuple-element.17.qb, bf16[640,256]{1,0:T(8,128)(2,1)S(1)} %get-tuple-element.18.refs_0_, bf16[640,256]{1,0:T(8,128)(2,1)S(1)} %collective-permute-done.17.refs_1_, ...), custom_call_target="tpu_custom_call" | custom-call | flops 21474836480 | bytes 2097152 | tf_op jit(solution)/shard_map/pallas_call | solution.py:210
  79.5 14.9 %all_to_all.10.m_ref = bf16[8,128,128]{2,1,0:T(8,128)(2,1)S(1)} all-to-all(bf16[8,128,128]{2,1,0:T(8,128)(2,1)S(1)} %bitcast.28), channel_id=1, replica_groups=mesh['yh'=2,'z'=8,'c'=2,'yl'=2,'x'=4] {'z'}, dimensions={0} | all-to-all | bytes 524288 | tf_op jit(solution)/shard_map/all_to_all | solution.py:307
  94.3 1.6 %shard_map.109 = (bf16[128,2048]{1,0:T(8,128)(2,1)}, bf16[64,2048]{1,0:T(8,128)(2,1)S(1)}, bf16[64,2048]{1,0:T(8,128)(2,1)S(1)}) custom-call(bf16[8,128,128]{2,1,0:T(8,128)(2,1)S(1)} %all_to_all.10.m_ref, bf16[1024,2048]{1,0:T(8,128)(2,1)S(1)} %bitcast.25, bf16[128,2048]{1,0:T(8,128)(2,1)S(1)} %bitcast.27), custom_call_target="tpu_custom_call" | custom-call | flops 536870912 | bytes 6291456 | tf_op jit(solution)/shard_map/pallas_call | solution.py:242
  95.9 3.4 %collective-permute-start.23 = (bf16[64,2048]{1,0:T(8,128)(2,1)S(1)}, bf16[64,2048]{1,0:T(8,128)(2,1)S(1)}, u32[]{:S(2)}, u32[]{:S(2)}) collective-permute-start(bf16[64,2048]{1,0:T(8,128)(2,1)S(1)} %get-tuple-element.22), channel_id=1, source_target_pairs={{0,1},{1,2},{2,3},{3,4},{4,5},{5,6},{6,7},{8,9},{9,10},{10,11},{11... | collective-permute-start | bytes 786440 | tf_op jit(solution)/shard_map/ppermute | solution.py:25
  99.3 3.4 %collective-permute-start.24 = (bf16[64,2048]{1,0:T(8,128)(2,1)S(1)}, bf16[64,2048]{1,0:T(8,128)(2,1)S(1)}, u32[]{:S(2)}, u32[]{:S(2)}) collective-permute-start(bf16[64,2048]{1,0:T(8,128)(2,1)S(1)} %get-tuple-element.23), channel_id=1, source_target_pairs={{0,1},{1,2},{2,3},{3,4},{4,5},{5,6},{6,7},{8,9},{9,10},{10,11},{11... | collective-permute-start | bytes 786440 | tf_op jit(solution)/shard_map/ppermute | solution.py:25
  102.7 6.4 %collective-permute-done.23 = bf16[64,2048]{1,0:T(8,128)(2,1)S(1)} collective-permute-done((bf16[64,2048]{1,0:T(8,128)(2,1)S(1)}, bf16[64,2048]{1,0:T(8,128)(2,1)S(1)}, u32[]{:S(2)}, u32[]{:S(2)}) %collective-permute-start.23) | collective-permute-done | bytes 262176 | tf_op jit(solution)/shard_map/ppermute | solution.py:25
  109.1 4.6 %collective-permute-done.24 = bf16[64,2048]{1,0:T(8,128)(2,1)S(1)} collective-permute-done((bf16[64,2048]{1,0:T(8,128)(2,1)S(1)}, bf16[64,2048]{1,0:T(8,128)(2,1)S(1)}, u32[]{:S(2)}, u32[]{:S(2)}) %collective-permute-start.24) | collective-permute-done | bytes 262176 | tf_op jit(solution)/shard_map/ppermute | solution.py:25
  113.7 0.8 maximum_bitcast_fusion
  (48 shorter events, 0.3 us)
Async XLA Ops:
  0.6 40.5 %copy-start = (f32[1,8]{1,0:T(1,128)S(1)}, f32[1,8]{1,0:T(1,128)}, u32[]{:S(2)}) copy-start(f32[1,8]{1,0:T(1,128)} %param.16) | copy-start | bytes 100
  2.8 55.5 %copy-start.7 = (s32[4096]{0:T(1024)S(1)}, s32[4096]{0:T(1024)}, u32[]{:S(2)}) copy-start(s32[4096]{0:T(1024)} %param.11) | copy-start | bytes 49156
  2.8 14.5 %collective-permute-start = (bf16[64,2048]{1,0:T(8,128)(2,1)}, bf16[64,2048]{1,0:T(8,128)(2,1)S(1)}, u32[]{:S(2)}, u32[]{:S(2)}) collective-permute-start(bf16[64,2048]{1,0:T(8,128)(2,1)} %get-tuple-element.13.refs_0_), channel_id=1, source_target_pairs={{0,112},{16,0},{32,16},{48,32},{64,48},{80,64},{96,80},{112,96},{1... | collective-permute-start | bytes 786440 | tf_op jit(solution)/shard_map/ppermute | solution.py:19
  8.8 19.4 %collective-permute-start.2 = (bf16[64,2048]{1,0:T(8,128)(2,1)}, bf16[64,2048]{1,0:T(8,128)(2,1)S(1)}, u32[]{:S(2)}, u32[]{:S(2)}) collective-permute-start(bf16[64,2048]{1,0:T(8,128)(2,1)} %get-tuple-element.13.refs_0_), channel_id=1, source_target_pairs={{0,16},{16,32},{32,48},{48,64},{64,80},{80,96},{96,112},{112,0},{1... | collective-permute-start | bytes 786440 | tf_op jit(solution)/shard_map/ppermute | solution.py:19
  8.8 15.7 %collective-permute-start.1 = (bf16[64,2048]{1,0:T(8,128)(2,1)}, bf16[64,2048]{1,0:T(8,128)(2,1)S(1)}, u32[]{:S(2)}, u32[]{:S(2)}) collective-permute-start(bf16[64,2048]{1,0:T(8,128)(2,1)} %get-tuple-element.14.refs_1_), channel_id=1, source_target_pairs={{0,112},{16,0},{32,16},{48,32},{64,48},{80,64},{96,80},{112,96},{1... | collective-permute-start | bytes 786440 | tf_op jit(solution)/shard_map/ppermute | solution.py:19
  12.0 21.7 %collective-permute-start.3 = (bf16[64,2048]{1,0:T(8,128)(2,1)}, bf16[64,2048]{1,0:T(8,128)(2,1)S(1)}, u32[]{:S(2)}, u32[]{:S(2)}) collective-permute-start(bf16[64,2048]{1,0:T(8,128)(2,1)} %get-tuple-element.14.refs_1_), channel_id=1, source_target_pairs={{0,16},{16,32},{32,48},{48,64},{64,80},{80,96},{96,112},{112,0},{1... | collective-permute-start | bytes 786440 | tf_op jit(solution)/shard_map/ppermute | solution.py:19
  12.0 18.8 %all-to-all-start = ((bf16[8,64,256]{2,1,0:T(8,128)(2,1)}), bf16[8,64,256]{2,1,0:T(8,128)(2,1)S(1)}, u32[]{:S(2)}, u32[]{:S(2)}) async-start(bf16[8,64,256]{2,1,0:T(8,128)(2,1)} %get-tuple-element.15), calls=%async_computation | async-start | bytes 524288 | tf_op jit(solution)/shard_map/all_to_all | solution.py:276
  17.4 16.5 %collective-permute-start.4 = (bf16[64,2048]{1,0:T(8,128)(2,1)S(1)}, bf16[64,2048]{1,0:T(8,128)(2,1)S(1)}, u32[]{:S(2)}, u32[]{:S(2)}) collective-permute-start(bf16[64,2048]{1,0:T(8,128)(2,1)S(1)} %collective-permute-done.refs_2_), channel_id=1, source_target_pairs={{0,112},{16,0},{32,16},{48,32},{64,48},{80,64},{96,80},{112,96},{1... | collective-permute-start | bytes 786440 | tf_op jit(solution)/shard_map/ppermute | solution.py:19
  24.4 13.4 %collective-permute-start.5 = (bf16[64,2048]{1,0:T(8,128)(2,1)S(1)}, bf16[64,2048]{1,0:T(8,128)(2,1)S(1)}, u32[]{:S(2)}, u32[]{:S(2)}) collective-permute-start(bf16[64,2048]{1,0:T(8,128)(2,1)S(1)} %collective-permute-done.1.refs_3_), channel_id=1, source_target_pairs={{0,112},{16,0},{32,16},{48,32},{64,48},{80,64},{96,80},{112,96},{1... | collective-permute-start | bytes 786440 | tf_op jit(solution)/shard_map/ppermute | solution.py:19
  28.2 9.7 %collective-permute-start.6 = (bf16[64,2048]{1,0:T(8,128)(2,1)S(1)}, bf16[64,2048]{1,0:T(8,128)(2,1)S(1)}, u32[]{:S(2)}, u32[]{:S(2)}) collective-permute-start(bf16[64,2048]{1,0:T(8,128)(2,1)S(1)} %collective-permute-done.2.refs_4_), channel_id=1, source_target_pairs={{0,16},{16,32},{32,48},{48,64},{64,80},{80,96},{96,112},{112,0},{1... | collective-permute-start | bytes 786440 | tf_op jit(solution)/shard_map/ppermute | solution.py:19
  30.8 10.3 %collective-permute-start.9 = (bf16[8,64,256]{2,1,0:T(8,128)(2,1)S(1)}, bf16[8,64,256]{2,1,0:T(8,128)(2,1)S(1)}, u32[]{:S(2)}, u32[]{:S(2)}) collective-permute-start(bf16[8,64,256]{2,1,0:T(8,128)(2,1)S(1)} %all-to-all-done.own), channel_id=1, source_target_pairs={{0,128},{128,0},{1,129},{129,1},{2,130},{130,2},{3,131},{131,3},{4... | collective-permute-start | bytes 786440 | tf_op jit(solution)/shard_map/ppermute | solution.py:19
  33.7 10.4 %collective-permute-start.7 = (bf16[64,2048]{1,0:T(8,128)(2,1)S(1)}, bf16[64,2048]{1,0:T(8,128)(2,1)S(1)}, u32[]{:S(2)}, u32[]{:S(2)}) collective-permute-start(bf16[64,2048]{1,0:T(8,128)(2,1)S(1)} %collective-permute-done.3.refs_5_), channel_id=1, source_target_pairs={{0,16},{16,32},{32,48},{48,64},{64,80},{80,96},{96,112},{112,0},{1... | collective-permute-start | bytes 786440 | tf_op jit(solution)/shard_map/ppermute | solution.py:19
  33.9 10.3 %collective-permute-start.8 = (bf16[8,64,256]{2,1,0:T(8,128)(2,1)S(1)}, bf16[8,64,256]{2,1,0:T(8,128)(2,1)S(1)}, u32[]{:S(2)}, u32[]{:S(2)}) collective-permute-start(bf16[8,64,256]{2,1,0:T(8,128)(2,1)S(1)} %all-to-all-done.own), channel_id=1, source_target_pairs={{0,8},{8,0},{1,9},{9,1},{2,10},{10,2},{3,11},{11,3},{4,12},{12,4},... | collective-permute-start | bytes 786440 | tf_op jit(solution)/shard_map/ppermute | solution.py:19
  37.8 9.1 %collective-permute-start.13 = (bf16[64,2048]{1,0:T(8,128)(2,1)S(1)}, bf16[64,2048]{1,0:T(8,128)(2,1)S(1)}, u32[]{:S(2)}, u32[]{:S(2)}) collective-permute-start(bf16[64,2048]{1,0:T(8,128)(2,1)S(1)} %collective-permute-done.6.refs_8_), channel_id=1, source_target_pairs={{0,16},{16,32},{32,48},{48,64},{64,80},{80,96},{96,112},{112,0},{1... | collective-permute-start | bytes 786440 | tf_op jit(solution)/shard_map/ppermute | solution.py:19
  37.8 9.1 %collective-permute-start.12 = (bf16[64,2048]{1,0:T(8,128)(2,1)S(1)}, bf16[64,2048]{1,0:T(8,128)(2,1)}, u32[]{:S(2)}, u32[]{:S(2)}) collective-permute-start(bf16[64,2048]{1,0:T(8,128)(2,1)S(1)} %collective-permute-done.5.refs_7_), channel_id=1, source_target_pairs={{0,112},{16,0},{32,16},{48,32},{64,48},{80,64},{96,80},{112,96},{1... | collective-permute-start | bytes 786440 | tf_op jit(solution)/shard_map/ppermute | solution.py:19
  41.1 9.6 %collective-permute-start.10 = (bf16[8,64,256]{2,1,0:T(8,128)(2,1)S(1)}, bf16[8,64,256]{2,1,0:T(8,128)(2,1)S(1)}, u32[]{:S(2)}, u32[]{:S(2)}) collective-permute-start(bf16[8,64,256]{2,1,0:T(8,128)(2,1)S(1)} %collective-permute-done.9.over), channel_id=1, source_target_pairs={{0,8},{8,0},{1,9},{9,1},{2,10},{10,2},{3,11},{11,3},{4,12},{12,4},... | collective-permute-start | bytes 786440 | tf_op jit(solution)/shard_map/ppermute | solution.py:19
  44.2 14.3 %collective-permute-start.11 = (bf16[64,2048]{1,0:T(8,128)(2,1)S(1)}, bf16[64,2048]{1,0:T(8,128)(2,1)S(1)}, u32[]{:S(2)}, u32[]{:S(2)}) collective-permute-start(bf16[64,2048]{1,0:T(8,128)(2,1)S(1)} %collective-permute-done.4.refs_6_), channel_id=1, source_target_pairs={{0,112},{16,0},{32,16},{48,32},{64,48},{80,64},{96,80},{112,96},{1... | collective-permute-start | bytes 786440 | tf_op jit(solution)/shard_map/ppermute | solution.py:19
  44.2 14.3 %collective-permute-start.14 = (bf16[64,2048]{1,0:T(8,128)(2,1)S(1)}, bf16[64,2048]{1,0:T(8,128)(2,1)S(1)}, u32[]{:S(2)}, u32[]{:S(2)}) collective-permute-start(bf16[64,2048]{1,0:T(8,128)(2,1)S(1)} %collective-permute-done.7.refs_9_), channel_id=1, source_target_pairs={{0,16},{16,32},{32,48},{48,64},{64,80},{80,96},{96,112},{112,0},{1... | collective-permute-start | bytes 786440 | tf_op jit(solution)/shard_map/ppermute | solution.py:19
  47.0 11.6 %collective-permute-start.15 = (bf16[64,2048]{1,0:T(8,128)(2,1)S(1)}, bf16[64,2048]{1,0:T(8,128)(2,1)S(1)}, u32[]{:S(2)}, u32[]{:S(2)}) collective-permute-start(bf16[64,2048]{1,0:T(8,128)(2,1)S(1)} %collective-permute-done.13.refs_2_), channel_id=1, source_target_pairs={{0,16},{16,32},{32,48},{48,64},{64,80},{80,96},{96,112},{112,0},{1... | collective-permute-start | bytes 786440 | tf_op jit(solution)/shard_map/ppermute | solution.py:19
  47.0 11.6 %collective-permute-start.16 = (bf16[64,2048]{1,0:T(8,128)(2,1)}, bf16[64,2048]{1,0:T(8,128)(2,1)S(1)}, u32[]{:S(2)}, u32[]{:S(2)}) collective-permute-start(bf16[64,2048]{1,0:T(8,128)(2,1)} %collective-permute-done.12.refs_1_), channel_id=1, source_target_pairs={{0,112},{16,0},{32,16},{48,32},{64,48},{80,64},{96,80},{112,96},{1... | collective-permute-start | bytes 786440 | tf_op jit(solution)/shard_map/ppermute | solution.py:19
  51.3 1.0 copy-start.3
  52.2 0.9 copy-start.4
  53.2 11.9 %copy-start.8 = (s32[1,8]{1,0:T(1,128)S(1)}, s32[1,8]{1,0:T(1,128)}, u32[]{:S(2)}) copy-start(s32[1,8]{1,0:T(1,128)} %constant.43) | copy-start | bytes 100
  55.4 0.7 copy-start.5
  56.1 14.5 %copy-start.6 = (bf16[640,128]{1,0:T(8,128)(2,1)S(1)}, bf16[640,128]{1,0:T(8,128)(2,1)}, u32[]{:S(2)}) copy-start(bf16[640,128]{1,0:T(8,128)(2,1)} %copy-done.5) | copy-start | bytes 491524
  56.1 8.6 %collective-permute-start.18 = (bf16[640,256]{1,0:T(8,128)(2,1)S(1)}, bf16[640,256]{1,0:T(8,128)(2,1)S(1)}, u32[]{:S(2)}, u32[]{:S(2)}) collective-permute-start(bf16[640,256]{1,0:T(8,128)(2,1)S(1)} %get-tuple-element.18.refs_0_), channel_id=1, source_target_pairs={{0,128},{128,0},{1,129},{129,1},{2,130},{130,2},{3,131},{131,3},{4... | collective-permute-start | bytes 983048 | tf_op jit(solution)/shard_map/ppermute | solution.py:19
  61.3 7.8 %collective-permute-start.21 = (bf16[384,256]{1,0:T(8,128)(2,1)S(1)}, bf16[384,256]{1,0:T(8,128)(2,1)S(1)}, u32[]{:S(2)}, u32[]{:S(2)}) collective-permute-start(bf16[384,256]{1,0:T(8,128)(2,1)S(1)} %get-tuple-element.19.refs_4_), channel_id=1, source_target_pairs={{0,128},{128,0},{1,129},{129,1},{2,130},{130,2},{3,131},{131,3},{4... | collective-permute-start | bytes 589832 | tf_op jit(solution)/shard_map/ppermute | solution.py:19
  64.5 4.7 %collective-permute-start.17 = (bf16[640,256]{1,0:T(8,128)(2,1)S(1)}, bf16[640,256]{1,0:T(8,128)(2,1)S(1)}, u32[]{:S(2)}, u32[]{:S(2)}) collective-permute-start(bf16[640,256]{1,0:T(8,128)(2,1)S(1)} %get-tuple-element.18.refs_0_), channel_id=1, source_target_pairs={{0,8},{8,0},{1,9},{9,1},{2,10},{10,2},{3,11},{11,3},{4,12},{12,4},... | collective-permute-start | bytes 983048 | tf_op jit(solution)/shard_map/ppermute | solution.py:19
  64.7 5.9 %collective-permute-start.19 = (bf16[640,256]{1,0:T(8,128)(2,1)S(1)}, bf16[640,256]{1,0:T(8,128)(2,1)S(1)}, u32[]{:S(2)}, u32[]{:S(2)}) collective-permute-start(bf16[640,256]{1,0:T(8,128)(2,1)S(1)} %collective-permute-done.18.refs_2_), channel_id=1, source_target_pairs={{0,8},{8,0},{1,9},{9,1},{2,10},{10,2},{3,11},{11,3},{4,12},{12,4},... | collective-permute-start | bytes 983048 | tf_op jit(solution)/shard_map/ppermute | solution.py:19
  65.6 3.6 %collective-permute-start.20 = (bf16[384,256]{1,0:T(8,128)(2,1)S(1)}, bf16[384,256]{1,0:T(8,128)(2,1)S(1)}, u32[]{:S(2)}, u32[]{:S(2)}) collective-permute-start(bf16[384,256]{1,0:T(8,128)(2,1)S(1)} %get-tuple-element.19.refs_4_), channel_id=1, source_target_pairs={{0,8},{8,0},{1,9},{9,1},{2,10},{10,2},{3,11},{11,3},{4,12},{12,4},... | collective-permute-start | bytes 589832 | tf_op jit(solution)/shard_map/ppermute | solution.py:19
  69.1 1.4 %collective-permute-start.22 = (bf16[384,256]{1,0:T(8,128)(2,1)S(1)}, bf16[384,256]{1,0:T(8,128)(2,1)S(1)}, u32[]{:S(2)}, u32[]{:S(2)}) collective-permute-start(bf16[384,256]{1,0:T(8,128)(2,1)S(1)} %collective-permute-done.21.refs_6_), channel_id=1, source_target_pairs={{0,8},{8,0},{1,9},{9,1},{2,10},{10,2},{3,11},{11,3},{4,12},{12,4},... | collective-permute-start | bytes 589832 | tf_op jit(solution)/shard_map/ppermute | solution.py:19
  70.6 23.8 %copy-start.1 = (bf16[1,1024,2048]{2,1,0:T(8,128)(2,1)S(1)}, bf16[1,1024,2048]{2,1,0:T(8,128)(2,1)}, u32[]{:S(2)}) copy-start(bf16[1,1024,2048]{2,1,0:T(8,128)(2,1)} %param.15) | copy-start | bytes 12582916
  70.6 23.8 %copy-start.2 = (bf16[1,128,2048]{2,1,0:T(8,128)(2,1)S(1)}, bf16[1,128,2048]{2,1,0:T(8,128)(2,1)}, u32[]{:S(2)}) copy-start(bf16[1,128,2048]{2,1,0:T(8,128)(2,1)} %param.9) | copy-start | bytes 1572868
  95.9 13.2 %collective-permute-start.23 = (bf16[64,2048]{1,0:T(8,128)(2,1)S(1)}, bf16[64,2048]{1,0:T(8,128)(2,1)S(1)}, u32[]{:S(2)}, u32[]{:S(2)}) collective-permute-start(bf16[64,2048]{1,0:T(8,128)(2,1)S(1)} %get-tuple-element.22), channel_id=1, source_target_pairs={{0,1},{1,2},{2,3},{3,4},{4,5},{5,6},{6,7},{8,9},{9,10},{10,11},{11... | collective-permute-start | bytes 786440 | tf_op jit(solution)/shard_map/ppermute | solution.py:25
  99.3 14.4 %collective-permute-start.24 = (bf16[64,2048]{1,0:T(8,128)(2,1)S(1)}, bf16[64,2048]{1,0:T(8,128)(2,1)S(1)}, u32[]{:S(2)}, u32[]{:S(2)}) collective-permute-start(bf16[64,2048]{1,0:T(8,128)(2,1)S(1)} %get-tuple-element.23), channel_id=1, source_target_pairs={{0,1},{1,2},{2,3},{3,4},{4,5},{5,6},{6,7},{8,9},{9,10},{10,11},{11... | collective-permute-start | bytes 786440 | tf_op jit(solution)/shard_map/ppermute | solution.py:25
